TPU v7x, 32 devices: a whole 2x2x4 slice. The times are simulated.
32 devices in a mesh: dp: 8 (over z, core), tensor: 4 (over y, x).
Axes of the slice: x: 2, y: 2, z: 4, core: 2. Of those that a mesh axis runs over, the one named last changes fastest.
Arguments:
- hidden_in: bfloat16 [8192, 2048], P(('dp', 'tensor')), may hold values from -6 to 6
- gain_attn: bfloat16 [2048], P('dp'), may hold values from 0.099609375 to 1.8984375
- w_query: bfloat16 [2048, 2048], P('dp', 'tensor'), may hold values from -0.125 to 0.125
- w_key: bfloat16 [2048, 512], P('dp', 'tensor'), may hold values from -0.125 to 0.125
- w_value: bfloat16 [2048, 512], P('dp', 'tensor'), may hold values from -0.125 to 0.125
- w_out: bfloat16 [2048, 2048], P('tensor', 'dp'), may hold values from -0.5 to 0.5
- gain_mlp: bfloat16 [2048], P('dp'), may hold values from 0.099609375 to 1.8984375
- w_gate: bfloat16 [2048, 8192], P('dp', 'tensor'), may hold values from -0.125 to 0.125
- w_up: bfloat16 [2048, 8192], P('dp', 'tensor'), may hold values from -0.125 to 0.125
- w_down: bfloat16 [8192, 2048], P('tensor', 'dp'), may hold values from -0.09375 to 0.09375
- positions: int32 [8192], P('dp'), may hold values from 0 to 3069, as said below
- cotangent: bfloat16 [8192, 2048], P(('dp', 'tensor')), may hold values from -6 to 6
Outputs:
- out: bfloat16 [8192, 2048], P(('dp', 'tensor'))
- grad_in: float32 [8192, 2048], P(('dp', 'tensor'))
- grad_gain_attn: float32 [2048], P(('dp', 'tensor'))
- grad_query: float32 [2048, 2048], P('dp', 'tensor')
- grad_key: float32 [2048, 512], P('dp', 'tensor')
- grad_value: float32 [2048, 512], P('dp', 'tensor')
- grad_out_proj: float32 [2048, 2048], P('tensor', 'dp')
- grad_gain_mlp: float32 [2048], P(('dp', 'tensor'))
- grad_gate: float32 [2048, 8192], P('dp', 'tensor')
- grad_up: float32 [2048, 8192], P('dp', 'tensor')
- grad_down: float32 [8192, 2048], P('tensor', 'dp')
Inputs may be any that keep to these rules, and one draw needn't show every extreme that they name: Within each sequence the first position is 0 and positions rise by 1 to 3 from one token to the next; in one sequence they rise by 3 at every token.
All inputs are finite; a program needn't handle non-finite values.
Results may differ from a plain program's by a relative error of at most 0.02.
Values may be sent and summed in bfloat16 or wider, within the bound.
No kernel may reach another device: no remote copies, remote signals or barrier semaphores. Data moves between devices by JAX's collectives and lax.ppermute only.
A program may use at most 256 MiB of HBM per device.

v0:
```python
import functools
import math

import jax
import jax.numpy as jnp
from jax import lax
from jax.experimental import pallas as pl
from jax.experimental.pallas import tpu as pltpu
from jax.sharding import PartitionSpec as P

HEAD_DIM = 64
PAIR = 2 * HEAD_DIM
SEQ_LEN = 1024


EPS = 1e-05
ROPE_BASE = 500000.0
SCALE = 1.0 / math.sqrt(HEAD_DIM)
PARAMS = pltpu.CompilerParams(vmem_limit_bytes=58 * 2**20)
ONCE = pl.Buffered(1)

barrier = lax.optimization_barrier


def hint(flops):
    return pl.CostEstimate(flops=flops, bytes_accessed=0, transcendentals=0)


def rms_scale(values):
    return lax.rsqrt(jnp.mean(values * values, axis=-1, keepdims=True) + EPS)


def norm_back(grad, values, scale, gain):
    inner = grad * gain
    cubed = scale * scale * scale
    result = scale * inner - values * cubed * jnp.mean(inner * values, axis=-1, keepdims=True)
    return (result, jnp.sum(grad * values * scale, axis=0))


def mm(left, right):
    return jnp.dot(left, right, preferred_element_type=jnp.float32)


def mm_nt(left, right):
    return lax.dot_general(left, right, (((1,), (1,)), ((), ())), preferred_element_type=jnp.float32)


def mm_tn(left, right):
    return lax.dot_general(left, right, (((0,), (0,)), ((), ())), preferred_element_type=jnp.float32)


def lane_index(rows):
    return lax.broadcasted_iota(jnp.int32, (rows, PAIR), 1)


def turn(pair, cosine, sine):
    lower = lane_index(pair.shape[0]) % HEAD_DIM < HEAD_DIM // 2
    other = jnp.where(
        lower, pltpu.roll(pair, PAIR - HEAD_DIM // 2, 1), pltpu.roll(pair, HEAD_DIM // 2, 1)
    )
    return pair * cosine + other * sine


def project_kernel(place_ref, *refs, size, q_width, kv_width):
    x_refs = refs[:size]
    gain_ref, qo_ref, qx_ref, kvo_ref, kvx_ref, cos_ref, sin_ref = refs[size:-4]
    n_ref, q_ref, k_ref, v_ref = refs[-4:]
    rows = q_ref.shape[0]
    half = qo_ref.shape[0]

    def one(x_ref):
        x = x_ref[...].astype(jnp.float32)
        normed = (x * rms_scale(x) * gain_ref[...]).astype(jnp.bfloat16)
        n_ref[...] = normed
        cosine, sine = cos_ref[...], sin_ref[...]
        own, other = normed[:, :half], normed[:, half:]
        lin = mm(own, qo_ref[...]) + mm(other, qx_ref[...])
        for low in range(0, q_width, PAIR):
            query = turn(lin[:, low : low + PAIR], cosine, sine).astype(jnp.bfloat16)
            q_ref[:, low : low + PAIR] = query * jnp.bfloat16(SCALE)
        lin = mm(own, kvo_ref[...]) + mm(other, kvx_ref[...])
        first = lane_index(rows) < HEAD_DIM
        for ref, start, rotate in ((k_ref, 0, True), (v_ref, kv_width, False)):
            for head in range(kv_width // HEAD_DIM):
                low = start + head * HEAD_DIM
                block = lin[:, low // PAIR * PAIR : low // PAIR * PAIR + PAIR]
                if rotate:
                    block = turn(block, cosine, sine)
                moved = pltpu.roll(block, HEAD_DIM, 1)
                if low % PAIR:
                    block, moved = moved, block
                ref[head, 0] = jnp.where(first, block, 0.0).astype(jnp.bfloat16)
                ref[head, 1] = jnp.where(first, 0.0, moved).astype(jnp.bfloat16)

    for step in range(size):
        pl.when(pl.program_id(0) == step)(functools.partial(one, x_refs[step]))


class Columns:
    def __init__(self, q_width, kv_width):
        self.q_width, self.kv_width = q_width, kv_width

    def spec(self, part, rows, place=lambda *_: 0):
        width, start = {
            "q": (self.q_width, 0),
            "out": (self.q_width, self.q_width),
            "kv": (2 * self.kv_width, 2 * self.q_width),
        }[part]
        index = start // width
        mode = {"pipeline_mode": ONCE} if place() == 0 else {}
        return pl.BlockSpec((rows, width), lambda *grid: (place(*grid), index), **mode)


def project(me, blocks, gain, own, other, cosine, sine, columns):
    size = len(blocks)
    rows, features = blocks[0].shape
    total = rows * size
    q_width, kv_width = columns.q_width, columns.kv_width
    key_heads = kv_width // HEAD_DIM
    width = q_width + 2 * kv_width
    half = features // 2
    fixed = lambda p, m: (0, 0)
    placed = lambda p, m: (jnp.bitwise_xor(p, m[0]), 0)
    padded = pl.BlockSpec(
        (key_heads, 2, rows, PAIR), lambda p, m: (0, 0, jnp.bitwise_xor(p, m[0]), 0)
    )
    spec = pltpu.PrefetchScalarGridSpec(
        num_scalar_prefetch=1,
        grid=(size,),
        in_specs=[pl.BlockSpec((rows, features), fixed, pipeline_mode=ONCE)] * size
        + [
            pl.BlockSpec((1, features), fixed),
            columns.spec("q", half),
            columns.spec("q", half),
            columns.spec("kv", half),
            columns.spec("kv", half),
            pl.BlockSpec((rows, PAIR), placed),
            pl.BlockSpec((rows, PAIR), placed),
        ],
        out_specs=[
            pl.BlockSpec((rows, features), lambda p, m: (p, 0)),
            pl.BlockSpec((rows, q_width), lambda p, m: (p, 0)),
            padded,
            padded,
        ],
    )
    padded_shape = jax.ShapeDtypeStruct((key_heads, 2, total, PAIR), jnp.bfloat16)
    return pl.pallas_call(
        functools.partial(project_kernel, size=size, q_width=q_width, kv_width=kv_width),
        grid_spec=spec,
        out_shape=[
            jax.ShapeDtypeStruct((total, features), jnp.bfloat16),
            jax.ShapeDtypeStruct((total, q_width), jnp.bfloat16),
            padded_shape,
            padded_shape,
        ],
        compiler_params=PARAMS,
        cost_estimate=hint(2 * total * features * width // 16),
    )(me, *blocks, gain, own, other, own, other, cosine, sine)


def attend_kernel(
    me_ref, q_ref, k_ref, v_ref, wo_ref, wx_ref, o_ref, l_ref, *refs, size, heads, group
):
    part_refs, vt_ref = refs[:size], refs[size]
    rows = q_ref.shape[0]
    half = wo_ref.shape[0]
    mine = jnp.bitwise_xor(me_ref[0], pl.program_id(0))
    key_place = lax.broadcasted_iota(jnp.int32, (rows, rows), 0)
    query_place = lax.broadcasted_iota(jnp.int32, (rows, rows), 1)

    @pl.when(pl.program_id(0) == 0)
    def _():
        for head in range(heads // group):
            for side in range(2):
                vt_ref[head, side] = v_ref[head, side].T

    def one(span):
        keys = span * rows
        for pair in range(heads // 2):
            head = 2 * pair // group
            lanes = slice(pair * PAIR, (pair + 1) * PAIR)
            query = q_ref[:, lanes]
            acc = None
            inverse = []
            for side in range(2):
                diag = mm_nt(k_ref[head, side, keys : keys + rows, :], query)
                diag = jnp.where(key_place <= query_place, diag, -1e9)
                top = jnp.max(diag, axis=0, keepdims=True)
                if span:
                    body = mm_nt(k_ref[head, side, :keys, :], query)
                    top = jnp.maximum(top, jnp.max(body, axis=0, keepdims=True))
                diag = jnp.exp(diag - top)
                total = jnp.sum(diag, axis=0, keepdims=True)
                part = mm(vt_ref[head, side, :, keys : keys + rows], diag.astype(jnp.bfloat16))
                if span:
                    body = jnp.exp(body - top)
                    total = total + jnp.sum(body, axis=0, keepdims=True)
                    part = part + mm(vt_ref[head, side, :, :keys], body.astype(jnp.bfloat16))
                acc = part if acc is None else acc + part
                inverse.append(jnp.broadcast_to(1.0 / total, (HEAD_DIM, rows)))
                l_ref[2 * pair + side : 2 * pair + side + 1, :] = top + jnp.log(total)
            acc = acc * jnp.concatenate(inverse, axis=0)
            o_ref[:, lanes] = acc.T.astype(jnp.bfloat16)

    for span in range(size):
        pl.when(mine == span)(functools.partial(one, span))

    def project_out(ref):
        ref[:, :half] = mm_nt(o_ref[...], wo_ref[...]).astype(jnp.bfloat16)
        ref[:, half:] = mm_nt(o_ref[...], wx_ref[...]).astype(jnp.bfloat16)

    for step in range(size):
        pl.when(pl.program_id(0) == step)(functools.partial(project_out, part_refs[step]))


def attend(me, query, key_pad, value_pad, own, other, columns, size, group):
    total, width = query.shape
    features = 2 * own.shape[0]
    rows, heads = total // size, width // HEAD_DIM
    whole = pl.BlockSpec(key_pad.shape, lambda p, m: (0, 0, 0, 0), pipeline_mode=ONCE)
    spec = pltpu.PrefetchScalarGridSpec(
        num_scalar_prefetch=1,
        grid=(size,),
        in_specs=[pl.BlockSpec((rows, width), lambda p, m: (p, 0)), whole, whole]
        + [columns.spec("out", features // 2)] * 2,
        out_specs=[
            pl.BlockSpec((rows, width), lambda p, m: (p, 0)),
            pl.BlockSpec((heads, rows), lambda p, m: (0, p)),
        ]
        + [pl.BlockSpec((rows, features), lambda p, m: (0, 0))] * size,
        scratch_shapes=[pltpu.VMEM((heads // group, 2, PAIR, total), jnp.bfloat16)],
    )
    return pl.pallas_call(
        functools.partial(attend_kernel, size=size, heads=heads, group=group),
        grid_spec=spec,
        out_shape=[
            jax.ShapeDtypeStruct((total, width), jnp.bfloat16),
            jax.ShapeDtypeStruct((heads, total), jnp.float32),
        ]
        + [jax.ShapeDtypeStruct((rows, features), jnp.bfloat16)] * size,
        compiler_params=PARAMS,
        cost_estimate=hint(8 * heads * total * total * HEAD_DIM // 16),
    )(me, query, key_pad, value_pad, own, other)


def attend_back_kernel(
    me_ref, q_ref, l_ref, k_ref, v_ref, cos_ref, sin_ref, *refs, size, heads, group
):
    do_refs = refs[:size]
    out_ref, dk_ref, dv_ref, kt_ref, do_ref = refs[size:]
    rows = q_ref.shape[0]
    key_heads = heads // group
    step = pl.program_id(0)
    me = me_ref[0]
    mine = jnp.bitwise_xor(me, step)
    key_place = lax.broadcasted_iota(jnp.int32, (rows, rows), 0)
    query_place = lax.broadcasted_iota(jnp.int32, (rows, rows), 1)

    def rows_of(block):
        return pl.ds(pl.multiple_of(block * rows, rows), rows)

    @pl.when(step == 0)
    def _():
        dk_ref[...] = jnp.zeros_like(dk_ref)
        dv_ref[...] = jnp.zeros_like(dv_ref)
        for head in range(key_heads):
            for side in range(2):
                kt_ref[head, side] = k_ref[head, side].T

    def fetch(ref):
        do_ref[...] = ref[...]

    for block in range(size):
        pl.when(step == block)(functools.partial(fetch, do_refs[block]))

    def one(span):
        keys = span * rows
        parts = [(keys, keys + rows, True)] + ([(0, keys, False)] if span else [])
        cosine, sine = cos_ref[keys : keys + rows, :], sin_ref[keys : keys + rows, :]
        for pair in range(heads // 2):
            head = 2 * pair // group
            lanes = slice(pair * PAIR, (pair + 1) * PAIR)
            query, grad = q_ref[:, lanes], do_ref[:, lanes]
            acc = None
            for side in range(2):
                log_total = l_ref[2 * pair + side : 2 * pair + side + 1, :]
                inner = None
                kept = []
                for low, high, diagonal in parts:
                    probs = mm_nt(k_ref[head, side, low:high, :], query)
                    probs = jnp.exp(probs - log_total)
                    if diagonal:
                        probs = jnp.where(key_place <= query_place, probs, 0.0)
                    prob_grad = mm_nt(v_ref[head, side, low:high, :], grad)
                    dv_ref[head, side, low:high, :] += mm(probs.astype(jnp.bfloat16), grad)
                    term = jnp.sum(probs * prob_grad, axis=0, keepdims=True)
                    inner = term if inner is None else inner + term
                    kept.append((low, high, probs, prob_grad))
                for low, high, probs, prob_grad in kept:
                    score_grad = (probs * (prob_grad - inner)).astype(jnp.bfloat16)
                    dk_ref[head, side, low:high, :] += mm(score_grad, query)
                    part = mm(kt_ref[head, side, :, low:high], score_grad)
                    acc = part if acc is None else acc + part
            turned = turn(acc.T * SCALE, cosine, -sine)
            out_ref[rows_of(step), lanes] = turned.astype(jnp.bfloat16)

    for span in range(size):
        pl.when(mine == span)(functools.partial(one, span))

    @pl.when(step == size - 1)
    def _():
        first = lane_index(rows) < HEAD_DIM
        wanted = [(dk_ref, head, True) for head in range(key_heads)]
        wanted += [(dv_ref, head, False) for head in range(key_heads)]
        for span in range(size):
            place = slice(span * rows, (span + 1) * rows)
            cosine, sine = cos_ref[place, :], sin_ref[place, :]
            for block in range(len(wanted) // 2):
                halves, rotate = [], []
                for half in range(2):
                    ref, head, is_key = wanted[2 * block + half]
                    low, high = ref[head, 0, place, :], ref[head, 1, place, :]
                    if half:
                        halves.append(pltpu.roll(low, HEAD_DIM, 1) + high)
                    else:
                        halves.append(low + pltpu.roll(high, HEAD_DIM, 1))
                    rotate.append(is_key)
                value = jnp.where(first, halves[0], halves[1])
                if rotate[0] and rotate[1]:
                    value = turn(value, cosine, -sine)
                elif rotate[0]:
                    value = jnp.where(first, turn(value, cosine, -sine), value)
                start = heads * HEAD_DIM + block * PAIR
                target = rows_of(jnp.bitwise_xor(me, span))
                out_ref[target, start : start + PAIR] = value.astype(jnp.bfloat16)


def attend_back(
    me, query, log_total, key_pad, value_pad, cosine, sine, attended_grad, group
):
    total, width = query.shape
    size = len(attended_grad)
    rows, heads = total // size, width // HEAD_DIM
    key_heads = heads // group
    out_width = width + 2 * key_heads * HEAD_DIM
    whole = pl.BlockSpec(key_pad.shape, lambda p, m: (0, 0, 0, 0), pipeline_mode=ONCE)
    table = pl.BlockSpec((total, PAIR), lambda p, m: (0, 0), pipeline_mode=ONCE)
    spec = pltpu.PrefetchScalarGridSpec(
        num_scalar_prefetch=1,
        grid=(size,),
        in_specs=[
            pl.BlockSpec((rows, width), lambda p, m: (p, 0)),
            pl.BlockSpec((heads, rows), lambda p, m: (0, p)),
            whole,
            whole,
            table,
            table,
        ]
        + [pl.BlockSpec((rows, width), lambda p, m: (0, 0), pipeline_mode=ONCE)] * size,
        out_specs=pl.BlockSpec((total, out_width), lambda p, m: (0, 0)),
        scratch_shapes=[
            pltpu.VMEM(key_pad.shape, jnp.float32),
            pltpu.VMEM(key_pad.shape, jnp.float32),
            pltpu.VMEM((key_heads, 2, PAIR, total), jnp.bfloat16),
            pltpu.VMEM((rows, width), jnp.bfloat16),
        ],
    )
    return pl.pallas_call(
        functools.partial(attend_back_kernel, size=size, heads=heads, group=group),
        grid_spec=spec,
        out_shape=jax.ShapeDtypeStruct((total, out_width), jnp.bfloat16),
        compiler_params=PARAMS,
        cost_estimate=hint(20 * heads * total * total * HEAD_DIM),
    )(me, query, log_total, key_pad, value_pad, cosine, sine, *attended_grad)


def grouped(arrays, counts):
    arrays = iter(arrays)
    return [[next(arrays) for _ in range(count)] for count in counts]


def mlp_kernel(*refs, n_counts, e_counts, adds):
    size = len(n_counts)
    pieces = sum(n_counts) + sum(e_counts)
    n_refs = grouped(refs, n_counts)
    e_refs = grouped(refs[sum(n_counts) :], e_counts)
    gate_o, up_o, down_o, gate_x, up_x, down_x = refs[pieces : pieces + 6]
    y_ref, n_ref, e_ref = refs[-3:]
    dn_refs = refs[-3 - size if adds else -4 : -3]
    dg_ref, du_ref, h_ref = refs[-6 - size if adds else -7 :][:3]
    half = gate_o.shape[0]

    def fetch(step):
        for target, sources in ((n_ref, n_refs[step]), (e_ref, e_refs[step])):
            low = 0
            for source in sources:
                high = low + source.shape[0]
                target[low:high] = source[...]
                low = high

    for step in range(size):
        pl.when(pl.program_id(0) == step)(functools.partial(fetch, step))
    gate = mm(n_ref[:, :half], gate_o[...]) + mm(n_ref[:, half:], gate_x[...])
    up = mm(n_ref[:, :half], up_o[...]) + mm(n_ref[:, half:], up_x[...])
    grad = mm(e_ref[:, :half], down_o[...]) + mm(e_ref[:, half:], down_x[...])
    sigma = jax.nn.sigmoid(gate)
    silu = gate * sigma
    hidden = (silu * up).astype(jnp.bfloat16)
    gate_grad = (grad * up * sigma * (1.0 + gate * (1.0 - sigma))).astype(jnp.bfloat16)
    up_grad = (grad * silu).astype(jnp.bfloat16)
    dg_ref[...] = gate_grad
    du_ref[...] = up_grad
    h_ref[...] = hidden
    for part, gate_w, up_w, down_w in ((0, gate_o, up_o, down_o), (1, gate_x, up_x, down_x)):
        lanes = slice(part * half, (part + 1) * half)
        dn = mm_nt(gate_grad, gate_w[...]) + mm_nt(up_grad, up_w[...])
        y = mm_nt(hidden, down_w[...])
        if adds:
            dn = dn + refs[pieces + 6][:, lanes].astype(jnp.float32)
            y = y + refs[pieces + 7][:, lanes].astype(jnp.float32)
        y_ref[:, lanes] = y.astype(jnp.bfloat16)
        dn = dn.astype(jnp.bfloat16)

        def store(ref):
            ref[:, lanes] = dn

        if adds:
            for step in range(size):
                pl.when(pl.program_id(0) == step)(functools.partial(store, dn_refs[step]))
        else:
            store(dn_refs[0])


def mlp(tokens, cot, own, other, earlier):
    size = len(tokens)
    rows, features = tokens[0][0].shape
    half, units = own.shape[0], own.shape[1] // 3
    total = rows * size
    fixed = lambda p: (0, 0)
    moving = lambda p: (p, 0)
    wide = pl.BlockSpec((rows, features), moving)
    sums = jax.ShapeDtypeStruct((total, features), jnp.bfloat16)
    dn_specs, dn_shapes = [wide], [sums]
    if earlier:
        dn_specs = [pl.BlockSpec((rows, features), fixed)] * size
        dn_shapes = [jax.ShapeDtypeStruct((rows, features), jnp.bfloat16)] * size
    pieces = sum(tokens, []) + sum(cot, [])
    thirds = [
        pl.BlockSpec((half, units), lambda p, t=t: (0, t), pipeline_mode=ONCE) for t in range(3)
    ]
    return pl.pallas_call(
        functools.partial(
            mlp_kernel,
            n_counts=[len(group) for group in tokens],
            e_counts=[len(group) for group in cot],
            adds=bool(earlier),
        ),
        grid=(size,),
        in_specs=[pl.BlockSpec(piece.shape, fixed, pipeline_mode=ONCE) for piece in pieces]
        + thirds * 2
        + [wide] * len(earlier),
        out_specs=[pl.BlockSpec((rows, units), moving)] * 3 + dn_specs + [wide],
        out_shape=[jax.ShapeDtypeStruct((total, units), jnp.bfloat16)] * 3 + dn_shapes + [sums],
        scratch_shapes=[pltpu.VMEM((rows, features), jnp.bfloat16)] * 2,
        compiler_params=PARAMS,
        cost_estimate=hint(12 * total * features * units),
    )(*pieces, own, own, own, other, other, other, *earlier)


def add_refs(refs):
    total = refs[0][...].astype(jnp.float32)
    for ref in refs[1:]:
        total = total + ref[...].astype(jnp.float32)
    return total


def store_by_device(out_ref, values, core, chips):
    width = values.shape[1] // (2 * chips)
    for chip in range(chips):
        own = values[:, chip * width : (chip + 1) * width]
        other = values[:, (chips + chip) * width : (chips + chip + 1) * width]
        low = 2 * chip * width
        out_ref[:, low : low + width] = jnp.where(core == 0, own, other)
        out_ref[:, low + width : low + 2 * width] = jnp.where(core == 0, other, own)


def middle_kernel(*refs):
    x_ref, gain_ref, middle_ref, normed_ref = refs[-4:]
    values = x_ref[...].astype(jnp.float32) + add_refs(refs[:-4])
    middle_ref[...] = values
    normed_ref[...] = (values * rms_scale(values) * gain_ref[...]).astype(jnp.bfloat16)


def input_back_kernel(core_ref, *refs, chips):
    x_ref, before_ref, gain_ref, out_ref = refs[-4:]
    values = x_ref[...].astype(jnp.float32)
    inner = add_refs(refs[:-4]) * gain_ref[...]
    scale = rms_scale(values)
    mean = jnp.mean(inner * values, axis=-1, keepdims=True)
    result = before_ref[...] + scale * inner - values * (scale * scale * scale) * mean
    store_by_device(out_ref, result, core_ref[0], chips)


def output_kernel(core_ref, *refs, chips):
    middle_ref, out_ref = refs[-2:]
    values = middle_ref[...] + add_refs(refs[:-2])
    store_by_device(out_ref, values.astype(jnp.bfloat16), core_ref[0], chips)


def row_call(body, dtypes, arrays, core=None):
    rows, features = arrays[0].shape
    steps = 2
    wide = pl.BlockSpec((rows // steps, features), lambda i, *_: (i, 0))
    row = pl.BlockSpec((1, features), lambda i, *_: (0, 0))
    scalars = [] if core is None else [jnp.full((1,), core, jnp.int32)]
    return pl.pallas_call(
        body,
        grid_spec=pltpu.PrefetchScalarGridSpec(
            num_scalar_prefetch=len(scalars),
            grid=(steps,),
            in_specs=[row if array.shape[0] == 1 else wide for array in arrays],
            out_specs=[wide] * len(dtypes),
        ),
        out_shape=[jax.ShapeDtypeStruct((rows, features), dtype) for dtype in dtypes],
        compiler_params=PARAMS,
        cost_estimate=hint(0),
    )(*scalars, *arrays)


def unpack_kernel(sum_ref, q_ref, k_ref, v_ref, out_ref):
    q_width, kv_width = q_ref.shape[1], k_ref.shape[1]
    values = sum_ref[...].astype(jnp.float32)
    q_ref[...] = values[:, :q_width]
    kv = values[:, q_width : q_width + 2 * kv_width]
    k_ref[...] = kv[:, :kv_width]
    v_ref[...] = kv[:, kv_width:]
    out_ref[...] = values[:, q_width + 2 * kv_width :].T


def unpack(sums, q_width, kv_width):
    rows = sums.shape[0]
    widths = [(rows, q_width), (rows, kv_width), (rows, kv_width), (q_width, rows)]
    return pl.pallas_call(
        unpack_kernel,
        out_shape=[jax.ShapeDtypeStruct(shape, jnp.float32) for shape in widths],
        compiler_params=PARAMS,
        cost_estimate=hint(0),
    )(sums)


def unpack_shares_kernel(one_ref, two_ref, gate_ref, up_ref, down_ref):
    units = one_ref.shape[1] // 3
    for part, ref in enumerate((one_ref, two_ref)):
        cut = slice(part * units, (part + 1) * units)
        gate_ref[:, cut] = ref[:, :units].astype(jnp.float32)
        up_ref[:, cut] = ref[:, units : 2 * units].astype(jnp.float32)
        down_ref[cut, :] = ref[:, 2 * units :].astype(jnp.float32).T


def unpack_shares(one, two):
    rows, width = one.shape
    units = 2 * width // 3
    shapes = [(rows, units), (rows, units), (units, rows)]
    return pl.pallas_call(
        unpack_shares_kernel,
        out_shape=[jax.ShapeDtypeStruct(shape, jnp.float32) for shape in shapes],
        compiler_params=PARAMS,
        cost_estimate=hint(0),
    )(one, two)


def middle_back_kernel(*refs, parts, size):
    n_refs, refs = refs[:parts], refs[parts:]
    x_ref, e_ref, gain_ref, refs = refs[0], refs[1], refs[2], refs[3:]
    own_refs, other_refs, refs = refs[:size], refs[size : 2 * size], refs[2 * size :]
    grad_ref, branch_ref, part_ref, do_refs = refs[0], refs[1], refs[2], refs[3:]
    half = own_refs[0].shape[0]
    grad = add_refs(n_refs)
    values = x_ref[...]
    scale = rms_scale(values)
    result, part = norm_back(grad, values, scale, gain_ref[...])

    @pl.when(pl.program_id(0) == 0)
    def _():
        part_ref[...] = jnp.zeros_like(part_ref)

    part_ref[...] += part[None, :]
    result = result + e_ref[...].astype(jnp.float32)
    grad_ref[...] = result
    branch = result.astype(jnp.bfloat16)
    branch_ref[...] = branch
    for own, other, do_ref in zip(own_refs, other_refs, do_refs):
        do = mm(branch[:, :half], own[...]) + mm(branch[:, half:], other[...])
        do_ref[...] = do.astype(jnp.bfloat16)


def middle_back(arrived, middle, cot, gain, own, other):
    parts, size = len(arrived), len(own)
    rows, features = middle.shape
    width = own[0].shape[1]
    steps = 2
    wide = pl.BlockSpec((rows // steps, features), lambda i: (i, 0))
    narrow = pl.BlockSpec((rows // steps, width), lambda i: (i, 0))
    row = pl.BlockSpec((1, features), lambda i: (0, 0))
    weight = pl.BlockSpec((features // 2, width), lambda i: (0, 0), pipeline_mode=ONCE)
    grad, branch, part, *do = pl.pallas_call(
        functools.partial(middle_back_kernel, parts=parts, size=size),
        grid=(steps,),
        in_specs=[wide] * parts + [wide, wide, row] + [weight] * (2 * size),
        out_specs=[wide, wide, row] + [narrow] * size,
        out_shape=[
            jax.ShapeDtypeStruct((rows, features), jnp.float32),
            jax.ShapeDtypeStruct((rows, features), jnp.bfloat16),
            jax.ShapeDtypeStruct((1, features), jnp.float32),
        ]
        + [jax.ShapeDtypeStruct((rows, width), jnp.bfloat16)] * size,
        compiler_params=PARAMS,
        cost_estimate=hint(2 * rows * features * width * size),
    )(*arrived, middle, cot, gain, *own, *other)
    return grad, branch, part[0], do


def column_grad(blocks, other, mine, theirs):
    total = mm_tn(other[...], theirs[...])
    low = 0
    for block in blocks:
        high = low + block.shape[0]
        total = total + mm_tn(block[...], mine[low:high, :])
        low = high
    return total


def grad_kernel(*refs, n_count, e_count):
    n_refs, refs = refs[:n_count], refs[n_count:]
    e_refs, refs = refs[:e_count], refs[e_count:]
    n_other, e_other = refs[:2]
    acts, out_ref = refs[2:-1], refs[-1]
    units = acts[0].shape[1]
    for third in range(3):
        blocks, other = (e_refs, e_other) if third == 2 else (n_refs, n_other)
        grad = column_grad(blocks, other, acts[third], acts[third + 3])
        out_ref[0, :, third * units : (third + 1) * units] = grad.astype(jnp.bfloat16)


def mlp_grads(chips, tokens, cot, tokens_other, cot_other, mine, theirs):
    tokens, cot = sum(tokens, []), sum(cot, [])
    features = tokens[0].shape[1]
    total, units = mine[0].shape
    depth = features // (2 * chips)
    long = pl.BlockSpec((total, depth), lambda b: (0, b))
    fixed = pl.BlockSpec((total, units), lambda b: (0, 0), pipeline_mode=ONCE)
    return pl.pallas_call(
        functools.partial(grad_kernel, n_count=len(tokens), e_count=len(cot)),
        grid=(chips,),
        in_specs=[pl.BlockSpec((p.shape[0], depth), lambda b: (0, b)) for p in tokens + cot]
        + [long, long]
        + [fixed] * 6,
        out_specs=pl.BlockSpec((1, depth, 3 * units), lambda b: (b, 0, 0)),
        out_shape=jax.ShapeDtypeStruct((chips, depth, 3 * units), jnp.bfloat16),
        compiler_params=PARAMS,
        cost_estimate=hint(6 * total * features * units),
    )(*tokens, *cot, tokens_other, cot_other, *mine, *theirs)


def attn_grad_kernel(*refs, size):
    e_refs = refs[2 : 2 + size]
    n_ref, n_other = refs[:2]
    e_other, d_ref, d_other, o_ref, o_other, q_ref, kv_ref, g1_ref, g2_ref = refs[2 + size : -2]
    out_ref, gain_ref = refs[-2:]
    width, out_width = d_ref.shape[1], o_ref.shape[1]
    grad = column_grad([n_ref], n_other, d_ref, d_other)
    out_ref[0, :, :width] = grad.astype(jnp.bfloat16)
    out_grad = column_grad(e_refs, e_other, o_ref, o_other)
    out_ref[0, :, width : width + out_width] = out_grad.astype(jnp.bfloat16)
    cut = q_ref.shape[1]
    first = jnp.sum(grad[:, :cut] * q_ref[...].astype(jnp.float32), axis=1, keepdims=True)
    first += jnp.sum(grad[:, cut:] * kv_ref[...].astype(jnp.float32), axis=1, keepdims=True)
    first = first / g1_ref[...]
    lane = lane_index(grad.shape[0])
    gain_ref[0] = jnp.where(lane == 0, first, g2_ref[...])


def attn_grads(
    chips, tokens, branch, mine, theirs, weights, columns, gain_one, gain_two_part
):
    size = len(branch)
    qkv_grad, attended = mine
    tokens_other, branch_other, qkv_other, attended_other = theirs
    total, features = tokens.shape
    rows = total // size
    width, out_width = qkv_grad.shape[1], attended.shape[1]
    depth = features // (2 * chips)
    column = lambda b: (0, b)
    row = lambda b: (b, 0)
    long = pl.BlockSpec((total, depth), column)
    fixed = lambda array: pl.BlockSpec(array.shape, lambda b: (0, 0), pipeline_mode=ONCE)
    place = lambda b: (b, 0, 0)
    return pl.pallas_call(
        functools.partial(attn_grad_kernel, size=size),
        grid=(chips,),
        in_specs=[long, long]
        + [pl.BlockSpec((rows, depth), column)] * size
        + [long]
        + [fixed(qkv_grad)] * 2
        + [fixed(attended)] * 2
        + [
            columns.spec("q", depth, lambda b=None: b),
            columns.spec("kv", depth, lambda b=None: b),
            pl.BlockSpec((depth, 1), row),
            pl.BlockSpec((depth, 1), row),
        ],
        out_specs=[
            pl.BlockSpec((1, depth, width + out_width), place),
            pl.BlockSpec((1, depth, PAIR), place),
        ],
        out_shape=[
            jax.ShapeDtypeStruct((chips, depth, width + out_width), jnp.bfloat16),
            jax.ShapeDtypeStruct((chips, depth, PAIR), jnp.float32),
        ],
        compiler_params=PARAMS,
        cost_estimate=hint(2 * total * features * (width + out_width)),
    )(
        tokens,
        tokens_other,
        *branch,
        branch_other,
        qkv_grad,
        qkv_other,
        attended,
        attended_other,
        weights,
        weights,
        gain_one,
        gain_two_part,
    )


def input_grad_kernel(d_ref, qo_ref, qx_ref, kvo_ref, kvx_ref, *out_refs):
    half, cut = qo_ref.shape

    def one(ref):
        query, rest = d_ref[:, :cut], d_ref[:, cut:]
        own = mm_nt(query, qo_ref[...]) + mm_nt(rest, kvo_ref[...])
        other = mm_nt(query, qx_ref[...]) + mm_nt(rest, kvx_ref[...])
        ref[:, :half] = own.astype(jnp.bfloat16)
        ref[:, half:] = other.astype(jnp.bfloat16)

    for step, ref in enumerate(out_refs):
        pl.when(pl.program_id(0) == step)(functools.partial(one, ref))


def input_grad(qkv_grad, own, other, columns, size):
    total, width = qkv_grad.shape
    features = 2 * own.shape[0]
    rows = total // size
    fixed = lambda i: (0, 0)
    weights = [columns.spec(part, own.shape[0]) for part in ("q", "q", "kv", "kv")]
    return pl.pallas_call(
        input_grad_kernel,
        grid=(size,),
        in_specs=[pl.BlockSpec((rows, width), lambda i: (i, 0))] + weights,
        out_specs=[pl.BlockSpec((rows, features), fixed)] * size,
        out_shape=[jax.ShapeDtypeStruct((rows, features), jnp.bfloat16)] * size,
        compiler_params=PARAMS,
        cost_estimate=hint(2 * total * features * width),
    )(qkv_grad, own, other, own, other)


def swap(values, step):
    size = lax.axis_size("tensor")
    return lax.ppermute(values, "tensor", [(i, i ^ step) for i in range(size)])


def spread(values):
    return [values] + [swap(values, step) for step in range(1, lax.axis_size("tensor"))]


def send_blocks(blocks):
    return [blocks[0]] + [swap(block, step + 1) for step, block in enumerate(blocks[1:])]


def spread_around(values, held):
    if lax.axis_size("tensor") != 4:
        blocks = spread(values)
        first, held = barrier((blocks[1], held))
        return [[blocks[0]], [first]] + [[block] for block in blocks[2:]], held
    half = values.shape[0] // 2
    top, bottom = values[:half], values[half:]
    x_bottom, y_top = swap(bottom, 1), swap(top, 2)
    x_bottom, y_top, top, bottom, held = barrier((x_bottom, y_top, top, bottom, held))
    far = [swap(y_top, 1), swap(x_bottom, 2)]
    x_top, y_bottom = swap(top, 1), swap(bottom, 2)
    return [[values], [x_top, x_bottom], [y_top, y_bottom], far], held


def merge_kernel(x_ref, y_ref, top_ref, bottom_ref, x_out, y_out):
    half = top_ref.shape[0]
    x_out[:half] = x_ref[:half]
    x_out[half:] = add_refs([x_ref.at[half:], bottom_ref]).astype(jnp.bfloat16)
    y_out[:half] = add_refs([y_ref.at[:half], top_ref]).astype(jnp.bfloat16)
    y_out[half:] = y_ref[half:]


def send_sum(blocks, held=()):
    if len(blocks) != 4:
        return send_blocks(blocks), held
    own, near_x, near_y, far = blocks
    half = far.shape[0] // 2
    top, bottom = swap(far[:half], 1), swap(far[half:], 2)
    near_x, near_y = pl.pallas_call(
        merge_kernel,
        out_shape=[jax.ShapeDtypeStruct(near_x.shape, near_x.dtype)] * 2,
        compiler_params=PARAMS,
        cost_estimate=hint(0),
    )(near_x, near_y, top, bottom)
    near_x, near_y, held = barrier((near_x, near_y, held))
    return [own, swap(near_x, 1), swap(near_y, 2)], held


def add_up(blocks):
    total = blocks[0].astype(jnp.float32)
    for block in blocks[1:]:
        total = total + block.astype(jnp.float32)
    return total


def cross(values):
    count = lax.axis_size("dp")
    return lax.ppermute(values, "dp", [(i, i ^ 1) for i in range(count)])


def tables(positions):
    freqs = ROPE_BASE ** (-jnp.arange(0, HEAD_DIM, 2).astype(jnp.float32) / HEAD_DIM)
    angles = positions.astype(jnp.float32)[:, None] * freqs[None, :]
    cosine, sine = jnp.cos(angles), jnp.sin(angles)
    return (
        jnp.concatenate([cosine] * 4, axis=1),
        jnp.concatenate([-sine, sine, -sine, sine], axis=1),
    )


def chip_lines():
    count = lax.axis_size("dp")
    return [list(range(core, count, 2)) for core in range(2)]


def gather(values):
    return lax.all_gather(values, "dp", axis=0, tiled=True, axis_index_groups=chip_lines())


def scatter(values):
    total = lax.psum_scatter(
        values, "dp", scatter_dimension=0, tiled=True, axis_index_groups=chip_lines()
    )
    return total[0]


def along(values, step):
    count = lax.axis_size("dp")
    return lax.ppermute(values, "dp", [(i, (i + 2 * step) % count) for i in range(count)])


def line_parts(parts):
    chips = lax.axis_size("dp") // 2
    chip = lax.axis_index("dp") // 2
    blocks = [lax.dynamic_index_in_dim(parts, chip, 0, keepdims=False)]
    for step in range(1, chips):
        sent = lax.dynamic_index_in_dim(parts, (chip + step) % chips, 0, keepdims=False)
        blocks.append(along(sent, step))
    return blocks


def own_part(values):
    size = lax.axis_size("tensor")
    me = lax.axis_index("tensor")
    blocks = values.reshape((size, -1) + values.shape[1:])
    own = lax.dynamic_index_in_dim(blocks, me, 0, keepdims=False)
    for step in range(1, size):
        sent = lax.dynamic_index_in_dim(blocks, me ^ step, 0, keepdims=False)
        own = own + swap(sent, step)
    return own


def stack_kernel(*refs):
    low = 0
    for ref in refs[:-1]:
        high = low + ref.shape[0]
        refs[-1][low:high, :] = ref[...]
        low = high


def other_half(blocks):
    features = blocks[0].shape[1]
    shape = (sum(block.shape[0] for block in blocks), features // 2)
    halves = pl.pallas_call(
        stack_kernel,
        grid=(1,),
        in_specs=[pl.BlockSpec((b.shape[0], features // 2), lambda i: (0, 1)) for b in blocks],
        out_specs=pl.BlockSpec(shape, lambda i: (0, 0)),
        out_shape=jax.ShapeDtypeStruct(shape, blocks[0].dtype),
        compiler_params=PARAMS,
        cost_estimate=hint(0),
    )(*blocks)
    return cross(halves)


def feature_blocks(values):
    width = values.shape[-1] // lax.axis_size("dp")
    return [values[..., low : low + width] for low in range(0, values.shape[-1], width)]


def by_core(values, core):
    blocks = feature_blocks(values)
    pairs = list(zip(blocks[0::2], blocks[1::2]))
    own = [jnp.where(core == 0, even, odd) for even, odd in pairs]
    other = [jnp.where(core == 0, odd, even) for even, odd in pairs]
    return jnp.concatenate(own + other, axis=-1)


def per_device(
    hidden_in,
    gain_attn,
    w_query,
    w_key,
    w_value,
    w_out,
    gain_mlp,
    w_gate,
    w_up,
    w_down,
    positions,
    cotangent,
):
    size = lax.axis_size("tensor")
    chips = lax.axis_size("dp") // 2
    me = lax.axis_index("tensor")
    me_array = jnp.full((1,), me, jnp.int32)
    core = lax.axis_index("dp") % 2
    q_width, kv_width = w_query.shape[1], w_key.shape[1]
    group = q_width // kv_width
    units = w_down.shape[0] // 2
    half = hidden_in.shape[1] // 2

    columns = Columns(q_width, kv_width)
    attn_shard = jnp.concatenate([w_query, w_out.T, w_key, w_value], axis=1)
    attn_shard, hidden_in, gain_attn = barrier((attn_shard, hidden_in, gain_attn))
    attn_own = gather(attn_shard)
    residual = by_core(hidden_in, core)
    blocks_in = spread(residual)
    gains = lax.all_gather(jnp.stack([gain_attn, gain_mlp]), "dp", axis=1, tiled=True)
    gains = by_core(gains, core).astype(jnp.float32)
    cosine, sine = tables(positions)
    cotangent = by_core(cotangent, core)
    down_t = w_down.T
    shares = []
    for part in range(2):
        cut = slice(part * units, (part + 1) * units)
        shares.append(jnp.concatenate([w_gate[:, cut], w_up[:, cut], down_t[:, cut]], axis=1))
    shares, attn_own, blocks_in, cosine, sine, gains, cotangent = barrier(
        (shares, attn_own, blocks_in, cosine, sine, gains, cotangent)
    )
    mlp_own = [gather(share) for share in shares]
    cot_blocks = spread(cotangent)
    gain_one, gain_two = gains[0], gains[1]
    attn = (attn_own, cross(attn_own))

    tokens_one, query, key_pad, value_pad = project(
        me_array, blocks_in, gain_one[None, :], *attn, cosine, sine, columns
    )
    attended, log_total, *parts = attend(
        me_array, query, key_pad, value_pad, *attn, columns, size, group
    )
    parts, cot_blocks, tokens_one, attended = barrier((parts, cot_blocks, tokens_one, attended))
    arrived, _ = send_sum(parts)
    cot_other = other_half(cot_blocks)
    cot_blocks = [[block] for block in cot_blocks]
    early = (cross(tokens_one[:, half:]), cross(attended))
    arrived, cot_other, early = barrier((arrived, cot_other, early))
    out_t = [w[:, q_width : 2 * q_width] for w in attn]
    middle, normed_two = row_call(
        middle_kernel, [jnp.float32, jnp.bfloat16], [*arrived, residual, gain_two[None, :]]
    )
    tokens_two, own_share = spread_around(normed_two, mlp_own[0])
    weights = (own_share, cross(own_share))
    tokens_two, weights, out_own = barrier((tokens_two, weights, out_t[0]))
    tokens_other = other_half(sum(tokens_two, []))
    *acts, dn_part, y_part = mlp(tokens_two, cot_blocks, *weights, ())
    out_blocks = spread(out_own)
    acts, tokens_other = barrier((acts, tokens_other))
    acts_other = [cross(act) for act in acts]
    grads_one = mlp_grads(
        chips, tokens_two, cot_blocks, tokens_other, cot_other, acts, acts_other
    )
    grads_one, own_share = barrier((grads_one, mlp_own[1]))
    sums_one = scatter(grads_one)
    weights = (own_share, cross(own_share))
    *acts, y_part = mlp(tokens_two, cot_blocks, *weights, (dn_part, y_part))
    acts, dn_part = acts[:3], acts[3:]
    acts, dn_part, out_blocks = barrier((acts, dn_part, out_blocks))
    acts_other = [cross(act) for act in acts]
    arrived, acts = send_sum(dn_part, acts)
    out_other = [out_t[1]] + [cross(block) for block in out_blocks[1:]]
    grads_two = mlp_grads(
        chips, tokens_two, cot_blocks, tokens_other, cot_other, acts, acts_other
    )
    grads_two, arrived, out_other, y_part = barrier((grads_two, arrived, out_other, y_part))
    y_blocks = list(y_part.reshape((size, -1) + y_part.shape[1:]))
    y_early = [swap(y_blocks[step], step) for step in range(1, 3)]
    sums_two = scatter(grads_two)
    middle_grad, branch, gain_two_part, do_blocks = middle_back(
        arrived, middle, cotangent, gain_two[None, :], out_blocks, out_other
    )
    do_blocks = send_blocks(do_blocks)
    gain_two_other = cross(gain_two_part[half:])
    do_blocks, branch, gain_two_other, y_blocks, y_early = barrier(
        (do_blocks, branch, gain_two_other, y_blocks, y_early)
    )
    branch_blocks = spread(branch)
    qkv_grad = attend_back(
        me_array, query, log_total, key_pad, value_pad, cosine, sine, do_blocks, group
    )
    qkv_grad, sums_one = barrier((qkv_grad, sums_one))
    qkv_other = cross(qkv_grad)
    normed_part = input_grad(qkv_grad, *attn, columns, size)
    branch_blocks, normed_part = barrier((branch_blocks, normed_part))
    branch_other = other_half(branch_blocks)
    tokens_other, attended_other = early
    grads, gain_parts = attn_grads(
        chips,
        tokens_one,
        branch_blocks,
        (qkv_grad, attended),
        (tokens_other, branch_other, qkv_other, attended_other),
        attn_own,
        columns,
        gain_one[:half, None],
        (gain_two_part[:half] + gain_two_other)[:, None],
    )
    arrived, (grads, sums_two) = send_sum(normed_part, (grads, sums_two))
    attn_sums = scatter(grads)
    gain_sums = add_up(line_parts(gain_parts[:, :, :2]))
    unpacked = unpack_shares(sums_one, sums_two)
    arrived, y_blocks, unpacked, gain_sums = barrier((arrived, y_blocks, unpacked, gain_sums))
    grad_gate, grad_up, grad_down = unpacked
    y_late = [swap(y_blocks[step], step) for step in range(3, size)]
    (grad_in,) = row_call(
        functools.partial(input_back_kernel, chips=chips),
        [jnp.float32],
        [*arrived, residual, middle_grad, gain_one[None, :]],
        core,
    )
    grad_in, gain_sums = barrier((grad_in, gain_sums))
    gain_sums = own_part(gain_sums)
    y_late, grad_in, gain_sums = barrier((y_late, grad_in, gain_sums))
    (out,) = row_call(
        functools.partial(output_kernel, chips=chips),
        [jnp.bfloat16],
        [y_blocks[0], *y_early, *y_late, middle],
        core,
    )
    out, attn_sums = barrier((out, attn_sums))
    grad_query, grad_key, grad_value, grad_out = unpack(attn_sums, q_width, kv_width)
    return (
        out,
        grad_in,
        gain_sums[:, 0],
        grad_query,
        grad_key,
        grad_value,
        grad_out,
        gain_sums[:, 1],
        grad_gate,
        grad_up,
        grad_down,
    )


def solution(mesh):
    return jax.shard_map(
        per_device,
        mesh=mesh,
        in_specs=(
            P(("dp", "tensor"), None),
            P("dp"),
            P("dp", "tensor"),
            P("dp", "tensor"),
            P("dp", "tensor"),
            P("tensor", "dp"),
            P("dp"),
            P("dp", "tensor"),
            P("dp", "tensor"),
            P("tensor", "dp"),
            P("dp"),
            P(("dp", "tensor"), None),
        ),
        out_specs=(
            P(("dp", "tensor"), None),
            P(("dp", "tensor"), None),
            P(("dp", "tensor")),
            P("dp", "tensor"),
            P("dp", "tensor"),
            P("dp", "tensor"),
            P("tensor", "dp"),
            P(("dp", "tensor")),
            P("dp", "tensor"),
            P("dp", "tensor"),
            P("tensor", "dp"),
        ),
        check_vma=False,
    )
```

profile of v0, /device:TPU:0, one launch (start us, length us, event | category | flops | bytes accessed | tf_op | source)
XLA Modules:
  0.0 595.2 jit_solution(12509021940738283512)
XLA Ops:
  8.4 1.9 pad_maximum_fusion.2
  11.7 4.0 collective-permute-start.2
  16.5 12.4 %all_gather.13 = bf16[2,2048]{1,0:T(2,128)(2,1)S(1)} all-gather(bf16[2,256]{1,0:T(2,128)(2,1)S(1)} %pad_maximum_fusion.5), channel_id=1, replica_groups=mesh['dp'=8,'tensor'=4] {'dp'}, dimensions={1}, use_global_device_ids=true | all-gather | bytes 9216 | tf_op jit(solution)/shard_map/all_gather | solution.py:951
  29.0 1.5 copy.37
  36.3 1.9 fusion
  38.2 1.8 pad_maximum_fusion.3
  40.3 1.8 pad_maximum_fusion
  42.1 19.4 %collective-permute-done.1.refs_2_ = bf16[256,2048]{1,0:T(8,128)(2,1)} collective-permute-done((bf16[256,2048]{1,0:T(8,128)(2,1)S(1)}, bf16[256,2048]{1,0:T(8,128)(2,1)}, u32[]{:S(2)}, u32[]{:S(2)}) %collective-permute-start.1) | collective-permute-done | bytes 1048608 | tf_op jit(solution)/shard_map/ppermute | solution.py:772
  61.7 11.3 %all-gather.4.cloned.1.call-done.refs_5_.refs_7_.wo_ref.qo_ref.kvo_ref.refs_11_.refs_12_ = bf16[1024,1280]{1,0:T(8,128)(2,1)} async-done(((bf16[256,1280]{1,0:T(8,128)(2,1)}), bf16[1024,1280]{1,0:T(8,128)(2,1)}) %all-gather.4.cloned.1.call-update) | async-done | bytes 2621456 | tf_op jit(solution)/shard_map/all_gather | solution.py:849
  73.1 2.4 collective-permute-start.6
  78.2 1.5 copy-done
  79.7 11.9 %shard_map.203 = (bf16[1024,2048]{1,0:T(8,128)(2,1)}, bf16[1024,512]{1,0:T(8,128)(2,1)}, bf16[2,2,1024,128]{3,2,1,0:T(8,128)(2,1)}, bf16[2,2,1024,128]{3,2,1,0:T(8,128)(2,1)}) custom-call(s32[1]{0:T(128)} %bitcast.1.place_ref.me_ref, bf16[256,2048]{1,0:T(8,128)(2,1)} %copy-done.1, bf16[256,2048]{1,0:T(8,128)(2,1)} %collective-permute-done.refs_1_, ...), custom_call_target="tpu_custom_call" | custom-call | flops 201326592 | tf_op jit(solution)/shard_map/pallas_call | solution.py:148
  91.6 19.4 %shard_map.204 = (bf16[1024,512]{1,0:T(8,128)(2,1)}, f32[8,1024]{1,0:T(8,128)}, bf16[256,2048]{1,0:T(8,128)(2,1)}, bf16[256,2048]{1,0:T(8,128)(2,1)}, bf16[256,2...) custom-call(s32[1]{0:T(128)} %bitcast.1.place_ref.me_ref, bf16[1024,512]{1,0:T(8,128)(2,1)} %get-tuple-element.189.q_ref, ...), custom_call_target="tpu_custom_call" | custom-call | flops 268435456 | tf_op jit(solution)/shard_map/pallas_call | solution.py:234
  111.0 11.4 %collective-permute-done.5.refs_2_.refs_9_ = bf16[256,2048]{1,0:T(8,128)(2,1)} collective-permute-done((bf16[256,2048]{1,0:T(8,128)(2,1)}, bf16[256,2048]{1,0:T(8,128)(2,1)}, u32[]{:S(2)}, u32[]{:S(2)}) %collective-permute-start.5) | collective-permute-done | bytes 1048608 | tf_op jit(solution)/shard_map/ppermute | solution.py:772
  122.5 1.6 slice.192
  124.0 3.1 shard_map.206
  128.9 1.5 collective-permute-start.8
  131.3 11.6 %collective-permute-done.8.bottom_ref = bf16[128,2048]{1,0:T(8,128)(2,1)S(1)} collective-permute-done((bf16[128,2048]{1,0:T(8,128)(2,1)S(1)}, bf16[128,2048]{1,0:T(8,128)(2,1)S(1)}, u32[]{:S(2)}, u32[]{:S(2)}) %collective-permute-start.8) | collective-permute-done | bytes 524320 | tf_op jit(solution)/shard_map/ppermute | solution.py:772
  144.2 3.3 shard_map.205
  149.5 22.1 %collective-permute-done.9.refs_1_ = bf16[256,2048]{1,0:T(8,128)(2,1)S(1)} collective-permute-done((bf16[256,2048]{1,0:T(8,128)(2,1)}, bf16[256,2048]{1,0:T(8,128)(2,1)S(1)}, u32[]{:S(2)}, u32[]{:S(2)}) %collective-permute-start.9) | collective-permute-done | bytes 1048608 | tf_op jit(solution)/shard_map/ppermute | solution.py:772
  173.8 4.5 shard_map.207
  181.6 10.1 %collective-permute-done.15.refs_3_ = bf16[128,2048]{1,0:T(8,128)(2,1)S(1)} collective-permute-done((bf16[128,2048]{1,0:T(8,128)(2,1)S(1)}, bf16[128,2048]{1,0:T(8,128)(2,1)S(1)}, u32[]{:S(2)}, u32[]{:S(2)}) %collective-permute-start.15) | collective-permute-done | bytes 524320 | tf_op jit(solution)/shard_map/ppermute | solution.py:772
  196.5 1.4 slice.196.refs_6_
  197.9 9.2 %collective-permute-done.16.refs_1_ = bf16[128,2048]{1,0:T(8,128)(2,1)S(1)} collective-permute-done((bf16[128,2048]{1,0:T(8,128)(2,1)S(1)}, bf16[128,2048]{1,0:T(8,128)(2,1)S(1)}, u32[]{:S(2)}, u32[]{:S(2)}) %collective-permute-start.16) | collective-permute-done | bytes 524320 | tf_op jit(solution)/shard_map/ppermute | solution.py:772
  208.3 10.5 %collective-permute-done.19.refs_6_ = bf16[128,2048]{1,0:T(8,128)(2,1)S(1)} collective-permute-done((bf16[128,2048]{1,0:T(8,128)(2,1)S(1)}, bf16[128,2048]{1,0:T(8,128)(2,1)S(1)}, u32[]{:S(2)}, u32[]{:S(2)}) %collective-permute-start.19) | collective-permute-done | bytes 524320 | tf_op jit(solution)/shard_map/ppermute | solution.py:772
  219.8 3.0 shard_map.209
  222.8 37.2 %shard_map.208 = (bf16[1024,1024]{1,0:T(8,128)(2,1)}, bf16[1024,1024]{1,0:T(8,128)(2,1)}, bf16[1024,1024]{1,0:T(8,128)(2,1)}, bf16[1024,2048]{1,0:T(8,128)(2,1)}, bf16[1024,2048]{1,0:T(8,128)(2,1)}) custom-call(bf16[256,2048]{1,0:T(8,128)(2,1)} %get-tuple-element.221.refs_0_, bf16[128,2048]{1,0:T(8,128)(2,1)} %copy-done.28, bf16[128,2048]{1,0:T(8,128)(2,1)} %copy-done.27, ...), custom_call_target="tpu_custom_call" | custom-call | flops 25769803776 | tf_op jit(solution)/shard_map/pallas_call | solution.py:452
  261.1 5.7 collective-permute-done.22.refs_16_
  267.8 3.0 collective-permute-done.24.refs_18_
  270.8 23.8 %shard_map.210 = bf16[4,256,3072]{2,1,0:T(8,128)(2,1)} custom-call(bf16[256,2048]{1,0:T(8,128)(2,1)} %get-tuple-element.221.refs_0_, bf16[128,2048]{1,0:T(8,128)(2,1)} %copy-done.28, bf16[128,2048]{1,0:T(8,128)(2,1)} %copy-done.27, bf16[128,2048]{1,0:T(8,128)(2,1)} %copy-done.26, bf16[128,2048]{1,0:T(8,128)(2,1)} %copy-done.29, ...), custom_call_target="tpu_custom_call" | custom-call | flops 12884901888 | tf_op jit(solution)/shard_map/pallas_call | solution.py:653
  294.6 11.3 %all-gather.8.cloned.1.call-done.refs_11_.refs_12_.refs_13_ = bf16[1024,3072]{1,0:T(8,128)(2,1)} async-done(((bf16[256,3072]{1,0:T(8,128)(2,1)}), bf16[1024,3072]{1,0:T(8,128)(2,1)}) %all-gather.8.cloned.1.call-update) | async-done | bytes 6291472 | tf_op jit(solution)/shard_map/all_gather | solution.py:849
  306.1 2.4 collective-permute-start.28
  309.6 6.9 %collective-permute-done.25.refs_14_.refs_15_.refs_16_ = bf16[1024,3072]{1,0:T(8,128)(2,1)} collective-permute-done((bf16[1024,3072]{1,0:T(8,128)(2,1)}, bf16[1024,3072]{1,0:T(8,128)(2,1)}, u32[]{:S(2)}, u32[]{:S(2)}) %collective-permute-start.25) | collective-permute-done | bytes 6291488 | tf_op jit(solution)/shard_map/ppermute | solution.py:830
  316.5 40.8 %shard_map.211 = (bf16[1024,1024]{1,0:T(8,128)(2,1)}, bf16[1024,1024]{1,0:T(8,128)(2,1)}, bf16[1024,1024]{1,0:T(8,128)(2,1)}, bf16[256,2048]{1,0:T(8,128)(2,1)},...) custom-call(bf16[256,2048]{1,0:T(8,128)(2,1)} %get-tuple-element.221, ...), custom_call_target="tpu_custom_call" | custom-call | flops 25769803776 | tf_op jit(solution)/shard_map/pallas_call | solution.py:452
  359.4 1.5 collective-permute-start.30
  361.0 1.5 collective-permute-start.29
  362.4 2.3 slice.220.refs_10_
  364.7 8.9 %collective-permute-done.30.bottom_ref = bf16[128,2048]{1,0:T(8,128)(2,1)S(1)} collective-permute-done((bf16[128,2048]{1,0:T(8,128)(2,1)S(1)}, bf16[128,2048]{1,0:T(8,128)(2,1)S(1)}, u32[]{:S(2)}, u32[]{:S(2)}) %collective-permute-start.30) | collective-permute-done | bytes 524320 | tf_op jit(solution)/shard_map/ppermute | solution.py:772
  375.6 3.3 shard_map.212
  379.1 1.5 collective-permute-start.34
  381.3 23.7 %shard_map.213 = bf16[4,256,3072]{2,1,0:T(8,128)(2,1)} custom-call(bf16[256,2048]{1,0:T(8,128)(2,1)} %get-tuple-element.221.refs_0_, bf16[128,2048]{1,0:T(8,128)(2,1)} %copy-done.28, bf16[128,2048]{1,0:T(8,128)(2,1)} %copy-done.27, bf16[128,2048]{1,0:T(8,128)(2,1)} %copy-done.26, bf16[128,2048]{1,0:T(8,128)(2,1)} %copy-done.29, ...), custom_call_target="tpu_custom_call" | custom-call | flops 12884901888 | tf_op jit(solution)/shard_map/pallas_call | solution.py:653
  406.2 4.1 fusion.3
  412.1 9.7 %shard_map.214 = (f32[256,2048]{1,0:T(8,128)}, bf16[256,2048]{1,0:T(8,128)(2,1)}, f32[1,2048]{1,0:T(1,128)}, bf16[256,512]{1,0:T(8,128)(2,1)}, bf16[256,512]{1,0...) custom-call(bf16[256,2048]{1,0:T(8,128)(2,1)} %get-tuple-element.268.refs_0_, ...), custom_call_target="tpu_custom_call" | custom-call | flops 2147483648 | tf_op jit(solution)/shard_map/pallas_call | solution.py:607
  422.5 1.3 collective-permute-start.39
  426.0 17.2 %collective-permute-done.39.refs_1_ = bf16[256,512]{1,0:T(8,128)(2,1)S(1)} collective-permute-done((bf16[256,512]{1,0:T(8,128)(2,1)}, bf16[256,512]{1,0:T(8,128)(2,1)S(1)}, u32[]{:S(2)}, u32[]{:S(2)}) %collective-permute-start.39) | collective-permute-done | bytes 262176 | tf_op jit(solution)/shard_map/ppermute | solution.py:772
  443.2 4.1 collective-permute-done.41.refs_3_
  448.3 1.6 collective-permute-start.47
  450.5 1.3 collective-permute-start.45
  451.8 26.6 %shard_map.215.d_ref.refs_7_ = bf16[1024,768]{1,0:T(8,128)(2,1)} custom-call(s32[1]{0:T(128)} %bitcast.1.place_ref.me_ref, bf16[1024,512]{1,0:T(8,128)(2,1)} %get-tuple-element.189.q_ref, f32[8,1024]{1,0:T(8,128)} %get-tuple-element.285.l_ref, bf16[2,2,1024,128]{3,2,1,0:T(8,128)(2,1)} %get-tuple-element.190.k_ref, ...), custom_call_target="tpu_custom_call" | custom-call | flops 10737418240 | tf_op jit(solution)/shard_map/pallas_call | solution.py:369
  478.5 8.2 %shard_map.216 = (bf16[256,2048]{1,0:T(8,128)(2,1)}, bf16[256,2048]{1,0:T(8,128)(2,1)}, bf16[256,2048]{1,0:T(8,128)(2,1)}, bf16[256,2048]{1,0:T(8,128)(2,1)}) custom-call(bf16[1024,768]{1,0:T(8,128)(2,1)} %shard_map.215.d_ref.refs_7_, bf16[1024,1280]{1,0:T(8,128)(2,1)} %all-gather.4.cloned.1.call-done.refs_5_.refs_7_.wo_ref.qo_ref.kvo_ref.refs_11_.refs_12_, ...), custom_call_target="tpu_custom_call" | custom-call | flops 3221225472 | tf_op jit(solution)/shard_map/pallas_call | solution.py:759
  486.8 8.5 %collective-permute-done.46.refs_2_.refs_4_ = bf16[256,2048]{1,0:T(8,128)(2,1)S(1)} collective-permute-done((bf16[256,2048]{1,0:T(8,128)(2,1)}, bf16[256,2048]{1,0:T(8,128)(2,1)S(1)}, u32[]{:S(2)}, u32[]{:S(2)}) %collective-permute-start.46) | collective-permute-done | bytes 1048608 | tf_op jit(solution)/shard_map/ppermute | solution.py:772
  496.3 3.1 shard_map.218
  505.5 9.7 %collective-permute-done.49.bottom_ref = bf16[128,2048]{1,0:T(8,128)(2,1)} collective-permute-done((bf16[128,2048]{1,0:T(8,128)(2,1)}, bf16[128,2048]{1,0:T(8,128)(2,1)}, u32[]{:S(2)}, u32[]{:S(2)}) %collective-permute-start.49) | collective-permute-done | bytes 524320 | tf_op jit(solution)/shard_map/ppermute | solution.py:772
  516.2 3.3 shard_map.217
  520.6 11.7 %shard_map.219 = (bf16[4,256,1280]{2,1,0:T(8,128)(2,1)}, f32[4,256,128]{2,1,0:T(8,128)}) custom-call(bf16[1024,2048]{1,0:T(8,128)(2,1)} %get-tuple-element.209.refs_0_, bf16[1024,1024]{1,0:T(8,128)(2,1)} %copy-done.9, bf16[256,2048]{1,0:T(8,128)(2,1)} %get-tuple-element.303.refs_0_.refs_2_, bf16[256,2048]{1,0:T(8,128)(2,1)} %collective-permute-done.45.refs_1_.refs_3_, ...), custom_call_target="tpu_custom_call" | custom-call | flops 5368709120 | tf_op jit(solution)/shard_map/pallas_call | solution.py:699
  537.0 1.9 collective-permute-start.55
  538.9 2.5 collective-permute-start.56
  542.7 5.0 shard_map.220
  547.7 8.9 %collective-permute-done.52.refs_1_ = bf16[256,2048]{1,0:T(8,128)(2,1)S(1)} collective-permute-done((bf16[256,2048]{1,0:T(8,128)(2,1)}, bf16[256,2048]{1,0:T(8,128)(2,1)S(1)}, u32[]{:S(2)}, u32[]{:S(2)}) %collective-permute-start.52) | collective-permute-done | bytes 1048608 | tf_op jit(solution)/shard_map/ppermute | solution.py:772
  558.7 4.9 shard_map.221
  563.7 1.8 collective-permute-start.60
  567.3 14.1 %collective-permute-done.60 = f32[64,2]{0,1:T(2,128)S(1)} collective-permute-done((f32[64,2]{0,1:T(2,128)S(1)}, f32[64,2]{0,1:T(2,128)S(1)}, u32[]{:S(2)}, u32[]{:S(2)}) %collective-permute-start.60) | collective-permute-done | bytes 544 | tf_op jit(solution)/shard_map/ppermute | solution.py:772
  581.4 4.0 shard_map.222
  585.9 2.2 shard_map.223
  (249 shorter events, 65.9 us)
Async XLA Ops:
  7.2 65.8 %all-gather.4.cloned.1.call-start = ((), (), s32[]{:S(2)}) async-start(), calls=%async_computation.3 | async-start | bytes 3276800 | tf_op jit(solution)/shard_map/all_gather | solution.py:849
  11.7 30.3 %collective-permute-start.2 = (bf16[256,2048]{1,0:T(8,128)(2,1)S(1)}, bf16[256,2048]{1,0:T(8,128)(2,1)}, u32[]{:S(2)}, u32[]{:S(2)}) collective-permute-start(bf16[256,2048]{1,0:T(8,128)(2,1)S(1)} %select_dynamic-update-slice_fusion.8.refs_0_.refs_3_), channel_id=1, source_target_pairs={{0,3},{1,2},{2,1},{3,0},{4,7},{5,6},{6,5},{7,4},{8,11},{9,10},{10,... | collective-permute-start | bytes 3145736 | tf_op jit(solution)/shard_map/ppermute | solution.py:772
  15.7 45.7 %collective-permute-start.1 = (bf16[256,2048]{1,0:T(8,128)(2,1)S(1)}, bf16[256,2048]{1,0:T(8,128)(2,1)}, u32[]{:S(2)}, u32[]{:S(2)}) collective-permute-start(bf16[256,2048]{1,0:T(8,128)(2,1)S(1)} %select_dynamic-update-slice_fusion.8.refs_0_.refs_3_), channel_id=1, source_target_pairs={{0,2},{1,3},{2,0},{3,1},{4,6},{5,7},{6,4},{7,5},{8,10},{9,11},{10,... | collective-permute-start | bytes 3145736 | tf_op jit(solution)/shard_map/ppermute | solution.py:772
  16.2 45.5 %collective-permute-start = (bf16[256,2048]{1,0:T(8,128)(2,1)S(1)}, bf16[256,2048]{1,0:T(8,128)(2,1)}, u32[]{:S(2)}, u32[]{:S(2)}) collective-permute-start(bf16[256,2048]{1,0:T(8,128)(2,1)S(1)} %select_dynamic-update-slice_fusion.8.refs_0_.refs_3_), channel_id=1, source_target_pairs={{0,1},{1,0},{2,3},{3,2},{4,5},{5,4},{6,7},{7,6},{8,9},{9,8},{10,11... | collective-permute-start | bytes 3145736 | tf_op jit(solution)/shard_map/ppermute | solution.py:772
  16.4 175.9 %all-gather.6.cloned.1.call-start = ((), (), s32[]{:S(2)}) async-start(), calls=%async_computation.4 | async-start | bytes 7864320 | tf_op jit(solution)/shard_map/all_gather | solution.py:849
  73.0 232.9 %all-gather.8.cloned.1.call-start = ((), (), s32[]{:S(2)}) async-start(), calls=%async_computation.5 | async-start | bytes 7864320 | tf_op jit(solution)/shard_map/all_gather | solution.py:849
  73.1 5.2 collective-permute-start.3
  73.1 37.9 %collective-permute-start.6 = (bf16[256,2048]{1,0:T(8,128)(2,1)}, bf16[256,2048]{1,0:T(8,128)(2,1)}, u32[]{:S(2)}, u32[]{:S(2)}) collective-permute-start(bf16[256,2048]{1,0:T(8,128)(2,1)} %select_dynamic-update-slice_fusion.refs_0_.refs_7_.refs_4_), channel_id=1, source_target_pairs={{0,3},{1,2},{2,1},{3,0},{4,7},{5,6},{6,5},{7,4},{8,11},{9,10},{10,... | collective-permute-start | bytes 3145736 | tf_op jit(solution)/shard_map/ppermute | solution.py:772
  75.6 46.8 %collective-permute-start.5 = (bf16[256,2048]{1,0:T(8,128)(2,1)}, bf16[256,2048]{1,0:T(8,128)(2,1)}, u32[]{:S(2)}, u32[]{:S(2)}) collective-permute-start(bf16[256,2048]{1,0:T(8,128)(2,1)} %select_dynamic-update-slice_fusion.refs_0_.refs_7_.refs_4_), channel_id=1, source_target_pairs={{0,2},{1,3},{2,0},{3,1},{4,6},{5,7},{6,4},{7,5},{8,10},{9,11},{10,... | collective-permute-start | bytes 3145736 | tf_op jit(solution)/shard_map/ppermute | solution.py:772
  76.1 46.3 %collective-permute-start.4 = (bf16[256,2048]{1,0:T(8,128)(2,1)}, bf16[256,2048]{1,0:T(8,128)(2,1)}, u32[]{:S(2)}, u32[]{:S(2)}) collective-permute-start(bf16[256,2048]{1,0:T(8,128)(2,1)} %select_dynamic-update-slice_fusion.refs_0_.refs_7_.refs_4_), channel_id=1, source_target_pairs={{0,1},{1,0},{2,3},{3,2},{4,5},{5,4},{6,7},{7,6},{8,9},{9,8},{10,11... | collective-permute-start | bytes 3145736 | tf_op jit(solution)/shard_map/ppermute | solution.py:772
  127.2 45.6 %collective-permute-start.11 = (bf16[1024,1024]{1,0:T(8,128)(2,1)}, bf16[1024,1024]{1,0:T(8,128)(2,1)}, u32[]{:S(2)}, u32[]{:S(2)}) collective-permute-start(bf16[1024,1024]{1,0:T(8,128)(2,1)} %shard_map.206), channel_id=1, source_target_pairs={{0,4},{4,0},{8,12},{12,8},{16,20},{20,16},{24,28},{28,24},{1,5},{5... | collective-permute-start | bytes 6291464 | tf_op jit(solution)/shard_map/ppermute | solution.py:830
  127.2 45.6 %collective-permute-start.12 = (bf16[1024,1024]{1,0:T(8,128)(2,1)S(1)}, bf16[1024,1024]{1,0:T(8,128)(2,1)S(1)}, u32[]{:S(2)}, u32[]{:S(2)}) collective-permute-start(bf16[1024,1024]{1,0:T(8,128)(2,1)S(1)} %copy-done.10), channel_id=1, source_target_pairs={{0,4},{4,0},{8,12},{12,8},{16,20},{20,16},{24,28},{28,24},{1,5},{5... | collective-permute-start | bytes 6291464 | tf_op jit(solution)/shard_map/ppermute | solution.py:830
  128.9 14.0 %collective-permute-start.8 = (bf16[128,2048]{1,0:T(8,128)(2,1)S(1)}, bf16[128,2048]{1,0:T(8,128)(2,1)S(1)}, u32[]{:S(2)}, u32[]{:S(2)}) collective-permute-start(bf16[128,2048]{1,0:T(8,128)(2,1)S(1)} %get-tuple-element.355), channel_id=1, source_target_pairs={{0,2},{1,3},{2,0},{3,1},{4,6},{5,7},{6,4},{7,5},{8,10},{9,11},{10,... | collective-permute-start | bytes 1572872 | tf_op jit(solution)/shard_map/ppermute | solution.py:772
  130.4 13.7 %collective-permute-start.7 = (bf16[128,2048]{1,0:T(8,128)(2,1)S(1)}, bf16[128,2048]{1,0:T(8,128)(2,1)}, u32[]{:S(2)}, u32[]{:S(2)}) collective-permute-start(bf16[128,2048]{1,0:T(8,128)(2,1)S(1)} %get-tuple-element.356), channel_id=1, source_target_pairs={{0,1},{1,0},{2,3},{3,2},{4,5},{5,4},{6,7},{7,6},{8,9},{9,8},{10,11... | collective-permute-start | bytes 1572872 | tf_op jit(solution)/shard_map/ppermute | solution.py:772
  131.3 18.3 %collective-permute-start.13 = (bf16[1024,512]{1,0:T(8,128)(2,1)S(1)}, bf16[1024,512]{1,0:T(8,128)(2,1)}, u32[]{:S(2)}, u32[]{:S(2)}) collective-permute-start(bf16[1024,512]{1,0:T(8,128)(2,1)S(1)} %copy-done.12), channel_id=1, source_target_pairs={{0,4},{4,0},{8,12},{12,8},{16,20},{20,16},{24,28},{28,24},{1,5},{5... | collective-permute-start | bytes 3145736 | tf_op jit(solution)/shard_map/ppermute | solution.py:830
  147.5 24.2 %collective-permute-start.9 = (bf16[256,2048]{1,0:T(8,128)(2,1)}, bf16[256,2048]{1,0:T(8,128)(2,1)S(1)}, u32[]{:S(2)}, u32[]{:S(2)}) collective-permute-start(bf16[256,2048]{1,0:T(8,128)(2,1)} %get-tuple-element.203), channel_id=1, source_target_pairs={{0,1},{1,0},{2,3},{3,2},{4,5},{5,4},{6,7},{7,6},{8,9},{9,8},{10,11... | collective-permute-start | bytes 3145736 | tf_op jit(solution)/shard_map/ppermute | solution.py:772
  148.5 24.3 %collective-permute-start.10 = (bf16[256,2048]{1,0:T(8,128)(2,1)}, bf16[256,2048]{1,0:T(8,128)(2,1)S(1)}, u32[]{:S(2)}, u32[]{:S(2)}) collective-permute-start(bf16[256,2048]{1,0:T(8,128)(2,1)} %get-tuple-element.204), channel_id=1, source_target_pairs={{0,2},{1,3},{2,0},{3,1},{4,6},{5,7},{6,4},{7,5},{8,10},{9,11},{10,... | collective-permute-start | bytes 3145736 | tf_op jit(solution)/shard_map/ppermute | solution.py:772
  179.6 12.1 %collective-permute-start.15 = (bf16[128,2048]{1,0:T(8,128)(2,1)S(1)}, bf16[128,2048]{1,0:T(8,128)(2,1)S(1)}, u32[]{:S(2)}, u32[]{:S(2)}) collective-permute-start(bf16[128,2048]{1,0:T(8,128)(2,1)S(1)} %get-tuple-element.216), channel_id=1, source_target_pairs={{0,2},{1,3},{2,0},{3,1},{4,6},{5,7},{6,4},{7,5},{8,10},{9,11},{10,... | collective-permute-start | bytes 1572872 | tf_op jit(solution)/shard_map/ppermute | solution.py:772
  180.4 11.9 %collective-permute-start.14 = (bf16[128,2048]{1,0:T(8,128)(2,1)S(1)}, bf16[128,2048]{1,0:T(8,128)(2,1)S(1)}, u32[]{:S(2)}, u32[]{:S(2)}) collective-permute-start(bf16[128,2048]{1,0:T(8,128)(2,1)S(1)} %get-tuple-element.219), channel_id=1, source_target_pairs={{0,1},{1,0},{2,3},{3,2},{4,5},{5,4},{6,7},{7,6},{8,9},{9,8},{10,11... | collective-permute-start | bytes 1572872 | tf_op jit(solution)/shard_map/ppermute | solution.py:772
  192.3 26.6 %collective-permute-start.20 = (bf16[1024,3072]{1,0:T(8,128)(2,1)}, bf16[1024,3072]{1,0:T(8,128)(2,1)}, u32[]{:S(2)}, u32[]{:S(2)}) collective-permute-start(bf16[1024,3072]{1,0:T(8,128)(2,1)} %all-gather.6.cloned.1.call-done.refs_11_.refs_12_.refs_13_), channel_id=1, source_target_pairs={{0,4},{4,0},{8,12},{12,8},{16,20},{20,16},{24,28},{28,24},{1,5},{5... | collective-permute-start | bytes 18874376 | tf_op jit(solution)/shard_map/ppermute | solution.py:830
  192.3 286.2 %reduce-scatter.4.cloned.1.call-start = ((), (), s32[]{:S(2)}) async-start(), calls=%async_computation.6 | async-start | bytes 7864320 | tf_op jit(solution)/shard_map/reduce_scatter | solution.py:853
  192.4 14.8 %collective-permute-start.16 = (bf16[128,2048]{1,0:T(8,128)(2,1)S(1)}, bf16[128,2048]{1,0:T(8,128)(2,1)S(1)}, u32[]{:S(2)}, u32[]{:S(2)}) collective-permute-start(bf16[128,2048]{1,0:T(8,128)(2,1)S(1)} %get-tuple-element.216), channel_id=1, source_target_pairs={{0,1},{1,0},{2,3},{3,2},{4,5},{5,4},{6,7},{7,6},{8,9},{9,8},{10,11... | collective-permute-start | bytes 1572872 | tf_op jit(solution)/shard_map/ppermute | solution.py:772
  193.6 14.8 %collective-permute-start.17 = (bf16[128,2048]{1,0:T(8,128)(2,1)S(1)}, bf16[128,2048]{1,0:T(8,128)(2,1)S(1)}, u32[]{:S(2)}, u32[]{:S(2)}) collective-permute-start(bf16[128,2048]{1,0:T(8,128)(2,1)S(1)} %get-tuple-element.219), channel_id=1, source_target_pairs={{0,2},{1,3},{2,0},{3,1},{4,6},{5,7},{6,4},{7,5},{8,10},{9,11},{10,... | collective-permute-start | bytes 1572872 | tf_op jit(solution)/shard_map/ppermute | solution.py:772
  194.5 24.3 %collective-permute-start.19 = (bf16[128,2048]{1,0:T(8,128)(2,1)S(1)}, bf16[128,2048]{1,0:T(8,128)(2,1)S(1)}, u32[]{:S(2)}, u32[]{:S(2)}) collective-permute-start(bf16[128,2048]{1,0:T(8,128)(2,1)S(1)} %collective-permute-done.14.refs_2_), channel_id=1, source_target_pairs={{0,2},{1,3},{2,0},{3,1},{4,6},{5,7},{6,4},{7,5},{8,10},{9,11},{10,... | collective-permute-start | bytes 1572872 | tf_op jit(solution)/shard_map/ppermute | solution.py:772
  195.6 23.3 %collective-permute-start.18 = (bf16[128,2048]{1,0:T(8,128)(2,1)S(1)}, bf16[128,2048]{1,0:T(8,128)(2,1)S(1)}, u32[]{:S(2)}, u32[]{:S(2)}) collective-permute-start(bf16[128,2048]{1,0:T(8,128)(2,1)S(1)} %collective-permute-done.15.refs_3_), channel_id=1, source_target_pairs={{0,1},{1,0},{2,3},{3,2},{4,5},{5,4},{6,7},{7,6},{8,9},{9,8},{10,11... | collective-permute-start | bytes 1572872 | tf_op jit(solution)/shard_map/ppermute | solution.py:772
  222.8 37.2 %collective-permute-start.21 = (bf16[1024,1024]{1,0:T(8,128)(2,1)}, bf16[1024,1024]{1,0:T(8,128)(2,1)S(1)}, u32[]{:S(2)}, u32[]{:S(2)}) collective-permute-start(bf16[1024,1024]{1,0:T(8,128)(2,1)} %shard_map.209), channel_id=1, source_target_pairs={{0,4},{4,0},{8,12},{12,8},{16,20},{20,16},{24,28},{28,24},{1,5},{5... | collective-permute-start | bytes 6291464 | tf_op jit(solution)/shard_map/ppermute | solution.py:830
  260.1 6.8 %collective-permute-start.22 = (bf16[1024,1024]{1,0:T(8,128)(2,1)}, bf16[1024,1024]{1,0:T(8,128)(2,1)S(1)}, u32[]{:S(2)}, u32[]{:S(2)}) collective-permute-start(bf16[1024,1024]{1,0:T(8,128)(2,1)} %get-tuple-element.235.refs_13_), channel_id=1, source_target_pairs={{0,4},{4,0},{8,12},{12,8},{16,20},{20,16},{24,28},{28,24},{1,5},{5... | collective-permute-start | bytes 6291464 | tf_op jit(solution)/shard_map/ppermute | solution.py:830
  260.6 7.1 %collective-permute-start.23 = (bf16[1024,1024]{1,0:T(8,128)(2,1)}, bf16[1024,1024]{1,0:T(8,128)(2,1)}, u32[]{:S(2)}, u32[]{:S(2)}) collective-permute-start(bf16[1024,1024]{1,0:T(8,128)(2,1)} %get-tuple-element.236.refs_14_), channel_id=1, source_target_pairs={{0,4},{4,0},{8,12},{12,8},{16,20},{20,16},{24,28},{28,24},{1,5},{5... | collective-permute-start | bytes 6291464 | tf_op jit(solution)/shard_map/ppermute | solution.py:830
  260.7 10.0 %collective-permute-start.24 = (bf16[1024,1024]{1,0:T(8,128)(2,1)}, bf16[1024,1024]{1,0:T(8,128)(2,1)}, u32[]{:S(2)}, u32[]{:S(2)}) collective-permute-start(bf16[1024,1024]{1,0:T(8,128)(2,1)} %get-tuple-element.237.refs_15_), channel_id=1, source_target_pairs={{0,4},{4,0},{8,12},{12,8},{16,20},{20,16},{24,28},{28,24},{1,5},{5... | collective-permute-start | bytes 6291464 | tf_op jit(solution)/shard_map/ppermute | solution.py:830
  305.9 226.5 %reduce-scatter.6.cloned.1.call-start = ((), (), s32[]{:S(2)}) async-start(), calls=%async_computation.7 | async-start | bytes 7864320 | tf_op jit(solution)/shard_map/reduce_scatter | solution.py:853
  306.0 10.6 %collective-permute-start.25 = (bf16[1024,3072]{1,0:T(8,128)(2,1)}, bf16[1024,3072]{1,0:T(8,128)(2,1)}, u32[]{:S(2)}, u32[]{:S(2)}) collective-permute-start(bf16[1024,3072]{1,0:T(8,128)(2,1)} %all-gather.8.cloned.1.call-done.refs_11_.refs_12_.refs_13_), channel_id=1, source_target_pairs={{0,4},{4,0},{8,12},{12,8},{16,20},{20,16},{24,28},{28,24},{1,5},{5... | collective-permute-start | bytes 18874376 | tf_op jit(solution)/shard_map/ppermute | solution.py:830
  306.1 51.2 %collective-permute-start.28 = (bf16[1024,512]{1,0:T(8,128)(2,1)S(1)}, bf16[1024,512]{1,0:T(8,128)(2,1)S(1)}, u32[]{:S(2)}, u32[]{:S(2)}) collective-permute-start(bf16[1024,512]{1,0:T(8,128)(2,1)S(1)} %slice.196.refs_6_), channel_id=1, source_target_pairs={{0,3},{1,2},{2,1},{3,0},{4,7},{5,6},{6,5},{7,4},{8,11},{9,10},{10,... | collective-permute-start | bytes 3145736 | tf_op jit(solution)/shard_map/ppermute | solution.py:772
  308.5 48.8 %collective-permute-start.27 = (bf16[1024,512]{1,0:T(8,128)(2,1)S(1)}, bf16[1024,512]{1,0:T(8,128)(2,1)S(1)}, u32[]{:S(2)}, u32[]{:S(2)}) collective-permute-start(bf16[1024,512]{1,0:T(8,128)(2,1)S(1)} %slice.196.refs_6_), channel_id=1, source_target_pairs={{0,2},{1,3},{2,0},{3,1},{4,6},{5,7},{6,4},{7,5},{8,10},{9,11},{10,... | collective-permute-start | bytes 3145736 | tf_op jit(solution)/shard_map/ppermute | solution.py:772
  309.0 48.3 %collective-permute-start.26 = (bf16[1024,512]{1,0:T(8,128)(2,1)S(1)}, bf16[1024,512]{1,0:T(8,128)(2,1)}, u32[]{:S(2)}, u32[]{:S(2)}) collective-permute-start(bf16[1024,512]{1,0:T(8,128)(2,1)S(1)} %slice.196.refs_6_), channel_id=1, source_target_pairs={{0,1},{1,0},{2,3},{3,2},{4,5},{5,4},{6,7},{7,6},{8,9},{9,8},{10,11... | collective-permute-start | bytes 3145736 | tf_op jit(solution)/shard_map/ppermute | solution.py:772
  357.4 21.6 %collective-permute-start.31 = (bf16[1024,1024]{1,0:T(8,128)(2,1)}, bf16[1024,1024]{1,0:T(8,128)(2,1)}, u32[]{:S(2)}, u32[]{:S(2)}) collective-permute-start(bf16[1024,1024]{1,0:T(8,128)(2,1)} %get-tuple-element.258.refs_13_), channel_id=1, source_target_pairs={{0,4},{4,0},{8,12},{12,8},{16,20},{20,16},{24,28},{28,24},{1,5},{5... | collective-permute-start | bytes 6291464 | tf_op jit(solution)/shard_map/ppermute | solution.py:830
  357.6 21.5 %collective-permute-start.32 = (bf16[1024,1024]{1,0:T(8,128)(2,1)}, bf16[1024,1024]{1,0:T(8,128)(2,1)}, u32[]{:S(2)}, u32[]{:S(2)}) collective-permute-start(bf16[1024,1024]{1,0:T(8,128)(2,1)} %get-tuple-element.259.refs_14_), channel_id=1, source_target_pairs={{0,4},{4,0},{8,12},{12,8},{16,20},{20,16},{24,28},{28,24},{1,5},{5... | collective-permute-start | bytes 6291464 | tf_op jit(solution)/shard_map/ppermute | solution.py:830
  357.9 22.7 %collective-permute-start.33 = (bf16[1024,1024]{1,0:T(8,128)(2,1)}, bf16[1024,1024]{1,0:T(8,128)(2,1)}, u32[]{:S(2)}, u32[]{:S(2)}) collective-permute-start(bf16[1024,1024]{1,0:T(8,128)(2,1)} %get-tuple-element.260.refs_15_), channel_id=1, source_target_pairs={{0,4},{4,0},{8,12},{12,8},{16,20},{20,16},{24,28},{28,24},{1,5},{5... | collective-permute-start | bytes 6291464 | tf_op jit(solution)/shard_map/ppermute | solution.py:830
  359.4 14.2 %collective-permute-start.30 = (bf16[128,2048]{1,0:T(8,128)(2,1)S(1)}, bf16[128,2048]{1,0:T(8,128)(2,1)S(1)}, u32[]{:S(2)}, u32[]{:S(2)}) collective-permute-start(bf16[128,2048]{1,0:T(8,128)(2,1)S(1)} %get-tuple-element.351), channel_id=1, source_target_pairs={{0,2},{1,3},{2,0},{3,1},{4,6},{5,7},{6,4},{7,5},{8,10},{9,11},{10,... | collective-permute-start | bytes 1572872 | tf_op jit(solution)/shard_map/ppermute | solution.py:772
  361.0 13.9 %collective-permute-start.29 = (bf16[128,2048]{1,0:T(8,128)(2,1)S(1)}, bf16[128,2048]{1,0:T(8,128)(2,1)S(1)}, u32[]{:S(2)}, u32[]{:S(2)}) collective-permute-start(bf16[128,2048]{1,0:T(8,128)(2,1)S(1)} %get-tuple-element.352), channel_id=1, source_target_pairs={{0,1},{1,0},{2,3},{3,2},{4,5},{5,4},{6,7},{7,6},{8,9},{9,8},{10,11... | collective-permute-start | bytes 1572872 | tf_op jit(solution)/shard_map/ppermute | solution.py:772
  373.6 31.4 %collective-permute-start.36 = (bf16[1024,512]{1,0:T(8,128)(2,1)}, bf16[1024,512]{1,0:T(8,128)(2,1)S(1)}, u32[]{:S(2)}, u32[]{:S(2)}) collective-permute-start(bf16[1024,512]{1,0:T(8,128)(2,1)} %collective-permute-done.26.refs_7_), channel_id=1, source_target_pairs={{0,4},{4,0},{8,12},{12,8},{16,20},{20,16},{24,28},{28,24},{1,5},{5... | collective-permute-start | bytes 3145736 | tf_op jit(solution)/shard_map/ppermute | solution.py:830
  374.8 30.3 %collective-permute-start.37 = (bf16[1024,512]{1,0:T(8,128)(2,1)S(1)}, bf16[1024,512]{1,0:T(8,128)(2,1)}, u32[]{:S(2)}, u32[]{:S(2)}) collective-permute-start(bf16[1024,512]{1,0:T(8,128)(2,1)S(1)} %collective-permute-done.27.refs_8_), channel_id=1, source_target_pairs={{0,4},{4,0},{8,12},{12,8},{16,20},{20,16},{24,28},{28,24},{1,5},{5... | collective-permute-start | bytes 3145736 | tf_op jit(solution)/shard_map/ppermute | solution.py:830
  379.0 26.1 %collective-permute-start.38 = (bf16[1024,512]{1,0:T(8,128)(2,1)S(1)}, bf16[1024,512]{1,0:T(8,128)(2,1)}, u32[]{:S(2)}, u32[]{:S(2)}) collective-permute-start(bf16[1024,512]{1,0:T(8,128)(2,1)S(1)} %collective-permute-done.28.refs_9_), channel_id=1, source_target_pairs={{0,4},{4,0},{8,12},{12,8},{16,20},{20,16},{24,28},{28,24},{1,5},{5... | collective-permute-start | bytes 3145736 | tf_op jit(solution)/shard_map/ppermute | solution.py:830
  379.1 26.0 %collective-permute-start.34 = (bf16[256,2048]{1,0:T(8,128)(2,1)}, bf16[256,2048]{1,0:T(8,128)(2,1)}, u32[]{:S(2)}, u32[]{:S(2)}) collective-permute-start(bf16[256,2048]{1,0:T(8,128)(2,1)} %get-tuple-element.262), channel_id=1, source_target_pairs={{0,1},{1,0},{2,3},{3,2},{4,5},{5,4},{6,7},{7,6},{8,9},{9,8},{10,11... | collective-permute-start | bytes 3145736 | tf_op jit(solution)/shard_map/ppermute | solution.py:772
  380.6 25.5 %collective-permute-start.35 = (bf16[256,2048]{1,0:T(8,128)(2,1)}, bf16[256,2048]{1,0:T(8,128)(2,1)}, u32[]{:S(2)}, u32[]{:S(2)}) collective-permute-start(bf16[256,2048]{1,0:T(8,128)(2,1)} %get-tuple-element.263), channel_id=1, source_target_pairs={{0,2},{1,3},{2,0},{3,1},{4,6},{5,7},{6,4},{7,5},{8,10},{9,11},{10,... | collective-permute-start | bytes 3145736 | tf_op jit(solution)/shard_map/ppermute | solution.py:772
  406.2 179.8 %reduce-scatter.8.cloned.1.call-start = ((), (), s32[]{:S(2)}) async-start(), calls=%async_computation.8 | async-start | bytes 3276800 | tf_op jit(solution)/shard_map/reduce_scatter | solution.py:853
  410.3 37.0 %collective-permute-start.44 = (bf16[256,2048]{1,0:T(8,128)(2,1)S(1)}, bf16[256,2048]{1,0:T(8,128)(2,1)S(1)}, u32[]{:S(2)}, u32[]{:S(2)}) collective-permute-start(bf16[256,2048]{1,0:T(8,128)(2,1)S(1)} %get-tuple-element.346), channel_id=1, source_target_pairs={{0,2},{1,3},{2,0},{3,1},{4,6},{5,7},{6,4},{7,5},{8,10},{9,11},{10,... | collective-permute-start | bytes 3145736 | tf_op jit(solution)/shard_map/ppermute | solution.py:772
  411.5 35.9 %collective-permute-start.43 = (bf16[256,2048]{1,0:T(8,128)(2,1)S(1)}, bf16[256,2048]{1,0:T(8,128)(2,1)S(1)}, u32[]{:S(2)}, u32[]{:S(2)}) collective-permute-start(bf16[256,2048]{1,0:T(8,128)(2,1)S(1)} %get-tuple-element.347), channel_id=1, source_target_pairs={{0,1},{1,0},{2,3},{3,2},{4,5},{5,4},{6,7},{7,6},{8,9},{9,8},{10,11... | collective-permute-start | bytes 3145736 | tf_op jit(solution)/shard_map/ppermute | solution.py:772
  422.5 20.6 %collective-permute-start.39 = (bf16[256,512]{1,0:T(8,128)(2,1)}, bf16[256,512]{1,0:T(8,128)(2,1)S(1)}, u32[]{:S(2)}, u32[]{:S(2)}) collective-permute-start(bf16[256,512]{1,0:T(8,128)(2,1)} %get-tuple-element.278), channel_id=1, source_target_pairs={{0,1},{1,0},{2,3},{3,2},{4,5},{5,4},{6,7},{7,6},{8,9},{9,8},{10,11... | collective-permute-start | bytes 786440 | tf_op jit(solution)/shard_map/ppermute | solution.py:772
  423.8 19.3 %collective-permute-start.40 = (bf16[256,512]{1,0:T(8,128)(2,1)}, bf16[256,512]{1,0:T(8,128)(2,1)S(1)}, u32[]{:S(2)}, u32[]{:S(2)}) collective-permute-start(bf16[256,512]{1,0:T(8,128)(2,1)} %get-tuple-element.279), channel_id=1, source_target_pairs={{0,2},{1,3},{2,0},{3,1},{4,6},{5,7},{6,4},{7,5},{8,10},{9,11},{10,... | collective-permute-start | bytes 786440 | tf_op jit(solution)/shard_map/ppermute | solution.py:772
  424.7 22.6 %collective-permute-start.41 = (bf16[256,512]{1,0:T(8,128)(2,1)}, bf16[256,512]{1,0:T(8,128)(2,1)S(1)}, u32[]{:S(2)}, u32[]{:S(2)}) collective-permute-start(bf16[256,512]{1,0:T(8,128)(2,1)} %get-tuple-element.280), channel_id=1, source_target_pairs={{0,3},{1,2},{2,1},{3,0},{4,7},{5,6},{6,5},{7,4},{8,11},{9,10},{10,... | collective-permute-start | bytes 786440 | tf_op jit(solution)/shard_map/ppermute | solution.py:772
  448.3 38.4 %collective-permute-start.47 = (bf16[256,2048]{1,0:T(8,128)(2,1)}, bf16[256,2048]{1,0:T(8,128)(2,1)S(1)}, u32[]{:S(2)}, u32[]{:S(2)}) collective-permute-start(bf16[256,2048]{1,0:T(8,128)(2,1)} %get-tuple-element.303.refs_0_.refs_2_), channel_id=1, source_target_pairs={{0,3},{1,2},{2,1},{3,0},{4,7},{5,6},{6,5},{7,4},{8,11},{9,10},{10,... | collective-permute-start | bytes 3145736 | tf_op jit(solution)/shard_map/ppermute | solution.py:772
  450.0 45.3 %collective-permute-start.46 = (bf16[256,2048]{1,0:T(8,128)(2,1)}, bf16[256,2048]{1,0:T(8,128)(2,1)S(1)}, u32[]{:S(2)}, u32[]{:S(2)}) collective-permute-start(bf16[256,2048]{1,0:T(8,128)(2,1)} %get-tuple-element.303.refs_0_.refs_2_), channel_id=1, source_target_pairs={{0,2},{1,3},{2,0},{3,1},{4,6},{5,7},{6,4},{7,5},{8,10},{9,11},{10,... | collective-permute-start | bytes 3145736 | tf_op jit(solution)/shard_map/ppermute | solution.py:772
  450.5 45.3 %collective-permute-start.45 = (bf16[256,2048]{1,0:T(8,128)(2,1)}, bf16[256,2048]{1,0:T(8,128)(2,1)}, u32[]{:S(2)}, u32[]{:S(2)}) collective-permute-start(bf16[256,2048]{1,0:T(8,128)(2,1)} %get-tuple-element.303.refs_0_.refs_2_), channel_id=1, source_target_pairs={{0,1},{1,0},{2,3},{3,2},{4,5},{5,4},{6,7},{7,6},{8,9},{9,8},{10,11... | collective-permute-start | bytes 3145736 | tf_op jit(solution)/shard_map/ppermute | solution.py:772
  499.4 20.1 %collective-permute-start.50 = (bf16[1024,1024]{1,0:T(8,128)(2,1)}, bf16[1024,1024]{1,0:T(8,128)(2,1)}, u32[]{:S(2)}, u32[]{:S(2)}) collective-permute-start(bf16[1024,1024]{1,0:T(8,128)(2,1)} %shard_map.218), channel_id=1, source_target_pairs={{0,4},{4,0},{8,12},{12,8},{16,20},{20,16},{24,28},{28,24},{1,5},{5... | collective-permute-start | bytes 6291464 | tf_op jit(solution)/shard_map/ppermute | solution.py:830
  499.5 20.0 %collective-permute-start.51 = (bf16[1024,768]{1,0:T(8,128)(2,1)S(1)}, bf16[1024,768]{1,0:T(8,128)(2,1)S(1)}, u32[]{:S(2)}, u32[]{:S(2)}) collective-permute-start(bf16[1024,768]{1,0:T(8,128)(2,1)S(1)} %copy-done.3), channel_id=1, source_target_pairs={{0,4},{4,0},{8,12},{12,8},{16,20},{20,16},{24,28},{28,24},{1,5},{5... | collective-permute-start | bytes 4718600 | tf_op jit(solution)/shard_map/ppermute | solution.py:830
  501.0 14.3 %collective-permute-start.49 = (bf16[128,2048]{1,0:T(8,128)(2,1)}, bf16[128,2048]{1,0:T(8,128)(2,1)}, u32[]{:S(2)}, u32[]{:S(2)}) collective-permute-start(bf16[128,2048]{1,0:T(8,128)(2,1)} %get-tuple-element.349), channel_id=1, source_target_pairs={{0,2},{1,3},{2,0},{3,1},{4,6},{5,7},{6,4},{7,5},{8,10},{9,11},{10,... | collective-permute-start | bytes 1572872 | tf_op jit(solution)/shard_map/ppermute | solution.py:772
  502.3 13.9 %collective-permute-start.48 = (bf16[128,2048]{1,0:T(8,128)(2,1)}, bf16[128,2048]{1,0:T(8,128)(2,1)}, u32[]{:S(2)}, u32[]{:S(2)}) collective-permute-start(bf16[128,2048]{1,0:T(8,128)(2,1)} %get-tuple-element.350), channel_id=1, source_target_pairs={{0,1},{1,0},{2,3},{3,2},{4,5},{5,4},{6,7},{7,6},{8,9},{9,8},{10,11... | collective-permute-start | bytes 1572872 | tf_op jit(solution)/shard_map/ppermute | solution.py:772
  532.4 24.2 %collective-permute-start.52 = (bf16[256,2048]{1,0:T(8,128)(2,1)}, bf16[256,2048]{1,0:T(8,128)(2,1)S(1)}, u32[]{:S(2)}, u32[]{:S(2)}) collective-permute-start(bf16[256,2048]{1,0:T(8,128)(2,1)} %get-tuple-element.311), channel_id=1, source_target_pairs={{0,1},{1,0},{2,3},{3,2},{4,5},{5,4},{6,7},{7,6},{8,9},{9,8},{10,11... | collective-permute-start | bytes 3145736 | tf_op jit(solution)/shard_map/ppermute | solution.py:772
  533.6 23.9 %collective-permute-start.53 = (bf16[256,2048]{1,0:T(8,128)(2,1)}, bf16[256,2048]{1,0:T(8,128)(2,1)S(1)}, u32[]{:S(2)}, u32[]{:S(2)}) collective-permute-start(bf16[256,2048]{1,0:T(8,128)(2,1)} %get-tuple-element.312), channel_id=1, source_target_pairs={{0,2},{1,3},{2,0},{3,1},{4,6},{5,7},{6,4},{7,5},{8,10},{9,11},{10,... | collective-permute-start | bytes 3145736 | tf_op jit(solution)/shard_map/ppermute | solution.py:772
  536.0 5.5 collective-permute-start.54
  557.5 23.9 %collective-permute-start.57 = (bf16[256,2048]{1,0:T(8,128)(2,1)S(1)}, bf16[256,2048]{1,0:T(8,128)(2,1)}, u32[]{:S(2)}, u32[]{:S(2)}) collective-permute-start(bf16[256,2048]{1,0:T(8,128)(2,1)S(1)} %copy-done.24), channel_id=1, source_target_pairs={{0,3},{1,2},{2,1},{3,0},{4,7},{5,6},{6,5},{7,4},{8,11},{9,10},{10,... | collective-permute-start | bytes 3145736 | tf_op jit(solution)/shard_map/ppermute | solution.py:772
  563.7 17.7 %collective-permute-start.60 = (f32[64,2]{0,1:T(2,128)S(1)}, f32[64,2]{0,1:T(2,128)S(1)}, u32[]{:S(2)}, u32[]{:S(2)}) collective-permute-start(f32[64,2]{0,1:T(2,128)S(1)} %bitcast.47), channel_id=1, source_target_pairs={{0,3},{1,2},{2,1},{3,0},{4,7},{5,6},{6,5},{7,4},{8,11},{9,10},{10,... | collective-permute-start | bytes 1544 | tf_op jit(solution)/shard_map/ppermute | solution.py:772
  565.5 15.9 %collective-permute-start.58 = (f32[64,2]{0,1:T(2,128)S(1)}, f32[64,2]{0,1:T(2,128)S(1)}, u32[]{:S(2)}, u32[]{:S(2)}) collective-permute-start(f32[64,2]{0,1:T(2,128)S(1)} %bitcast.46), channel_id=1, source_target_pairs={{0,1},{1,0},{2,3},{3,2},{4,5},{5,4},{6,7},{7,6},{8,9},{9,8},{10,11... | collective-permute-start | bytes 1544 | tf_op jit(solution)/shard_map/ppermute | solution.py:772
  566.3 15.1 %collective-permute-start.59 = (f32[64,2]{0,1:T(2,128)S(1)}, f32[64,2]{0,1:T(2,128)S(1)}, u32[]{:S(2)}, u32[]{:S(2)}) collective-permute-start(f32[64,2]{0,1:T(2,128)S(1)} %bitcast.45), channel_id=1, source_target_pairs={{0,2},{1,3},{2,0},{3,1},{4,6},{5,7},{6,4},{7,5},{8,10},{9,11},{10,... | collective-permute-start | bytes 1544 | tf_op jit(solution)/shard_map/ppermute | solution.py:772
  (47 other events, 444.6 us)
Sparse Core Ops, SparseCore 0:
  16.5 56.4 all-gather.3
  75.1 114.1 all-gather.5
  192.5 113.3 all-gather.7
  308.0 108.9 reduce-scatter.3
  419.2 111.2 reduce-scatter.5
  532.7 52.5 reduce-scatter.7
where the time goes:
time: 604 us; the launch traced here: 595 us
  Pallas kernels  253 us (42%)
  waiting for transfers between devices  216 us (36%)
  starting transfers between devices  53.9 us (9%)
  local copies, waits for them, and re-layouts  30.1 us (5%)
  between operations  15 us (2%)
  other arithmetic  14.6 us (2%)
  blocking collectives  12.4 us (2%)
    ppermute x39, waiting for transfers between devices, swap(): return lax.ppermute(values, 'tensor', [(i, i ^ step) for i in range(size)])  175 us
    pallas_call x2, Pallas kernels, mlp(): pl.pallas_call(functools.partial(mlp_kernel, n_counts=[len(group) for gro...  78 us
    pallas_call x2, Pallas kernels, mlp_grads(): pl.pallas_call(functools.partial(grad_kernel, n_count=len(tokens), e_coun...  47.6 us
    ppermute x39, starting transfers between devices, swap(): return lax.ppermute(values, 'tensor', [(i, i ^ step) for i in range(size)])  45.2 us
    pallas_call x1, Pallas kernels, attend_back(): pl.pallas_call(functools.partial(attend_back_kernel, size=size, heads=hea...  26.6 us
    all_gather x3, waiting for transfers between devices, gather(): lax.all_gather(values, 'dp', axis=0, tiled=True, axis_index_groups=chip_l...  22.5 us
    pallas_call x1, Pallas kernels, attend(): pl.pallas_call(functools.partial(attend_kernel, size=size, heads=heads, g...  19.4 us
    ppermute x19, waiting for transfers between devices, cross(): return lax.ppermute(values, 'dp', [(i, i ^ 1) for i in range(count)])  17.5 us
  transfers between devices with their start and end apart: 67, of which 34 were waited for; matrix products, arithmetic and copies ran while one was open for 6% of the time, Pallas kernels for 42%

commit v1 on v0

--- a/solution.py
+++ b/solution.py
@@ -477,9 +477,9 @@
 
 def store_by_device(out_ref, values, core, chips):
     width = values.shape[1] // (2 * chips)
-    for chip in range(chips):
-        own = values[:, chip * width : (chip + 1) * width]
-        other = values[:, (chips + chip) * width : (chips + chip + 1) * width]
+    for place, chip in enumerate(ring_order(chips)):
+        own = values[:, place * width : (place + 1) * width]
+        other = values[:, (chips + place) * width : (chips + place + 1) * width]
         low = 2 * chip * width
         out_ref[:, low : low + width] = jnp.where(core == 0, own, other)
         out_ref[:, low + width : low + 2 * width] = jnp.where(core == 0, other, own)
@@ -840,9 +840,13 @@
     )
 
 
+def ring_order(chips):
+    return list(range(0, chips, 2)) + list(range(1, chips, 2))[::-1]
+
+
 def chip_lines():
-    count = lax.axis_size("dp")
-    return [list(range(core, count, 2)) for core in range(2)]
+    chips = lax.axis_size("dp") // 2
+    return [[2 * chip + core for chip in ring_order(chips)] for core in range(2)]
 
 
 def gather(values):
@@ -864,10 +868,12 @@
 def line_parts(parts):
     chips = lax.axis_size("dp") // 2
     chip = lax.axis_index("dp") // 2
-    blocks = [lax.dynamic_index_in_dim(parts, chip, 0, keepdims=False)]
-    for step in range(1, chips):
-        sent = lax.dynamic_index_in_dim(parts, (chip + step) % chips, 0, keepdims=False)
-        blocks.append(along(sent, step))
+    order = ring_order(chips)
+    places = jnp.array([order.index(c % chips) for c in range(2 * chips)], jnp.int32)
+    blocks = []
+    for step in range(chips):
+        sent = lax.dynamic_index_in_dim(parts, places[chip + step], 0, keepdims=False)
+        blocks.append(along(sent, step) if step else sent)
     return blocks
 
 
@@ -912,7 +918,7 @@
 
 def by_core(values, core):
     blocks = feature_blocks(values)
-    pairs = list(zip(blocks[0::2], blocks[1::2]))
+    pairs = [(blocks[2 * chip], blocks[2 * chip + 1]) for chip in ring_order(len(blocks) // 2)]
     own = [jnp.where(core == 0, even, odd) for even, odd in pairs]
     other = [jnp.where(core == 0, odd, even) for even, odd in pairs]
     return jnp.concatenate(own + other, axis=-1)

time: 604 us -> 604 us (level)
  between operations: 15 us -> 22.8 us
  waiting for transfers between devices: 216 us -> 209 us
    ppermute x39, waiting for transfers between devices: 175 us -> 168 us  [swap(): return lax.ppermute(values, 'tensor', [(i, i ^ step) for i in range(size)])]
  transfers between devices with their start and end apart: 67 -> 67, of which waited for: 34 -> 35; matrix products, arithmetic and copies ran while one was open for 6% -> 6% of each run, Pallas kernels for 42% -> 42%
where the time goes in v1:
time: 604 us; the launch traced here: 596 us
  Pallas kernels  253 us (42%)
  waiting for transfers between devices  209 us (35%)
  starting transfers between devices  53.7 us (9%)
  local copies, waits for them, and re-layouts  30.8 us (5%)
  between operations  22.8 us (4%)
  other arithmetic  14.6 us (2%)
  blocking collectives  12.4 us (2%)
    ppermute x39, waiting for transfers between devices, swap(): return lax.ppermute(values, 'tensor', [(i, i ^ step) for i in range(size)])  168 us
    pallas_call x2, Pallas kernels, mlp(): pl.pallas_call(functools.partial(mlp_kernel, n_counts=[len(group) for gro...  78 us
    pallas_call x2, Pallas kernels, mlp_grads(): pl.pallas_call(functools.partial(grad_kernel, n_count=len(tokens), e_coun...  47.6 us
    ppermute x39, starting transfers between devices, swap(): return lax.ppermute(values, 'tensor', [(i, i ^ step) for i in range(size)])  46 us
    pallas_call x1, Pallas kernels, attend_back(): pl.pallas_call(functools.partial(attend_back_kernel, size=size, heads=hea...  26.6 us
    all_gather x3, waiting for transfers between devices, gather(): lax.all_gather(values, 'dp', axis=0, tiled=True, axis_index_groups=chip_l...  21.4 us
    pallas_call x1, Pallas kernels, attend(): pl.pallas_call(functools.partial(attend_kernel, size=size, heads=heads, g...  19.3 us
    ppermute x19, waiting for transfers between devices, cross(): return lax.ppermute(values, 'dp', [(i, i ^ 1) for i in range(count)])  17.5 us
  transfers between devices with their start and end apart: 67, of which 35 were waited for; matrix products, arithmetic and copies ran while one was open for 6% of the time, Pallas kernels for 42%

profile of v1, /device:TPU:0, one launch (start us, length us, event | category | flops | bytes accessed | tf_op | source)
XLA Modules:
  0.0 595.8 jit_solution(15904018433779471663)
XLA Ops:
  8.4 1.9 pad_maximum_fusion.2
  11.7 4.0 collective-permute-start.2
  16.5 12.4 %all_gather.13 = bf16[2,2048]{1,0:T(2,128)(2,1)S(1)} all-gather(bf16[2,256]{1,0:T(2,128)(2,1)S(1)} %pad_maximum_fusion.5), channel_id=1, replica_groups=mesh['dp'=8,'tensor'=4] {'dp'}, dimensions={1}, use_global_device_ids=true | all-gather | bytes 9216 | tf_op jit(solution)/shard_map/all_gather | solution.py:957
  29.0 1.5 copy.38
  36.3 1.9 fusion
  38.2 1.8 pad_maximum_fusion.3
  40.3 1.8 pad_maximum_fusion
  42.1 19.4 %collective-permute-done.1.refs_2_ = bf16[256,2048]{1,0:T(8,128)(2,1)} collective-permute-done((bf16[256,2048]{1,0:T(8,128)(2,1)S(1)}, bf16[256,2048]{1,0:T(8,128)(2,1)}, u32[]{:S(2)}, u32[]{:S(2)}) %collective-permute-start.1) | collective-permute-done | bytes 1048608 | tf_op jit(solution)/shard_map/ppermute | solution.py:772
  61.7 10.7 %all-gather.4.cloned.1.call-done.refs_5_.refs_7_.wo_ref.qo_ref.kvo_ref.refs_11_.refs_12_ = bf16[1024,1280]{1,0:T(8,128)(2,1)} async-done(((bf16[256,1280]{1,0:T(8,128)(2,1)}), bf16[1024,1280]{1,0:T(8,128)(2,1)}) %all-gather.4.cloned.1.call-update) | async-done | bytes 2621456 | tf_op jit(solution)/shard_map/all_gather | solution.py:853
  72.6 2.4 collective-permute-start.6
  77.7 1.5 copy-done
  79.2 11.8 %shard_map.212 = (bf16[1024,2048]{1,0:T(8,128)(2,1)}, bf16[1024,512]{1,0:T(8,128)(2,1)}, bf16[2,2,1024,128]{3,2,1,0:T(8,128)(2,1)}, bf16[2,2,1024,128]{3,2,1,0:T(8,128)(2,1)}) custom-call(s32[1]{0:T(128)} %bitcast.1.place_ref.me_ref, bf16[256,2048]{1,0:T(8,128)(2,1)} %copy-done.1, bf16[256,2048]{1,0:T(8,128)(2,1)} %collective-permute-done.refs_1_, ...), custom_call_target="tpu_custom_call" | custom-call | flops 201326592 | tf_op jit(solution)/shard_map/pallas_call | solution.py:148
  91.0 19.3 %shard_map.213 = (bf16[1024,512]{1,0:T(8,128)(2,1)}, f32[8,1024]{1,0:T(8,128)}, bf16[256,2048]{1,0:T(8,128)(2,1)}, bf16[256,2048]{1,0:T(8,128)(2,1)}, bf16[256,2...) custom-call(s32[1]{0:T(128)} %bitcast.1.place_ref.me_ref, bf16[1024,512]{1,0:T(8,128)(2,1)} %get-tuple-element.189.q_ref, ...), custom_call_target="tpu_custom_call" | custom-call | flops 268435456 | tf_op jit(solution)/shard_map/pallas_call | solution.py:234
  110.4 11.5 %collective-permute-done.5.refs_2_.refs_9_ = bf16[256,2048]{1,0:T(8,128)(2,1)} collective-permute-done((bf16[256,2048]{1,0:T(8,128)(2,1)}, bf16[256,2048]{1,0:T(8,128)(2,1)}, u32[]{:S(2)}, u32[]{:S(2)}) %collective-permute-start.5) | collective-permute-done | bytes 1048608 | tf_op jit(solution)/shard_map/ppermute | solution.py:772
  121.9 1.6 slice.192
  123.5 3.1 shard_map.215
  128.4 1.5 collective-permute-start.8
  130.7 11.6 %collective-permute-done.8.bottom_ref = bf16[128,2048]{1,0:T(8,128)(2,1)S(1)} collective-permute-done((bf16[128,2048]{1,0:T(8,128)(2,1)S(1)}, bf16[128,2048]{1,0:T(8,128)(2,1)S(1)}, u32[]{:S(2)}, u32[]{:S(2)}) %collective-permute-start.8) | collective-permute-done | bytes 524320 | tf_op jit(solution)/shard_map/ppermute | solution.py:772
  143.6 3.3 shard_map.214
  149.0 22.1 %collective-permute-done.9.refs_1_ = bf16[256,2048]{1,0:T(8,128)(2,1)S(1)} collective-permute-done((bf16[256,2048]{1,0:T(8,128)(2,1)}, bf16[256,2048]{1,0:T(8,128)(2,1)S(1)}, u32[]{:S(2)}, u32[]{:S(2)}) %collective-permute-start.9) | collective-permute-done | bytes 1048608 | tf_op jit(solution)/shard_map/ppermute | solution.py:772
  173.2 4.5 shard_map.216
  181.1 10.1 %collective-permute-done.15.refs_3_ = bf16[128,2048]{1,0:T(8,128)(2,1)S(1)} collective-permute-done((bf16[128,2048]{1,0:T(8,128)(2,1)S(1)}, bf16[128,2048]{1,0:T(8,128)(2,1)S(1)}, u32[]{:S(2)}, u32[]{:S(2)}) %collective-permute-start.15) | collective-permute-done | bytes 524320 | tf_op jit(solution)/shard_map/ppermute | solution.py:772
  195.9 1.4 slice.196.refs_6_
  197.3 9.2 %collective-permute-done.16.refs_1_ = bf16[128,2048]{1,0:T(8,128)(2,1)S(1)} collective-permute-done((bf16[128,2048]{1,0:T(8,128)(2,1)S(1)}, bf16[128,2048]{1,0:T(8,128)(2,1)S(1)}, u32[]{:S(2)}, u32[]{:S(2)}) %collective-permute-start.16) | collective-permute-done | bytes 524320 | tf_op jit(solution)/shard_map/ppermute | solution.py:772
  207.8 10.5 %collective-permute-done.19.refs_6_ = bf16[128,2048]{1,0:T(8,128)(2,1)S(1)} collective-permute-done((bf16[128,2048]{1,0:T(8,128)(2,1)S(1)}, bf16[128,2048]{1,0:T(8,128)(2,1)S(1)}, u32[]{:S(2)}, u32[]{:S(2)}) %collective-permute-start.19) | collective-permute-done | bytes 524320 | tf_op jit(solution)/shard_map/ppermute | solution.py:772
  219.3 3.0 shard_map.218
  222.3 37.2 %shard_map.217 = (bf16[1024,1024]{1,0:T(8,128)(2,1)}, bf16[1024,1024]{1,0:T(8,128)(2,1)}, bf16[1024,1024]{1,0:T(8,128)(2,1)}, bf16[1024,2048]{1,0:T(8,128)(2,1)}, bf16[1024,2048]{1,0:T(8,128)(2,1)}) custom-call(bf16[256,2048]{1,0:T(8,128)(2,1)} %get-tuple-element.221.refs_0_, bf16[128,2048]{1,0:T(8,128)(2,1)} %copy-done.28, bf16[128,2048]{1,0:T(8,128)(2,1)} %copy-done.27, ...), custom_call_target="tpu_custom_call" | custom-call | flops 25769803776 | tf_op jit(solution)/shard_map/pallas_call | solution.py:452
  260.6 5.7 collective-permute-done.22.refs_16_
  267.2 3.0 collective-permute-done.24.refs_18_
  270.2 23.9 %shard_map.219 = bf16[4,256,3072]{2,1,0:T(8,128)(2,1)} custom-call(bf16[256,2048]{1,0:T(8,128)(2,1)} %get-tuple-element.221.refs_0_, bf16[128,2048]{1,0:T(8,128)(2,1)} %copy-done.28, bf16[128,2048]{1,0:T(8,128)(2,1)} %copy-done.27, bf16[128,2048]{1,0:T(8,128)(2,1)} %copy-done.26, bf16[128,2048]{1,0:T(8,128)(2,1)} %copy-done.29, ...), custom_call_target="tpu_custom_call" | custom-call | flops 12884901888 | tf_op jit(solution)/shard_map/pallas_call | solution.py:653
  294.1 10.7 %all-gather.8.cloned.1.call-done.refs_11_.refs_12_.refs_13_ = bf16[1024,3072]{1,0:T(8,128)(2,1)} async-done(((bf16[256,3072]{1,0:T(8,128)(2,1)}), bf16[1024,3072]{1,0:T(8,128)(2,1)}) %all-gather.8.cloned.1.call-update) | async-done | bytes 6291472 | tf_op jit(solution)/shard_map/all_gather | solution.py:853
  304.9 2.4 collective-permute-start.28
  308.5 6.9 %collective-permute-done.25.refs_14_.refs_15_.refs_16_ = bf16[1024,3072]{1,0:T(8,128)(2,1)} collective-permute-done((bf16[1024,3072]{1,0:T(8,128)(2,1)}, bf16[1024,3072]{1,0:T(8,128)(2,1)}, u32[]{:S(2)}, u32[]{:S(2)}) %collective-permute-start.25) | collective-permute-done | bytes 6291488 | tf_op jit(solution)/shard_map/ppermute | solution.py:830
  315.4 40.8 %shard_map.220 = (bf16[1024,1024]{1,0:T(8,128)(2,1)}, bf16[1024,1024]{1,0:T(8,128)(2,1)}, bf16[1024,1024]{1,0:T(8,128)(2,1)}, bf16[256,2048]{1,0:T(8,128)(2,1)},...) custom-call(bf16[256,2048]{1,0:T(8,128)(2,1)} %get-tuple-element.221, ...), custom_call_target="tpu_custom_call" | custom-call | flops 25769803776 | tf_op jit(solution)/shard_map/pallas_call | solution.py:452
  358.2 1.5 collective-permute-start.30
  359.7 1.5 collective-permute-start.29
  361.2 2.3 slice.220.refs_10_
  363.5 9.0 %collective-permute-done.30.bottom_ref = bf16[128,2048]{1,0:T(8,128)(2,1)S(1)} collective-permute-done((bf16[128,2048]{1,0:T(8,128)(2,1)S(1)}, bf16[128,2048]{1,0:T(8,128)(2,1)S(1)}, u32[]{:S(2)}, u32[]{:S(2)}) %collective-permute-start.30) | collective-permute-done | bytes 524320 | tf_op jit(solution)/shard_map/ppermute | solution.py:772
  374.5 3.4 shard_map.221
  378.0 1.5 collective-permute-start.34
  380.2 23.7 %shard_map.222 = bf16[4,256,3072]{2,1,0:T(8,128)(2,1)} custom-call(bf16[256,2048]{1,0:T(8,128)(2,1)} %get-tuple-element.221.refs_0_, bf16[128,2048]{1,0:T(8,128)(2,1)} %copy-done.28, bf16[128,2048]{1,0:T(8,128)(2,1)} %copy-done.27, bf16[128,2048]{1,0:T(8,128)(2,1)} %copy-done.26, bf16[128,2048]{1,0:T(8,128)(2,1)} %copy-done.29, ...), custom_call_target="tpu_custom_call" | custom-call | flops 12884901888 | tf_op jit(solution)/shard_map/pallas_call | solution.py:653
  405.1 4.1 fusion.3
  411.0 9.6 %shard_map.223 = (f32[256,2048]{1,0:T(8,128)}, bf16[256,2048]{1,0:T(8,128)(2,1)}, f32[1,2048]{1,0:T(1,128)}, bf16[256,512]{1,0:T(8,128)(2,1)}, bf16[256,512]{1,0...) custom-call(bf16[256,2048]{1,0:T(8,128)(2,1)} %get-tuple-element.268.refs_0_, ...), custom_call_target="tpu_custom_call" | custom-call | flops 2147483648 | tf_op jit(solution)/shard_map/pallas_call | solution.py:607
  421.4 1.3 collective-permute-start.39
  424.9 17.2 %collective-permute-done.39.refs_1_ = bf16[256,512]{1,0:T(8,128)(2,1)S(1)} collective-permute-done((bf16[256,512]{1,0:T(8,128)(2,1)}, bf16[256,512]{1,0:T(8,128)(2,1)S(1)}, u32[]{:S(2)}, u32[]{:S(2)}) %collective-permute-start.39) | collective-permute-done | bytes 262176 | tf_op jit(solution)/shard_map/ppermute | solution.py:772
  442.0 4.2 collective-permute-done.41.refs_3_
  447.3 1.6 collective-permute-start.47
  449.4 1.4 collective-permute-start.45
  450.8 26.6 %shard_map.224.d_ref.refs_7_ = bf16[1024,768]{1,0:T(8,128)(2,1)} custom-call(s32[1]{0:T(128)} %bitcast.1.place_ref.me_ref, bf16[1024,512]{1,0:T(8,128)(2,1)} %get-tuple-element.189.q_ref, f32[8,1024]{1,0:T(8,128)} %get-tuple-element.285.l_ref, bf16[2,2,1024,128]{3,2,1,0:T(8,128)(2,1)} %get-tuple-element.190.k_ref, ...), custom_call_target="tpu_custom_call" | custom-call | flops 10737418240 | tf_op jit(solution)/shard_map/pallas_call | solution.py:369
  477.4 8.2 %shard_map.225 = (bf16[256,2048]{1,0:T(8,128)(2,1)}, bf16[256,2048]{1,0:T(8,128)(2,1)}, bf16[256,2048]{1,0:T(8,128)(2,1)}, bf16[256,2048]{1,0:T(8,128)(2,1)}) custom-call(bf16[1024,768]{1,0:T(8,128)(2,1)} %shard_map.224.d_ref.refs_7_, bf16[1024,1280]{1,0:T(8,128)(2,1)} %all-gather.4.cloned.1.call-done.refs_5_.refs_7_.wo_ref.qo_ref.kvo_ref.refs_11_.refs_12_, ...), custom_call_target="tpu_custom_call" | custom-call | flops 3221225472 | tf_op jit(solution)/shard_map/pallas_call | solution.py:759
  485.7 8.7 %collective-permute-done.46.refs_2_.refs_4_ = bf16[256,2048]{1,0:T(8,128)(2,1)S(1)} collective-permute-done((bf16[256,2048]{1,0:T(8,128)(2,1)}, bf16[256,2048]{1,0:T(8,128)(2,1)S(1)}, u32[]{:S(2)}, u32[]{:S(2)}) %collective-permute-start.46) | collective-permute-done | bytes 1048608 | tf_op jit(solution)/shard_map/ppermute | solution.py:772
  495.4 3.1 shard_map.227
  504.6 9.8 %collective-permute-done.49.bottom_ref = bf16[128,2048]{1,0:T(8,128)(2,1)} collective-permute-done((bf16[128,2048]{1,0:T(8,128)(2,1)}, bf16[128,2048]{1,0:T(8,128)(2,1)}, u32[]{:S(2)}, u32[]{:S(2)}) %collective-permute-start.49) | collective-permute-done | bytes 524320 | tf_op jit(solution)/shard_map/ppermute | solution.py:772
  515.2 3.3 shard_map.226
  519.7 11.7 %shard_map.228 = (bf16[4,256,1280]{2,1,0:T(8,128)(2,1)}, f32[4,256,128]{2,1,0:T(8,128)}) custom-call(bf16[1024,2048]{1,0:T(8,128)(2,1)} %get-tuple-element.209.refs_0_, bf16[1024,1024]{1,0:T(8,128)(2,1)} %copy-done.9, bf16[256,2048]{1,0:T(8,128)(2,1)} %get-tuple-element.303.refs_0_.refs_2_, bf16[256,2048]{1,0:T(8,128)(2,1)} %collective-permute-done.45.refs_1_.refs_3_, ...), custom_call_target="tpu_custom_call" | custom-call | flops 5368709120 | tf_op jit(solution)/shard_map/pallas_call | solution.py:699
  544.2 2.0 collective-permute-start.55
  546.2 2.5 collective-permute-start.56
  550.1 5.0 shard_map.229
  557.2 1.5 collective-permute-start.57
  558.7 5.0 shard_map.230
  563.8 1.5 collective-permute-start.60
  567.3 14.4 %collective-permute-done.60 = f32[64,2]{0,1:T(2,128)S(1)} collective-permute-done((f32[64,2]{0,1:T(2,128)S(1)}, f32[64,2]{0,1:T(2,128)S(1)}, u32[]{:S(2)}, u32[]{:S(2)}) %collective-permute-start.60) | collective-permute-done | bytes 544 | tf_op jit(solution)/shard_map/ppermute | solution.py:772
  582.1 4.0 shard_map.231
  586.6 2.2 shard_map.232
  (252 shorter events, 66.7 us)
Async XLA Ops:
  7.2 65.2 %all-gather.4.cloned.1.call-start = ((), (), s32[]{:S(2)}) async-start(), calls=%async_computation.3 | async-start | bytes 3276800 | tf_op jit(solution)/shard_map/all_gather | solution.py:853
  11.7 30.3 %collective-permute-start.2 = (bf16[256,2048]{1,0:T(8,128)(2,1)S(1)}, bf16[256,2048]{1,0:T(8,128)(2,1)}, u32[]{:S(2)}, u32[]{:S(2)}) collective-permute-start(bf16[256,2048]{1,0:T(8,128)(2,1)S(1)} %select_dynamic-update-slice_fusion.8.refs_0_.refs_3_), channel_id=1, source_target_pairs={{0,3},{1,2},{2,1},{3,0},{4,7},{5,6},{6,5},{7,4},{8,11},{9,10},{10,... | collective-permute-start | bytes 3145736 | tf_op jit(solution)/shard_map/ppermute | solution.py:772
  15.7 45.7 %collective-permute-start.1 = (bf16[256,2048]{1,0:T(8,128)(2,1)S(1)}, bf16[256,2048]{1,0:T(8,128)(2,1)}, u32[]{:S(2)}, u32[]{:S(2)}) collective-permute-start(bf16[256,2048]{1,0:T(8,128)(2,1)S(1)} %select_dynamic-update-slice_fusion.8.refs_0_.refs_3_), channel_id=1, source_target_pairs={{0,2},{1,3},{2,0},{3,1},{4,6},{5,7},{6,4},{7,5},{8,10},{9,11},{10,... | collective-permute-start | bytes 3145736 | tf_op jit(solution)/shard_map/ppermute | solution.py:772
  16.2 45.5 %collective-permute-start = (bf16[256,2048]{1,0:T(8,128)(2,1)S(1)}, bf16[256,2048]{1,0:T(8,128)(2,1)}, u32[]{:S(2)}, u32[]{:S(2)}) collective-permute-start(bf16[256,2048]{1,0:T(8,128)(2,1)S(1)} %select_dynamic-update-slice_fusion.8.refs_0_.refs_3_), channel_id=1, source_target_pairs={{0,1},{1,0},{2,3},{3,2},{4,5},{5,4},{6,7},{7,6},{8,9},{9,8},{10,11... | collective-permute-start | bytes 3145736 | tf_op jit(solution)/shard_map/ppermute | solution.py:772
  16.4 175.4 %all-gather.6.cloned.1.call-start = ((), (), s32[]{:S(2)}) async-start(), calls=%async_computation.4 | async-start | bytes 7864320 | tf_op jit(solution)/shard_map/all_gather | solution.py:853
  72.4 232.3 %all-gather.8.cloned.1.call-start = ((), (), s32[]{:S(2)}) async-start(), calls=%async_computation.5 | async-start | bytes 7864320 | tf_op jit(solution)/shard_map/all_gather | solution.py:853
  72.6 37.8 %collective-permute-start.6 = (bf16[256,2048]{1,0:T(8,128)(2,1)}, bf16[256,2048]{1,0:T(8,128)(2,1)}, u32[]{:S(2)}, u32[]{:S(2)}) collective-permute-start(bf16[256,2048]{1,0:T(8,128)(2,1)} %select_dynamic-update-slice_fusion.refs_0_.refs_7_.refs_4_), channel_id=1, source_target_pairs={{0,3},{1,2},{2,1},{3,0},{4,7},{5,6},{6,5},{7,4},{8,11},{9,10},{10,... | collective-permute-start | bytes 3145736 | tf_op jit(solution)/shard_map/ppermute | solution.py:772
  75.0 46.8 %collective-permute-start.5 = (bf16[256,2048]{1,0:T(8,128)(2,1)}, bf16[256,2048]{1,0:T(8,128)(2,1)}, u32[]{:S(2)}, u32[]{:S(2)}) collective-permute-start(bf16[256,2048]{1,0:T(8,128)(2,1)} %select_dynamic-update-slice_fusion.refs_0_.refs_7_.refs_4_), channel_id=1, source_target_pairs={{0,2},{1,3},{2,0},{3,1},{4,6},{5,7},{6,4},{7,5},{8,10},{9,11},{10,... | collective-permute-start | bytes 3145736 | tf_op jit(solution)/shard_map/ppermute | solution.py:772
  75.6 46.3 %collective-permute-start.4 = (bf16[256,2048]{1,0:T(8,128)(2,1)}, bf16[256,2048]{1,0:T(8,128)(2,1)}, u32[]{:S(2)}, u32[]{:S(2)}) collective-permute-start(bf16[256,2048]{1,0:T(8,128)(2,1)} %select_dynamic-update-slice_fusion.refs_0_.refs_7_.refs_4_), channel_id=1, source_target_pairs={{0,1},{1,0},{2,3},{3,2},{4,5},{5,4},{6,7},{7,6},{8,9},{9,8},{10,11... | collective-permute-start | bytes 3145736 | tf_op jit(solution)/shard_map/ppermute | solution.py:772
  126.6 45.6 %collective-permute-start.11 = (bf16[1024,1024]{1,0:T(8,128)(2,1)}, bf16[1024,1024]{1,0:T(8,128)(2,1)}, u32[]{:S(2)}, u32[]{:S(2)}) collective-permute-start(bf16[1024,1024]{1,0:T(8,128)(2,1)} %shard_map.215), channel_id=1, source_target_pairs={{0,4},{4,0},{8,12},{12,8},{16,20},{20,16},{24,28},{28,24},{1,5},{5... | collective-permute-start | bytes 6291464 | tf_op jit(solution)/shard_map/ppermute | solution.py:830
  126.6 45.6 %collective-permute-start.12 = (bf16[1024,1024]{1,0:T(8,128)(2,1)S(1)}, bf16[1024,1024]{1,0:T(8,128)(2,1)S(1)}, u32[]{:S(2)}, u32[]{:S(2)}) collective-permute-start(bf16[1024,1024]{1,0:T(8,128)(2,1)S(1)} %copy-done.10), channel_id=1, source_target_pairs={{0,4},{4,0},{8,12},{12,8},{16,20},{20,16},{24,28},{28,24},{1,5},{5... | collective-permute-start | bytes 6291464 | tf_op jit(solution)/shard_map/ppermute | solution.py:830
  128.4 14.0 %collective-permute-start.8 = (bf16[128,2048]{1,0:T(8,128)(2,1)S(1)}, bf16[128,2048]{1,0:T(8,128)(2,1)S(1)}, u32[]{:S(2)}, u32[]{:S(2)}) collective-permute-start(bf16[128,2048]{1,0:T(8,128)(2,1)S(1)} %get-tuple-element.355), channel_id=1, source_target_pairs={{0,2},{1,3},{2,0},{3,1},{4,6},{5,7},{6,4},{7,5},{8,10},{9,11},{10,... | collective-permute-start | bytes 1572872 | tf_op jit(solution)/shard_map/ppermute | solution.py:772
  129.9 13.7 %collective-permute-start.7 = (bf16[128,2048]{1,0:T(8,128)(2,1)S(1)}, bf16[128,2048]{1,0:T(8,128)(2,1)}, u32[]{:S(2)}, u32[]{:S(2)}) collective-permute-start(bf16[128,2048]{1,0:T(8,128)(2,1)S(1)} %get-tuple-element.356), channel_id=1, source_target_pairs={{0,1},{1,0},{2,3},{3,2},{4,5},{5,4},{6,7},{7,6},{8,9},{9,8},{10,11... | collective-permute-start | bytes 1572872 | tf_op jit(solution)/shard_map/ppermute | solution.py:772
  130.7 18.2 %collective-permute-start.13 = (bf16[1024,512]{1,0:T(8,128)(2,1)S(1)}, bf16[1024,512]{1,0:T(8,128)(2,1)}, u32[]{:S(2)}, u32[]{:S(2)}) collective-permute-start(bf16[1024,512]{1,0:T(8,128)(2,1)S(1)} %copy-done.12), channel_id=1, source_target_pairs={{0,4},{4,0},{8,12},{12,8},{16,20},{20,16},{24,28},{28,24},{1,5},{5... | collective-permute-start | bytes 3145736 | tf_op jit(solution)/shard_map/ppermute | solution.py:830
  146.9 24.2 %collective-permute-start.9 = (bf16[256,2048]{1,0:T(8,128)(2,1)}, bf16[256,2048]{1,0:T(8,128)(2,1)S(1)}, u32[]{:S(2)}, u32[]{:S(2)}) collective-permute-start(bf16[256,2048]{1,0:T(8,128)(2,1)} %get-tuple-element.203), channel_id=1, source_target_pairs={{0,1},{1,0},{2,3},{3,2},{4,5},{5,4},{6,7},{7,6},{8,9},{9,8},{10,11... | collective-permute-start | bytes 3145736 | tf_op jit(solution)/shard_map/ppermute | solution.py:772
  147.9 24.3 %collective-permute-start.10 = (bf16[256,2048]{1,0:T(8,128)(2,1)}, bf16[256,2048]{1,0:T(8,128)(2,1)S(1)}, u32[]{:S(2)}, u32[]{:S(2)}) collective-permute-start(bf16[256,2048]{1,0:T(8,128)(2,1)} %get-tuple-element.204), channel_id=1, source_target_pairs={{0,2},{1,3},{2,0},{3,1},{4,6},{5,7},{6,4},{7,5},{8,10},{9,11},{10,... | collective-permute-start | bytes 3145736 | tf_op jit(solution)/shard_map/ppermute | solution.py:772
  179.0 12.1 %collective-permute-start.15 = (bf16[128,2048]{1,0:T(8,128)(2,1)S(1)}, bf16[128,2048]{1,0:T(8,128)(2,1)S(1)}, u32[]{:S(2)}, u32[]{:S(2)}) collective-permute-start(bf16[128,2048]{1,0:T(8,128)(2,1)S(1)} %get-tuple-element.216), channel_id=1, source_target_pairs={{0,2},{1,3},{2,0},{3,1},{4,6},{5,7},{6,4},{7,5},{8,10},{9,11},{10,... | collective-permute-start | bytes 1572872 | tf_op jit(solution)/shard_map/ppermute | solution.py:772
  179.9 11.9 %collective-permute-start.14 = (bf16[128,2048]{1,0:T(8,128)(2,1)S(1)}, bf16[128,2048]{1,0:T(8,128)(2,1)S(1)}, u32[]{:S(2)}, u32[]{:S(2)}) collective-permute-start(bf16[128,2048]{1,0:T(8,128)(2,1)S(1)} %get-tuple-element.219), channel_id=1, source_target_pairs={{0,1},{1,0},{2,3},{3,2},{4,5},{5,4},{6,7},{7,6},{8,9},{9,8},{10,11... | collective-permute-start | bytes 1572872 | tf_op jit(solution)/shard_map/ppermute | solution.py:772
  191.7 26.6 %collective-permute-start.20 = (bf16[1024,3072]{1,0:T(8,128)(2,1)}, bf16[1024,3072]{1,0:T(8,128)(2,1)}, u32[]{:S(2)}, u32[]{:S(2)}) collective-permute-start(bf16[1024,3072]{1,0:T(8,128)(2,1)} %all-gather.6.cloned.1.call-done.refs_11_.refs_12_.refs_13_), channel_id=1, source_target_pairs={{0,4},{4,0},{8,12},{12,8},{16,20},{20,16},{24,28},{28,24},{1,5},{5... | collective-permute-start | bytes 18874376 | tf_op jit(solution)/shard_map/ppermute | solution.py:830
  191.8 285.7 %reduce-scatter.4.cloned.1.call-start = ((), (), s32[]{:S(2)}) async-start(), calls=%async_computation.6 | async-start | bytes 7864320 | tf_op jit(solution)/shard_map/reduce_scatter | solution.py:857
  191.8 14.8 %collective-permute-start.16 = (bf16[128,2048]{1,0:T(8,128)(2,1)S(1)}, bf16[128,2048]{1,0:T(8,128)(2,1)S(1)}, u32[]{:S(2)}, u32[]{:S(2)}) collective-permute-start(bf16[128,2048]{1,0:T(8,128)(2,1)S(1)} %get-tuple-element.216), channel_id=1, source_target_pairs={{0,1},{1,0},{2,3},{3,2},{4,5},{5,4},{6,7},{7,6},{8,9},{9,8},{10,11... | collective-permute-start | bytes 1572872 | tf_op jit(solution)/shard_map/ppermute | solution.py:772
  193.0 14.8 %collective-permute-start.17 = (bf16[128,2048]{1,0:T(8,128)(2,1)S(1)}, bf16[128,2048]{1,0:T(8,128)(2,1)S(1)}, u32[]{:S(2)}, u32[]{:S(2)}) collective-permute-start(bf16[128,2048]{1,0:T(8,128)(2,1)S(1)} %get-tuple-element.219), channel_id=1, source_target_pairs={{0,2},{1,3},{2,0},{3,1},{4,6},{5,7},{6,4},{7,5},{8,10},{9,11},{10,... | collective-permute-start | bytes 1572872 | tf_op jit(solution)/shard_map/ppermute | solution.py:772
  193.9 24.3 %collective-permute-start.19 = (bf16[128,2048]{1,0:T(8,128)(2,1)S(1)}, bf16[128,2048]{1,0:T(8,128)(2,1)S(1)}, u32[]{:S(2)}, u32[]{:S(2)}) collective-permute-start(bf16[128,2048]{1,0:T(8,128)(2,1)S(1)} %collective-permute-done.14.refs_2_), channel_id=1, source_target_pairs={{0,2},{1,3},{2,0},{3,1},{4,6},{5,7},{6,4},{7,5},{8,10},{9,11},{10,... | collective-permute-start | bytes 1572872 | tf_op jit(solution)/shard_map/ppermute | solution.py:772
  195.0 23.3 %collective-permute-start.18 = (bf16[128,2048]{1,0:T(8,128)(2,1)S(1)}, bf16[128,2048]{1,0:T(8,128)(2,1)S(1)}, u32[]{:S(2)}, u32[]{:S(2)}) collective-permute-start(bf16[128,2048]{1,0:T(8,128)(2,1)S(1)} %collective-permute-done.15.refs_3_), channel_id=1, source_target_pairs={{0,1},{1,0},{2,3},{3,2},{4,5},{5,4},{6,7},{7,6},{8,9},{9,8},{10,11... | collective-permute-start | bytes 1572872 | tf_op jit(solution)/shard_map/ppermute | solution.py:772
  222.3 37.2 %collective-permute-start.21 = (bf16[1024,1024]{1,0:T(8,128)(2,1)}, bf16[1024,1024]{1,0:T(8,128)(2,1)S(1)}, u32[]{:S(2)}, u32[]{:S(2)}) collective-permute-start(bf16[1024,1024]{1,0:T(8,128)(2,1)} %shard_map.218), channel_id=1, source_target_pairs={{0,4},{4,0},{8,12},{12,8},{16,20},{20,16},{24,28},{28,24},{1,5},{5... | collective-permute-start | bytes 6291464 | tf_op jit(solution)/shard_map/ppermute | solution.py:830
  259.5 6.8 %collective-permute-start.22 = (bf16[1024,1024]{1,0:T(8,128)(2,1)}, bf16[1024,1024]{1,0:T(8,128)(2,1)S(1)}, u32[]{:S(2)}, u32[]{:S(2)}) collective-permute-start(bf16[1024,1024]{1,0:T(8,128)(2,1)} %get-tuple-element.235.refs_13_), channel_id=1, source_target_pairs={{0,4},{4,0},{8,12},{12,8},{16,20},{20,16},{24,28},{28,24},{1,5},{5... | collective-permute-start | bytes 6291464 | tf_op jit(solution)/shard_map/ppermute | solution.py:830
  260.1 7.1 %collective-permute-start.23 = (bf16[1024,1024]{1,0:T(8,128)(2,1)}, bf16[1024,1024]{1,0:T(8,128)(2,1)}, u32[]{:S(2)}, u32[]{:S(2)}) collective-permute-start(bf16[1024,1024]{1,0:T(8,128)(2,1)} %get-tuple-element.236.refs_14_), channel_id=1, source_target_pairs={{0,4},{4,0},{8,12},{12,8},{16,20},{20,16},{24,28},{28,24},{1,5},{5... | collective-permute-start | bytes 6291464 | tf_op jit(solution)/shard_map/ppermute | solution.py:830
  260.2 10.0 %collective-permute-start.24 = (bf16[1024,1024]{1,0:T(8,128)(2,1)}, bf16[1024,1024]{1,0:T(8,128)(2,1)}, u32[]{:S(2)}, u32[]{:S(2)}) collective-permute-start(bf16[1024,1024]{1,0:T(8,128)(2,1)} %get-tuple-element.237.refs_15_), channel_id=1, source_target_pairs={{0,4},{4,0},{8,12},{12,8},{16,20},{20,16},{24,28},{28,24},{1,5},{5... | collective-permute-start | bytes 6291464 | tf_op jit(solution)/shard_map/ppermute | solution.py:830
  304.8 226.7 %reduce-scatter.6.cloned.1.call-start = ((), (), s32[]{:S(2)}) async-start(), calls=%async_computation.7 | async-start | bytes 7864320 | tf_op jit(solution)/shard_map/reduce_scatter | solution.py:857
  304.8 10.6 %collective-permute-start.25 = (bf16[1024,3072]{1,0:T(8,128)(2,1)}, bf16[1024,3072]{1,0:T(8,128)(2,1)}, u32[]{:S(2)}, u32[]{:S(2)}) collective-permute-start(bf16[1024,3072]{1,0:T(8,128)(2,1)} %all-gather.8.cloned.1.call-done.refs_11_.refs_12_.refs_13_), channel_id=1, source_target_pairs={{0,4},{4,0},{8,12},{12,8},{16,20},{20,16},{24,28},{28,24},{1,5},{5... | collective-permute-start | bytes 18874376 | tf_op jit(solution)/shard_map/ppermute | solution.py:830
  304.9 51.2 %collective-permute-start.28 = (bf16[1024,512]{1,0:T(8,128)(2,1)S(1)}, bf16[1024,512]{1,0:T(8,128)(2,1)S(1)}, u32[]{:S(2)}, u32[]{:S(2)}) collective-permute-start(bf16[1024,512]{1,0:T(8,128)(2,1)S(1)} %slice.196.refs_6_), channel_id=1, source_target_pairs={{0,3},{1,2},{2,1},{3,0},{4,7},{5,6},{6,5},{7,4},{8,11},{9,10},{10,... | collective-permute-start | bytes 3145736 | tf_op jit(solution)/shard_map/ppermute | solution.py:772
  307.3 48.8 %collective-permute-start.27 = (bf16[1024,512]{1,0:T(8,128)(2,1)S(1)}, bf16[1024,512]{1,0:T(8,128)(2,1)S(1)}, u32[]{:S(2)}, u32[]{:S(2)}) collective-permute-start(bf16[1024,512]{1,0:T(8,128)(2,1)S(1)} %slice.196.refs_6_), channel_id=1, source_target_pairs={{0,2},{1,3},{2,0},{3,1},{4,6},{5,7},{6,4},{7,5},{8,10},{9,11},{10,... | collective-permute-start | bytes 3145736 | tf_op jit(solution)/shard_map/ppermute | solution.py:772
  307.9 48.3 %collective-permute-start.26 = (bf16[1024,512]{1,0:T(8,128)(2,1)S(1)}, bf16[1024,512]{1,0:T(8,128)(2,1)}, u32[]{:S(2)}, u32[]{:S(2)}) collective-permute-start(bf16[1024,512]{1,0:T(8,128)(2,1)S(1)} %slice.196.refs_6_), channel_id=1, source_target_pairs={{0,1},{1,0},{2,3},{3,2},{4,5},{5,4},{6,7},{7,6},{8,9},{9,8},{10,11... | collective-permute-start | bytes 3145736 | tf_op jit(solution)/shard_map/ppermute | solution.py:772
  356.2 21.7 %collective-permute-start.31 = (bf16[1024,1024]{1,0:T(8,128)(2,1)}, bf16[1024,1024]{1,0:T(8,128)(2,1)}, u32[]{:S(2)}, u32[]{:S(2)}) collective-permute-start(bf16[1024,1024]{1,0:T(8,128)(2,1)} %get-tuple-element.258.refs_13_), channel_id=1, source_target_pairs={{0,4},{4,0},{8,12},{12,8},{16,20},{20,16},{24,28},{28,24},{1,5},{5... | collective-permute-start | bytes 6291464 | tf_op jit(solution)/shard_map/ppermute | solution.py:830
  356.4 21.6 %collective-permute-start.32 = (bf16[1024,1024]{1,0:T(8,128)(2,1)}, bf16[1024,1024]{1,0:T(8,128)(2,1)}, u32[]{:S(2)}, u32[]{:S(2)}) collective-permute-start(bf16[1024,1024]{1,0:T(8,128)(2,1)} %get-tuple-element.259.refs_14_), channel_id=1, source_target_pairs={{0,4},{4,0},{8,12},{12,8},{16,20},{20,16},{24,28},{28,24},{1,5},{5... | collective-permute-start | bytes 6291464 | tf_op jit(solution)/shard_map/ppermute | solution.py:830
  356.8 22.7 %collective-permute-start.33 = (bf16[1024,1024]{1,0:T(8,128)(2,1)}, bf16[1024,1024]{1,0:T(8,128)(2,1)}, u32[]{:S(2)}, u32[]{:S(2)}) collective-permute-start(bf16[1024,1024]{1,0:T(8,128)(2,1)} %get-tuple-element.260.refs_15_), channel_id=1, source_target_pairs={{0,4},{4,0},{8,12},{12,8},{16,20},{20,16},{24,28},{28,24},{1,5},{5... | collective-permute-start | bytes 6291464 | tf_op jit(solution)/shard_map/ppermute | solution.py:830
  358.2 14.3 %collective-permute-start.30 = (bf16[128,2048]{1,0:T(8,128)(2,1)S(1)}, bf16[128,2048]{1,0:T(8,128)(2,1)S(1)}, u32[]{:S(2)}, u32[]{:S(2)}) collective-permute-start(bf16[128,2048]{1,0:T(8,128)(2,1)S(1)} %get-tuple-element.351), channel_id=1, source_target_pairs={{0,2},{1,3},{2,0},{3,1},{4,6},{5,7},{6,4},{7,5},{8,10},{9,11},{10,... | collective-permute-start | bytes 1572872 | tf_op jit(solution)/shard_map/ppermute | solution.py:772
  359.7 14.0 %collective-permute-start.29 = (bf16[128,2048]{1,0:T(8,128)(2,1)S(1)}, bf16[128,2048]{1,0:T(8,128)(2,1)S(1)}, u32[]{:S(2)}, u32[]{:S(2)}) collective-permute-start(bf16[128,2048]{1,0:T(8,128)(2,1)S(1)} %get-tuple-element.352), channel_id=1, source_target_pairs={{0,1},{1,0},{2,3},{3,2},{4,5},{5,4},{6,7},{7,6},{8,9},{9,8},{10,11... | collective-permute-start | bytes 1572872 | tf_op jit(solution)/shard_map/ppermute | solution.py:772
  372.5 31.4 %collective-permute-start.36 = (bf16[1024,512]{1,0:T(8,128)(2,1)}, bf16[1024,512]{1,0:T(8,128)(2,1)S(1)}, u32[]{:S(2)}, u32[]{:S(2)}) collective-permute-start(bf16[1024,512]{1,0:T(8,128)(2,1)} %collective-permute-done.26.refs_7_), channel_id=1, source_target_pairs={{0,4},{4,0},{8,12},{12,8},{16,20},{20,16},{24,28},{28,24},{1,5},{5... | collective-permute-start | bytes 3145736 | tf_op jit(solution)/shard_map/ppermute | solution.py:830
  373.7 30.2 %collective-permute-start.37 = (bf16[1024,512]{1,0:T(8,128)(2,1)S(1)}, bf16[1024,512]{1,0:T(8,128)(2,1)}, u32[]{:S(2)}, u32[]{:S(2)}) collective-permute-start(bf16[1024,512]{1,0:T(8,128)(2,1)S(1)} %collective-permute-done.27.refs_8_), channel_id=1, source_target_pairs={{0,4},{4,0},{8,12},{12,8},{16,20},{20,16},{24,28},{28,24},{1,5},{5... | collective-permute-start | bytes 3145736 | tf_op jit(solution)/shard_map/ppermute | solution.py:830
  377.9 26.1 %collective-permute-start.38 = (bf16[1024,512]{1,0:T(8,128)(2,1)S(1)}, bf16[1024,512]{1,0:T(8,128)(2,1)}, u32[]{:S(2)}, u32[]{:S(2)}) collective-permute-start(bf16[1024,512]{1,0:T(8,128)(2,1)S(1)} %collective-permute-done.28.refs_9_), channel_id=1, source_target_pairs={{0,4},{4,0},{8,12},{12,8},{16,20},{20,16},{24,28},{28,24},{1,5},{5... | collective-permute-start | bytes 3145736 | tf_op jit(solution)/shard_map/ppermute | solution.py:830
  378.0 26.0 %collective-permute-start.34 = (bf16[256,2048]{1,0:T(8,128)(2,1)}, bf16[256,2048]{1,0:T(8,128)(2,1)}, u32[]{:S(2)}, u32[]{:S(2)}) collective-permute-start(bf16[256,2048]{1,0:T(8,128)(2,1)} %get-tuple-element.262), channel_id=1, source_target_pairs={{0,1},{1,0},{2,3},{3,2},{4,5},{5,4},{6,7},{7,6},{8,9},{9,8},{10,11... | collective-permute-start | bytes 3145736 | tf_op jit(solution)/shard_map/ppermute | solution.py:772
  379.5 25.5 %collective-permute-start.35 = (bf16[256,2048]{1,0:T(8,128)(2,1)}, bf16[256,2048]{1,0:T(8,128)(2,1)}, u32[]{:S(2)}, u32[]{:S(2)}) collective-permute-start(bf16[256,2048]{1,0:T(8,128)(2,1)} %get-tuple-element.263), channel_id=1, source_target_pairs={{0,2},{1,3},{2,0},{3,1},{4,6},{5,7},{6,4},{7,5},{8,10},{9,11},{10,... | collective-permute-start | bytes 3145736 | tf_op jit(solution)/shard_map/ppermute | solution.py:772
  405.0 181.5 %reduce-scatter.8.cloned.1.call-start = ((), (), s32[]{:S(2)}) async-start(), calls=%async_computation.8 | async-start | bytes 3276800 | tf_op jit(solution)/shard_map/reduce_scatter | solution.py:857
  409.2 37.1 %collective-permute-start.44 = (bf16[256,2048]{1,0:T(8,128)(2,1)S(1)}, bf16[256,2048]{1,0:T(8,128)(2,1)S(1)}, u32[]{:S(2)}, u32[]{:S(2)}) collective-permute-start(bf16[256,2048]{1,0:T(8,128)(2,1)S(1)} %get-tuple-element.346), channel_id=1, source_target_pairs={{0,2},{1,3},{2,0},{3,1},{4,6},{5,7},{6,4},{7,5},{8,10},{9,11},{10,... | collective-permute-start | bytes 3145736 | tf_op jit(solution)/shard_map/ppermute | solution.py:772
  410.3 35.9 %collective-permute-start.43 = (bf16[256,2048]{1,0:T(8,128)(2,1)S(1)}, bf16[256,2048]{1,0:T(8,128)(2,1)S(1)}, u32[]{:S(2)}, u32[]{:S(2)}) collective-permute-start(bf16[256,2048]{1,0:T(8,128)(2,1)S(1)} %get-tuple-element.347), channel_id=1, source_target_pairs={{0,1},{1,0},{2,3},{3,2},{4,5},{5,4},{6,7},{7,6},{8,9},{9,8},{10,11... | collective-permute-start | bytes 3145736 | tf_op jit(solution)/shard_map/ppermute | solution.py:772
  421.4 20.7 %collective-permute-start.39 = (bf16[256,512]{1,0:T(8,128)(2,1)}, bf16[256,512]{1,0:T(8,128)(2,1)S(1)}, u32[]{:S(2)}, u32[]{:S(2)}) collective-permute-start(bf16[256,512]{1,0:T(8,128)(2,1)} %get-tuple-element.278), channel_id=1, source_target_pairs={{0,1},{1,0},{2,3},{3,2},{4,5},{5,4},{6,7},{7,6},{8,9},{9,8},{10,11... | collective-permute-start | bytes 786440 | tf_op jit(solution)/shard_map/ppermute | solution.py:772
  422.7 19.3 %collective-permute-start.40 = (bf16[256,512]{1,0:T(8,128)(2,1)}, bf16[256,512]{1,0:T(8,128)(2,1)S(1)}, u32[]{:S(2)}, u32[]{:S(2)}) collective-permute-start(bf16[256,512]{1,0:T(8,128)(2,1)} %get-tuple-element.279), channel_id=1, source_target_pairs={{0,2},{1,3},{2,0},{3,1},{4,6},{5,7},{6,4},{7,5},{8,10},{9,11},{10,... | collective-permute-start | bytes 786440 | tf_op jit(solution)/shard_map/ppermute | solution.py:772
  423.6 22.6 %collective-permute-start.41 = (bf16[256,512]{1,0:T(8,128)(2,1)}, bf16[256,512]{1,0:T(8,128)(2,1)S(1)}, u32[]{:S(2)}, u32[]{:S(2)}) collective-permute-start(bf16[256,512]{1,0:T(8,128)(2,1)} %get-tuple-element.280), channel_id=1, source_target_pairs={{0,3},{1,2},{2,1},{3,0},{4,7},{5,6},{6,5},{7,4},{8,11},{9,10},{10,... | collective-permute-start | bytes 786440 | tf_op jit(solution)/shard_map/ppermute | solution.py:772
  447.3 38.4 %collective-permute-start.47 = (bf16[256,2048]{1,0:T(8,128)(2,1)}, bf16[256,2048]{1,0:T(8,128)(2,1)S(1)}, u32[]{:S(2)}, u32[]{:S(2)}) collective-permute-start(bf16[256,2048]{1,0:T(8,128)(2,1)} %get-tuple-element.303.refs_0_.refs_2_), channel_id=1, source_target_pairs={{0,3},{1,2},{2,1},{3,0},{4,7},{5,6},{6,5},{7,4},{8,11},{9,10},{10,... | collective-permute-start | bytes 3145736 | tf_op jit(solution)/shard_map/ppermute | solution.py:772
  448.8 45.6 %collective-permute-start.46 = (bf16[256,2048]{1,0:T(8,128)(2,1)}, bf16[256,2048]{1,0:T(8,128)(2,1)S(1)}, u32[]{:S(2)}, u32[]{:S(2)}) collective-permute-start(bf16[256,2048]{1,0:T(8,128)(2,1)} %get-tuple-element.303.refs_0_.refs_2_), channel_id=1, source_target_pairs={{0,2},{1,3},{2,0},{3,1},{4,6},{5,7},{6,4},{7,5},{8,10},{9,11},{10,... | collective-permute-start | bytes 3145736 | tf_op jit(solution)/shard_map/ppermute | solution.py:772
  449.4 45.5 %collective-permute-start.45 = (bf16[256,2048]{1,0:T(8,128)(2,1)}, bf16[256,2048]{1,0:T(8,128)(2,1)}, u32[]{:S(2)}, u32[]{:S(2)}) collective-permute-start(bf16[256,2048]{1,0:T(8,128)(2,1)} %get-tuple-element.303.refs_0_.refs_2_), channel_id=1, source_target_pairs={{0,1},{1,0},{2,3},{3,2},{4,5},{5,4},{6,7},{7,6},{8,9},{9,8},{10,11... | collective-permute-start | bytes 3145736 | tf_op jit(solution)/shard_map/ppermute | solution.py:772
  498.5 20.1 %collective-permute-start.50 = (bf16[1024,1024]{1,0:T(8,128)(2,1)}, bf16[1024,1024]{1,0:T(8,128)(2,1)}, u32[]{:S(2)}, u32[]{:S(2)}) collective-permute-start(bf16[1024,1024]{1,0:T(8,128)(2,1)} %shard_map.227), channel_id=1, source_target_pairs={{0,4},{4,0},{8,12},{12,8},{16,20},{20,16},{24,28},{28,24},{1,5},{5... | collective-permute-start | bytes 6291464 | tf_op jit(solution)/shard_map/ppermute | solution.py:830
  498.6 19.9 %collective-permute-start.51 = (bf16[1024,768]{1,0:T(8,128)(2,1)S(1)}, bf16[1024,768]{1,0:T(8,128)(2,1)S(1)}, u32[]{:S(2)}, u32[]{:S(2)}) collective-permute-start(bf16[1024,768]{1,0:T(8,128)(2,1)S(1)} %copy-done.3), channel_id=1, source_target_pairs={{0,4},{4,0},{8,12},{12,8},{16,20},{20,16},{24,28},{28,24},{1,5},{5... | collective-permute-start | bytes 4718600 | tf_op jit(solution)/shard_map/ppermute | solution.py:830
  500.1 14.3 %collective-permute-start.49 = (bf16[128,2048]{1,0:T(8,128)(2,1)}, bf16[128,2048]{1,0:T(8,128)(2,1)}, u32[]{:S(2)}, u32[]{:S(2)}) collective-permute-start(bf16[128,2048]{1,0:T(8,128)(2,1)} %get-tuple-element.349), channel_id=1, source_target_pairs={{0,2},{1,3},{2,0},{3,1},{4,6},{5,7},{6,4},{7,5},{8,10},{9,11},{10,... | collective-permute-start | bytes 1572872 | tf_op jit(solution)/shard_map/ppermute | solution.py:772
  501.3 13.9 %collective-permute-start.48 = (bf16[128,2048]{1,0:T(8,128)(2,1)}, bf16[128,2048]{1,0:T(8,128)(2,1)}, u32[]{:S(2)}, u32[]{:S(2)}) collective-permute-start(bf16[128,2048]{1,0:T(8,128)(2,1)} %get-tuple-element.350), channel_id=1, source_target_pairs={{0,1},{1,0},{2,3},{3,2},{4,5},{5,4},{6,7},{7,6},{8,9},{9,8},{10,11... | collective-permute-start | bytes 1572872 | tf_op jit(solution)/shard_map/ppermute | solution.py:772
  531.5 24.6 %collective-permute-start.52 = (bf16[256,2048]{1,0:T(8,128)(2,1)}, bf16[256,2048]{1,0:T(8,128)(2,1)S(1)}, u32[]{:S(2)}, u32[]{:S(2)}) collective-permute-start(bf16[256,2048]{1,0:T(8,128)(2,1)} %get-tuple-element.311), channel_id=1, source_target_pairs={{0,1},{1,0},{2,3},{3,2},{4,5},{5,4},{6,7},{7,6},{8,9},{9,8},{10,11... | collective-permute-start | bytes 3145736 | tf_op jit(solution)/shard_map/ppermute | solution.py:772
  532.7 24.5 %collective-permute-start.53 = (bf16[256,2048]{1,0:T(8,128)(2,1)}, bf16[256,2048]{1,0:T(8,128)(2,1)S(1)}, u32[]{:S(2)}, u32[]{:S(2)}) collective-permute-start(bf16[256,2048]{1,0:T(8,128)(2,1)} %get-tuple-element.312), channel_id=1, source_target_pairs={{0,2},{1,3},{2,0},{3,1},{4,6},{5,7},{6,4},{7,5},{8,10},{9,11},{10,... | collective-permute-start | bytes 3145736 | tf_op jit(solution)/shard_map/ppermute | solution.py:772
  544.1 5.5 collective-permute-start.54
  544.2 5.5 collective-permute-start.55
  557.2 24.8 %collective-permute-start.57 = (bf16[256,2048]{1,0:T(8,128)(2,1)S(1)}, bf16[256,2048]{1,0:T(8,128)(2,1)}, u32[]{:S(2)}, u32[]{:S(2)}) collective-permute-start(bf16[256,2048]{1,0:T(8,128)(2,1)S(1)} %copy-done.24), channel_id=1, source_target_pairs={{0,3},{1,2},{2,1},{3,0},{4,7},{5,6},{6,5},{7,4},{8,11},{9,10},{10,... | collective-permute-start | bytes 3145736 | tf_op jit(solution)/shard_map/ppermute | solution.py:772
  563.8 18.0 %collective-permute-start.60 = (f32[64,2]{0,1:T(2,128)S(1)}, f32[64,2]{0,1:T(2,128)S(1)}, u32[]{:S(2)}, u32[]{:S(2)}) collective-permute-start(f32[64,2]{0,1:T(2,128)S(1)} %bitcast.51), channel_id=1, source_target_pairs={{0,3},{1,2},{2,1},{3,0},{4,7},{5,6},{6,5},{7,4},{8,11},{9,10},{10,... | collective-permute-start | bytes 1544 | tf_op jit(solution)/shard_map/ppermute | solution.py:772
  565.3 16.8 %collective-permute-start.58 = (f32[64,2]{0,1:T(2,128)S(1)}, f32[64,2]{0,1:T(2,128)S(1)}, u32[]{:S(2)}, u32[]{:S(2)}) collective-permute-start(f32[64,2]{0,1:T(2,128)S(1)} %bitcast.50), channel_id=1, source_target_pairs={{0,1},{1,0},{2,3},{3,2},{4,5},{5,4},{6,7},{7,6},{8,9},{9,8},{10,11... | collective-permute-start | bytes 1544 | tf_op jit(solution)/shard_map/ppermute | solution.py:772
  566.3 15.8 %collective-permute-start.59 = (f32[64,2]{0,1:T(2,128)S(1)}, f32[64,2]{0,1:T(2,128)S(1)}, u32[]{:S(2)}, u32[]{:S(2)}) collective-permute-start(f32[64,2]{0,1:T(2,128)S(1)} %bitcast.49), channel_id=1, source_target_pairs={{0,2},{1,3},{2,0},{3,1},{4,6},{5,7},{6,4},{7,5},{8,10},{9,11},{10,... | collective-permute-start | bytes 1544 | tf_op jit(solution)/shard_map/ppermute | solution.py:772
  (48 other events, 449.0 us)
Sparse Core Ops, SparseCore 0:
  16.5 55.8 all-gather.3
  74.5 113.5 all-gather.5
  191.9 112.8 all-gather.7
  306.9 110.3 reduce-scatter.3
  419.5 111.2 reduce-scatter.5
  532.9 51.9 reduce-scatter.7

commit v2 on v0

--- a/solution.py
+++ b/solution.py
@@ -47,6 +47,19 @@
 
 def mm_tn(left, right):
     return lax.dot_general(left, right, (((0,), (0,)), ((), ())), preferred_element_type=jnp.float32)
+
+
+def partner_rows(size, rows):
+    return [rows] * 3 + [rows // 2] * 2 if size == 4 else [rows] * size
+
+
+def store_partner(refs, step, lanes, value):
+    if len(refs) == 5 and step == 3:
+        half = refs[3].shape[0]
+        refs[3][:, lanes] = value[:half]
+        refs[4][:, lanes] = value[half:]
+    else:
+        refs[step][:, lanes] = value
 
 
 def lane_index(rows):
@@ -162,7 +175,7 @@
 def attend_kernel(
     me_ref, q_ref, k_ref, v_ref, wo_ref, wx_ref, o_ref, l_ref, *refs, size, heads, group
 ):
-    part_refs, vt_ref = refs[:size], refs[size]
+    part_refs, vt_ref = refs[:-1], refs[-1]
     rows = q_ref.shape[0]
     half = wo_ref.shape[0]
     mine = jnp.bitwise_xor(me_ref[0], pl.program_id(0))
@@ -206,12 +219,14 @@
     for span in range(size):
         pl.when(mine == span)(functools.partial(one, span))
 
-    def project_out(ref):
-        ref[:, :half] = mm_nt(o_ref[...], wo_ref[...]).astype(jnp.bfloat16)
-        ref[:, half:] = mm_nt(o_ref[...], wx_ref[...]).astype(jnp.bfloat16)
+    def project_out(step):
+        for part, w_ref in enumerate((wo_ref, wx_ref)):
+            lanes = slice(part * half, (part + 1) * half)
+            product = mm_nt(o_ref[...], w_ref[...]).astype(jnp.bfloat16)
+            store_partner(part_refs, step, lanes, product)
 
     for step in range(size):
-        pl.when(pl.program_id(0) == step)(functools.partial(project_out, part_refs[step]))
+        pl.when(pl.program_id(0) == step)(functools.partial(project_out, step))
 
 
 def attend(me, query, key_pad, value_pad, own, other, columns, size, group):
@@ -228,7 +243,7 @@
             pl.BlockSpec((rows, width), lambda p, m: (p, 0)),
             pl.BlockSpec((heads, rows), lambda p, m: (0, p)),
         ]
-        + [pl.BlockSpec((rows, features), lambda p, m: (0, 0))] * size,
+        + [pl.BlockSpec((r, features), lambda p, m: (0, 0)) for r in partner_rows(size, rows)],
         scratch_shapes=[pltpu.VMEM((heads // group, 2, PAIR, total), jnp.bfloat16)],
     )
     return pl.pallas_call(
@@ -238,7 +253,7 @@
             jax.ShapeDtypeStruct((total, width), jnp.bfloat16),
             jax.ShapeDtypeStruct((heads, total), jnp.float32),
         ]
-        + [jax.ShapeDtypeStruct((rows, features), jnp.bfloat16)] * size,
+        + [jax.ShapeDtypeStruct((r, features), jnp.bfloat16) for r in partner_rows(size, rows)],
         compiler_params=PARAMS,
         cost_estimate=hint(8 * heads * total * total * HEAD_DIM // 16),
     )(me, query, key_pad, value_pad, own, other)
@@ -387,8 +402,9 @@
     e_refs = grouped(refs[sum(n_counts) :], e_counts)
     gate_o, up_o, down_o, gate_x, up_x, down_x = refs[pieces : pieces + 6]
     y_ref, n_ref, e_ref = refs[-3:]
-    dn_refs = refs[-3 - size if adds else -4 : -3]
-    dg_ref, du_ref, h_ref = refs[-6 - size if adds else -7 :][:3]
+    dn_count = len(partner_rows(size, n_ref.shape[0])) if adds else 1
+    dn_refs = refs[-3 - dn_count : -3]
+    dg_ref, du_ref, h_ref = refs[-6 - dn_count :][:3]
     half = gate_o.shape[0]
 
     def fetch(step):
@@ -422,14 +438,13 @@
         y_ref[:, lanes] = y.astype(jnp.bfloat16)
         dn = dn.astype(jnp.bfloat16)
 
-        def store(ref):
-            ref[:, lanes] = dn
-
         if adds:
             for step in range(size):
-                pl.when(pl.program_id(0) == step)(functools.partial(store, dn_refs[step]))
+                pl.when(pl.program_id(0) == step)(
+                    functools.partial(store_partner, dn_refs, step, lanes, dn)
+                )
         else:
-            store(dn_refs[0])
+            dn_refs[0][:, lanes] = dn
 
 
 def mlp(tokens, cot, own, other, earlier):
@@ -443,8 +458,9 @@
     sums = jax.ShapeDtypeStruct((total, features), jnp.bfloat16)
     dn_specs, dn_shapes = [wide], [sums]
     if earlier:
-        dn_specs = [pl.BlockSpec((rows, features), fixed)] * size
-        dn_shapes = [jax.ShapeDtypeStruct((rows, features), jnp.bfloat16)] * size
+        counts = partner_rows(size, rows)
+        dn_specs = [pl.BlockSpec((r, features), fixed) for r in counts]
+        dn_shapes = [jax.ShapeDtypeStruct((r, features), jnp.bfloat16) for r in counts]
     pieces = sum(tokens, []) + sum(cot, [])
     thirds = [
         pl.BlockSpec((half, units), lambda p, t=t: (0, t), pipeline_mode=ONCE) for t in range(3)
@@ -736,18 +752,18 @@
     )
 
 
-def input_grad_kernel(d_ref, qo_ref, qx_ref, kvo_ref, kvx_ref, *out_refs):
+def input_grad_kernel(d_ref, qo_ref, qx_ref, kvo_ref, kvx_ref, *out_refs, size):
     half, cut = qo_ref.shape
 
-    def one(ref):
+    def one(step):
         query, rest = d_ref[:, :cut], d_ref[:, cut:]
-        own = mm_nt(query, qo_ref[...]) + mm_nt(rest, kvo_ref[...])
-        other = mm_nt(query, qx_ref[...]) + mm_nt(rest, kvx_ref[...])
-        ref[:, :half] = own.astype(jnp.bfloat16)
-        ref[:, half:] = other.astype(jnp.bfloat16)
-
-    for step, ref in enumerate(out_refs):
-        pl.when(pl.program_id(0) == step)(functools.partial(one, ref))
+        for part, (q_ref, kv_ref) in enumerate(((qo_ref, kvo_ref), (qx_ref, kvx_ref))):
+            lanes = slice(part * half, (part + 1) * half)
+            product = mm_nt(query, q_ref[...]) + mm_nt(rest, kv_ref[...])
+            store_partner(out_refs, step, lanes, product.astype(jnp.bfloat16))
+
+    for step in range(size):
+        pl.when(pl.program_id(0) == step)(functools.partial(one, step))
 
 
 def input_grad(qkv_grad, own, other, columns, size):
@@ -757,11 +773,13 @@
     fixed = lambda i: (0, 0)
     weights = [columns.spec(part, own.shape[0]) for part in ("q", "q", "kv", "kv")]
     return pl.pallas_call(
-        input_grad_kernel,
+        functools.partial(input_grad_kernel, size=size),
         grid=(size,),
         in_specs=[pl.BlockSpec((rows, width), lambda i: (i, 0))] + weights,
-        out_specs=[pl.BlockSpec((rows, features), fixed)] * size,
-        out_shape=[jax.ShapeDtypeStruct((rows, features), jnp.bfloat16)] * size,
+        out_specs=[pl.BlockSpec((r, features), fixed) for r in partner_rows(size, rows)],
+        out_shape=[
+            jax.ShapeDtypeStruct((r, features), jnp.bfloat16) for r in partner_rows(size, rows)
+        ],
         compiler_params=PARAMS,
         cost_estimate=hint(2 * total * features * width),
     )(qkv_grad, own, other, own, other)
@@ -803,11 +821,10 @@
 
 
 def send_sum(blocks, held=()):
-    if len(blocks) != 4:
+    if lax.axis_size("tensor") != 4:
         return send_blocks(blocks), held
-    own, near_x, near_y, far = blocks
-    half = far.shape[0] // 2
-    top, bottom = swap(far[:half], 1), swap(far[half:], 2)
+    own, near_x, near_y, top, bottom = blocks
+    top, bottom = swap(top, 1), swap(bottom, 2)
     near_x, near_y = pl.pallas_call(
         merge_kernel,
         out_shape=[jax.ShapeDtypeStruct(near_x.shape, near_x.dtype)] * 2,

time: 604 us -> 603 us (level)
  transfers between devices with their start and end apart: 67 -> 67, of which waited for: 34 -> 33; matrix products, arithmetic and copies ran while one was open for 6% -> 5% of each run, Pallas kernels for 42% -> 42%
where the time goes in v2:
time: 603 us; the launch traced here: 594 us
  Pallas kernels  253 us (42%)
  waiting for transfers between devices  216 us (36%)
  starting transfers between devices  55.6 us (9%)
  local copies, waits for them, and re-layouts  27.6 us (5%)
  between operations  14.9 us (2%)
  other arithmetic  14.6 us (2%)
  blocking collectives  12.4 us (2%)
    ppermute x39, waiting for transfers between devices, swap(): return lax.ppermute(values, 'tensor', [(i, i ^ step) for i in range(size)])  174 us
    pallas_call x2, Pallas kernels, mlp(): pl.pallas_call(functools.partial(mlp_kernel, n_counts=[len(group) for gro...  78 us
    pallas_call x2, Pallas kernels, mlp_grads(): pl.pallas_call(functools.partial(grad_kernel, n_count=len(tokens), e_coun...  47.7 us
    ppermute x39, starting transfers between devices, swap(): return lax.ppermute(values, 'tensor', [(i, i ^ step) for i in range(size)])  46.5 us
    pallas_call x1, Pallas kernels, attend_back(): pl.pallas_call(functools.partial(attend_back_kernel, size=size, heads=hea...  26.6 us
    all_gather x3, waiting for transfers between devices, gather(): lax.all_gather(values, 'dp', axis=0, tiled=True, axis_index_groups=chip_l...  22.4 us
    pallas_call x1, Pallas kernels, attend(): pl.pallas_call(functools.partial(attend_kernel, size=size, heads=heads, g...  19.4 us
    ppermute x19, waiting for transfers between devices, cross(): return lax.ppermute(values, 'dp', [(i, i ^ 1) for i in range(count)])  17.5 us
  transfers between devices with their start and end apart: 67, of which 33 were waited for; matrix products, arithmetic and copies ran while one was open for 5% of the time, Pallas kernels for 42%

profile of v2, /device:TPU:0, one launch (start us, length us, event | category | flops | bytes accessed | tf_op | source)
XLA Modules:
  0.0 594.3 jit_solution(12038800421036310279)
XLA Ops:
  8.4 1.9 pad_maximum_fusion.2
  11.7 4.0 collective-permute-start.2
  16.5 12.4 %all_gather.13 = bf16[2,2048]{1,0:T(2,128)(2,1)S(1)} all-gather(bf16[2,256]{1,0:T(2,128)(2,1)S(1)} %pad_maximum_fusion.5), channel_id=1, replica_groups=mesh['dp'=8,'tensor'=4] {'dp'}, dimensions={1}, use_global_device_ids=true | all-gather | bytes 9216 | tf_op jit(solution)/shard_map/all_gather | solution.py:968
  29.0 1.5 copy.37
  36.3 1.9 fusion
  38.2 1.8 pad_maximum_fusion.3
  40.2 1.8 pad_maximum_fusion
  42.1 19.4 %collective-permute-done.1.refs_2_ = bf16[256,2048]{1,0:T(8,128)(2,1)} collective-permute-done((bf16[256,2048]{1,0:T(8,128)(2,1)S(1)}, bf16[256,2048]{1,0:T(8,128)(2,1)}, u32[]{:S(2)}, u32[]{:S(2)}) %collective-permute-start.1) | collective-permute-done | bytes 1048608 | tf_op jit(solution)/shard_map/ppermute | solution.py:790
  61.7 11.3 %all-gather.4.cloned.1.call-done.refs_5_.refs_7_.wo_ref.qo_ref.kvo_ref.refs_11_.refs_12_ = bf16[1024,1280]{1,0:T(8,128)(2,1)} async-done(((bf16[256,1280]{1,0:T(8,128)(2,1)}), bf16[1024,1280]{1,0:T(8,128)(2,1)}) %all-gather.4.cloned.1.call-update) | async-done | bytes 2621456 | tf_op jit(solution)/shard_map/all_gather | solution.py:866
  73.1 2.4 collective-permute-start.6
  78.2 1.5 copy-done
  79.7 11.9 %shard_map.203 = (bf16[1024,2048]{1,0:T(8,128)(2,1)}, bf16[1024,512]{1,0:T(8,128)(2,1)}, bf16[2,2,1024,128]{3,2,1,0:T(8,128)(2,1)}, bf16[2,2,1024,128]{3,2,1,0:T(8,128)(2,1)}) custom-call(s32[1]{0:T(128)} %bitcast.1.place_ref.me_ref, bf16[256,2048]{1,0:T(8,128)(2,1)} %copy-done.1, bf16[256,2048]{1,0:T(8,128)(2,1)} %collective-permute-done.refs_1_, ...), custom_call_target="tpu_custom_call" | custom-call | flops 201326592 | tf_op jit(solution)/shard_map/pallas_call | solution.py:161
  91.7 19.4 %shard_map.204 = (bf16[1024,512]{1,0:T(8,128)(2,1)}, f32[8,1024]{1,0:T(8,128)}, bf16[256,2048]{1,0:T(8,128)(2,1)}, bf16[256,2048]{1,0:T(8,128)(2,1)}, bf16[256,2...) custom-call(s32[1]{0:T(128)} %bitcast.1.place_ref.me_ref, ...), custom_call_target="tpu_custom_call" | custom-call | flops 268435456 | tf_op jit(solution)/shard_map/pallas_call | solution.py:249
  111.1 11.3 %collective-permute-done.5.refs_2_.refs_9_ = bf16[256,2048]{1,0:T(8,128)(2,1)} collective-permute-done((bf16[256,2048]{1,0:T(8,128)(2,1)}, bf16[256,2048]{1,0:T(8,128)(2,1)}, u32[]{:S(2)}, u32[]{:S(2)}) %collective-permute-start.5) | collective-permute-done | bytes 1048608 | tf_op jit(solution)/shard_map/ppermute | solution.py:790
  122.5 1.6 slice.172
  124.0 3.1 shard_map.206
  129.9 11.8 %collective-permute-done.7.top_ref = bf16[128,2048]{1,0:T(8,128)(2,1)S(1)} collective-permute-done((bf16[128,2048]{1,0:T(8,128)(2,1)}, bf16[128,2048]{1,0:T(8,128)(2,1)S(1)}, u32[]{:S(2)}, u32[]{:S(2)}) %collective-permute-start.7) | collective-permute-done | bytes 524320 | tf_op jit(solution)/shard_map/ppermute | solution.py:790
  143.0 3.3 shard_map.205
  148.4 22.1 %collective-permute-done.9.refs_1_ = bf16[256,2048]{1,0:T(8,128)(2,1)S(1)} collective-permute-done((bf16[256,2048]{1,0:T(8,128)(2,1)}, bf16[256,2048]{1,0:T(8,128)(2,1)S(1)}, u32[]{:S(2)}, u32[]{:S(2)}) %collective-permute-start.9) | collective-permute-done | bytes 1048608 | tf_op jit(solution)/shard_map/ppermute | solution.py:790
  172.6 4.5 shard_map.207
  180.5 9.9 %collective-permute-done.15.refs_3_ = bf16[128,2048]{1,0:T(8,128)(2,1)S(1)} collective-permute-done((bf16[128,2048]{1,0:T(8,128)(2,1)S(1)}, bf16[128,2048]{1,0:T(8,128)(2,1)S(1)}, u32[]{:S(2)}, u32[]{:S(2)}) %collective-permute-start.15) | collective-permute-done | bytes 524320 | tf_op jit(solution)/shard_map/ppermute | solution.py:790
  196.8 9.2 %collective-permute-done.16.refs_1_ = bf16[128,2048]{1,0:T(8,128)(2,1)S(1)} collective-permute-done((bf16[128,2048]{1,0:T(8,128)(2,1)S(1)}, bf16[128,2048]{1,0:T(8,128)(2,1)S(1)}, u32[]{:S(2)}, u32[]{:S(2)}) %collective-permute-start.16) | collective-permute-done | bytes 524320 | tf_op jit(solution)/shard_map/ppermute | solution.py:790
  207.2 10.5 %collective-permute-done.19.refs_6_ = bf16[128,2048]{1,0:T(8,128)(2,1)S(1)} collective-permute-done((bf16[128,2048]{1,0:T(8,128)(2,1)S(1)}, bf16[128,2048]{1,0:T(8,128)(2,1)S(1)}, u32[]{:S(2)}, u32[]{:S(2)}) %collective-permute-start.19) | collective-permute-done | bytes 524320 | tf_op jit(solution)/shard_map/ppermute | solution.py:790
  218.7 3.0 shard_map.209
  221.7 37.2 %shard_map.208 = (bf16[1024,1024]{1,0:T(8,128)(2,1)}, bf16[1024,1024]{1,0:T(8,128)(2,1)}, bf16[1024,1024]{1,0:T(8,128)(2,1)}, bf16[1024,2048]{1,0:T(8,128)(2,1)}, bf16[1024,2048]{1,0:T(8,128)(2,1)}) custom-call(bf16[256,2048]{1,0:T(8,128)(2,1)} %get-tuple-element.229.refs_0_, bf16[128,2048]{1,0:T(8,128)(2,1)} %copy-done.26, bf16[128,2048]{1,0:T(8,128)(2,1)} %copy-done.25, ...), custom_call_target="tpu_custom_call" | custom-call | flops 25769803776 | tf_op jit(solution)/shard_map/pallas_call | solution.py:468
  260.0 5.7 collective-permute-done.22.refs_16_
  266.6 3.0 collective-permute-done.24.refs_18_
  269.6 23.8 %shard_map.210 = bf16[4,256,3072]{2,1,0:T(8,128)(2,1)} custom-call(bf16[256,2048]{1,0:T(8,128)(2,1)} %get-tuple-element.229.refs_0_, bf16[128,2048]{1,0:T(8,128)(2,1)} %copy-done.26, bf16[128,2048]{1,0:T(8,128)(2,1)} %copy-done.25, bf16[128,2048]{1,0:T(8,128)(2,1)} %copy-done.24, bf16[128,2048]{1,0:T(8,128)(2,1)} %copy-done.27, ...), custom_call_target="tpu_custom_call" | custom-call | flops 12884901888 | tf_op jit(solution)/shard_map/pallas_call | solution.py:669
  293.5 11.1 %all-gather.8.cloned.1.call-done.refs_11_.refs_12_.refs_13_ = bf16[1024,3072]{1,0:T(8,128)(2,1)} async-done(((bf16[256,3072]{1,0:T(8,128)(2,1)}), bf16[1024,3072]{1,0:T(8,128)(2,1)}) %all-gather.8.cloned.1.call-update) | async-done | bytes 6291472 | tf_op jit(solution)/shard_map/all_gather | solution.py:866
  304.8 2.4 collective-permute-start.28
  308.3 6.9 %collective-permute-done.25.refs_14_.refs_15_.refs_16_ = bf16[1024,3072]{1,0:T(8,128)(2,1)} collective-permute-done((bf16[1024,3072]{1,0:T(8,128)(2,1)}, bf16[1024,3072]{1,0:T(8,128)(2,1)}, u32[]{:S(2)}, u32[]{:S(2)}) %collective-permute-start.25) | collective-permute-done | bytes 6291488 | tf_op jit(solution)/shard_map/ppermute | solution.py:847
  315.2 40.8 %shard_map.211 = (bf16[1024,1024]{1,0:T(8,128)(2,1)}, bf16[1024,1024]{1,0:T(8,128)(2,1)}, bf16[1024,1024]{1,0:T(8,128)(2,1)}, bf16[256,2048]{1,0:T(8,128)(2,1)},...) custom-call(bf16[256,2048]{1,0:T(8,128)(2,1)} %get-tuple-element.229, ...), custom_call_target="tpu_custom_call" | custom-call | flops 25769803776 | tf_op jit(solution)/shard_map/pallas_call | solution.py:468
  356.8 1.5 collective-permute-start.29
  359.7 2.3 slice.196.refs_10_
  362.0 9.2 %collective-permute-done.29.top_ref = bf16[128,2048]{1,0:T(8,128)(2,1)S(1)} collective-permute-done((bf16[128,2048]{1,0:T(8,128)(2,1)}, bf16[128,2048]{1,0:T(8,128)(2,1)S(1)}, u32[]{:S(2)}, u32[]{:S(2)}) %collective-permute-start.29) | collective-permute-done | bytes 524320 | tf_op jit(solution)/shard_map/ppermute | solution.py:790
  373.2 3.4 shard_map.212
  378.9 23.8 %shard_map.213 = bf16[4,256,3072]{2,1,0:T(8,128)(2,1)} custom-call(bf16[256,2048]{1,0:T(8,128)(2,1)} %get-tuple-element.229.refs_0_, bf16[128,2048]{1,0:T(8,128)(2,1)} %copy-done.26, bf16[128,2048]{1,0:T(8,128)(2,1)} %copy-done.25, bf16[128,2048]{1,0:T(8,128)(2,1)} %copy-done.24, bf16[128,2048]{1,0:T(8,128)(2,1)} %copy-done.27, ...), custom_call_target="tpu_custom_call" | custom-call | flops 12884901888 | tf_op jit(solution)/shard_map/pallas_call | solution.py:669
  403.7 4.1 fusion.3
  408.4 1.5 collective-permute-start.43
  409.9 9.7 %shard_map.214 = (f32[256,2048]{1,0:T(8,128)}, bf16[256,2048]{1,0:T(8,128)(2,1)}, f32[1,2048]{1,0:T(1,128)}, bf16[256,512]{1,0:T(8,128)(2,1)}, bf16[256,512]{1,0...) custom-call(bf16[256,2048]{1,0:T(8,128)(2,1)} %get-tuple-element.278.refs_0_, ...), custom_call_target="tpu_custom_call" | custom-call | flops 2147483648 | tf_op jit(solution)/shard_map/pallas_call | solution.py:623
  422.2 1.5 collective-permute-start.41
  423.8 16.4 %collective-permute-done.39.refs_1_ = bf16[256,512]{1,0:T(8,128)(2,1)S(1)} collective-permute-done((bf16[256,512]{1,0:T(8,128)(2,1)}, bf16[256,512]{1,0:T(8,128)(2,1)S(1)}, u32[]{:S(2)}, u32[]{:S(2)}) %collective-permute-start.39) | collective-permute-done | bytes 262176 | tf_op jit(solution)/shard_map/ppermute | solution.py:790
  440.1 4.9 collective-permute-done.41.refs_3_
  446.1 1.5 collective-permute-start.47
  447.5 1.5 collective-permute-start.46
  449.6 26.6 %shard_map.215.d_ref.refs_7_ = bf16[1024,768]{1,0:T(8,128)(2,1)} custom-call(s32[1]{0:T(128)} %bitcast.1.place_ref.me_ref, bf16[1024,512]{1,0:T(8,128)(2,1)} %get-tuple-element.195.q_ref, f32[8,1024]{1,0:T(8,128)} %get-tuple-element.295.l_ref, bf16[2,2,1024,128]{3,2,1,0:T(8,128)(2,1)} %get-tuple-element.196.k_ref, ...), custom_call_target="tpu_custom_call" | custom-call | flops 10737418240 | tf_op jit(solution)/shard_map/pallas_call | solution.py:384
  476.2 8.2 %shard_map.216 = (bf16[256,2048]{1,0:T(8,128)(2,1)}, bf16[256,2048]{1,0:T(8,128)(2,1)}, bf16[256,2048]{1,0:T(8,128)(2,1)}, bf16[128,2048]{1,0:T(8,128)(2,1)}, bf16[128,2048]{1,0:T(8,128)(2,1)}) custom-call(bf16[1024,768]{1,0:T(8,128)(2,1)} %shard_map.215.d_ref.refs_7_, ...), custom_call_target="tpu_custom_call" | custom-call | flops 3221225472 | tf_op jit(solution)/shard_map/pallas_call | solution.py:775
  484.5 8.8 %collective-permute-done.46.refs_2_.refs_4_ = bf16[256,2048]{1,0:T(8,128)(2,1)S(1)} collective-permute-done((bf16[256,2048]{1,0:T(8,128)(2,1)}, bf16[256,2048]{1,0:T(8,128)(2,1)S(1)}, u32[]{:S(2)}, u32[]{:S(2)}) %collective-permute-start.46) | collective-permute-done | bytes 1048608 | tf_op jit(solution)/shard_map/ppermute | solution.py:790
  494.3 3.1 shard_map.218
  502.0 10.1 %collective-permute-done.48.top_ref = bf16[128,2048]{1,0:T(8,128)(2,1)S(1)} collective-permute-done((bf16[128,2048]{1,0:T(8,128)(2,1)}, bf16[128,2048]{1,0:T(8,128)(2,1)S(1)}, u32[]{:S(2)}, u32[]{:S(2)}) %collective-permute-start.48) | collective-permute-done | bytes 524320 | tf_op jit(solution)/shard_map/ppermute | solution.py:790
  513.6 3.3 shard_map.217
  517.0 11.7 %shard_map.219 = (bf16[4,256,1280]{2,1,0:T(8,128)(2,1)}, f32[4,256,128]{2,1,0:T(8,128)}) custom-call(bf16[1024,2048]{1,0:T(8,128)(2,1)} %get-tuple-element.217.refs_0_, bf16[1024,1024]{1,0:T(8,128)(2,1)} %copy-done.9, bf16[256,2048]{1,0:T(8,128)(2,1)} %get-tuple-element.315.refs_0_.refs_2_, bf16[256,2048]{1,0:T(8,128)(2,1)} %collective-permute-done.45.refs_1_.refs_3_, ...), custom_call_target="tpu_custom_call" | custom-call | flops 5368709120 | tf_op jit(solution)/shard_map/pallas_call | solution.py:715
  529.2 1.5 collective-permute-start.52
  530.8 1.5 collective-permute-start.53
  534.2 1.5 collective-permute-start.54
  535.7 1.9 collective-permute-start.55
  537.6 2.5 collective-permute-start.56
  541.4 5.0 shard_map.220
  546.4 8.1 %collective-permute-done.52.refs_1_ = bf16[256,2048]{1,0:T(8,128)(2,1)S(1)} collective-permute-done((bf16[256,2048]{1,0:T(8,128)(2,1)}, bf16[256,2048]{1,0:T(8,128)(2,1)S(1)}, u32[]{:S(2)}, u32[]{:S(2)}) %collective-permute-start.52) | collective-permute-done | bytes 1048608 | tf_op jit(solution)/shard_map/ppermute | solution.py:790
  557.1 4.9 shard_map.221
  562.1 1.6 collective-permute-start.60
  565.7 14.9 %collective-permute-done.60 = f32[64,2]{0,1:T(2,128)S(1)} collective-permute-done((f32[64,2]{0,1:T(2,128)S(1)}, f32[64,2]{0,1:T(2,128)S(1)}, u32[]{:S(2)}, u32[]{:S(2)}) %collective-permute-start.60) | collective-permute-done | bytes 544 | tf_op jit(solution)/shard_map/ppermute | solution.py:790
  580.6 4.0 shard_map.222
  585.1 2.2 shard_map.223
  (246 shorter events, 64.3 us)
Async XLA Ops:
  7.2 65.8 %all-gather.4.cloned.1.call-start = ((), (), s32[]{:S(2)}) async-start(), calls=%async_computation.3 | async-start | bytes 3276800 | tf_op jit(solution)/shard_map/all_gather | solution.py:866
  11.7 30.3 %collective-permute-start.2 = (bf16[256,2048]{1,0:T(8,128)(2,1)S(1)}, bf16[256,2048]{1,0:T(8,128)(2,1)}, u32[]{:S(2)}, u32[]{:S(2)}) collective-permute-start(bf16[256,2048]{1,0:T(8,128)(2,1)S(1)} %select_dynamic-update-slice_fusion.8.refs_0_.refs_3_), channel_id=1, source_target_pairs={{0,3},{1,2},{2,1},{3,0},{4,7},{5,6},{6,5},{7,4},{8,11},{9,10},{10,... | collective-permute-start | bytes 3145736 | tf_op jit(solution)/shard_map/ppermute | solution.py:790
  15.7 45.7 %collective-permute-start.1 = (bf16[256,2048]{1,0:T(8,128)(2,1)S(1)}, bf16[256,2048]{1,0:T(8,128)(2,1)}, u32[]{:S(2)}, u32[]{:S(2)}) collective-permute-start(bf16[256,2048]{1,0:T(8,128)(2,1)S(1)} %select_dynamic-update-slice_fusion.8.refs_0_.refs_3_), channel_id=1, source_target_pairs={{0,2},{1,3},{2,0},{3,1},{4,6},{5,7},{6,4},{7,5},{8,10},{9,11},{10,... | collective-permute-start | bytes 3145736 | tf_op jit(solution)/shard_map/ppermute | solution.py:790
  16.2 45.5 %collective-permute-start = (bf16[256,2048]{1,0:T(8,128)(2,1)S(1)}, bf16[256,2048]{1,0:T(8,128)(2,1)}, u32[]{:S(2)}, u32[]{:S(2)}) collective-permute-start(bf16[256,2048]{1,0:T(8,128)(2,1)S(1)} %select_dynamic-update-slice_fusion.8.refs_0_.refs_3_), channel_id=1, source_target_pairs={{0,1},{1,0},{2,3},{3,2},{4,5},{5,4},{6,7},{7,6},{8,9},{9,8},{10,11... | collective-permute-start | bytes 3145736 | tf_op jit(solution)/shard_map/ppermute | solution.py:790
  16.4 174.8 %all-gather.6.cloned.1.call-start = ((), (), s32[]{:S(2)}) async-start(), calls=%async_computation.4 | async-start | bytes 7864320 | tf_op jit(solution)/shard_map/all_gather | solution.py:866
  73.0 231.6 %all-gather.8.cloned.1.call-start = ((), (), s32[]{:S(2)}) async-start(), calls=%async_computation.5 | async-start | bytes 7864320 | tf_op jit(solution)/shard_map/all_gather | solution.py:866
  73.1 5.2 collective-permute-start.3
  73.1 37.9 %collective-permute-start.6 = (bf16[256,2048]{1,0:T(8,128)(2,1)}, bf16[256,2048]{1,0:T(8,128)(2,1)}, u32[]{:S(2)}, u32[]{:S(2)}) collective-permute-start(bf16[256,2048]{1,0:T(8,128)(2,1)} %select_dynamic-update-slice_fusion.refs_0_.refs_7_.refs_4_), channel_id=1, source_target_pairs={{0,3},{1,2},{2,1},{3,0},{4,7},{5,6},{6,5},{7,4},{8,11},{9,10},{10,... | collective-permute-start | bytes 3145736 | tf_op jit(solution)/shard_map/ppermute | solution.py:790
  75.6 46.8 %collective-permute-start.5 = (bf16[256,2048]{1,0:T(8,128)(2,1)}, bf16[256,2048]{1,0:T(8,128)(2,1)}, u32[]{:S(2)}, u32[]{:S(2)}) collective-permute-start(bf16[256,2048]{1,0:T(8,128)(2,1)} %select_dynamic-update-slice_fusion.refs_0_.refs_7_.refs_4_), channel_id=1, source_target_pairs={{0,2},{1,3},{2,0},{3,1},{4,6},{5,7},{6,4},{7,5},{8,10},{9,11},{10,... | collective-permute-start | bytes 3145736 | tf_op jit(solution)/shard_map/ppermute | solution.py:790
  76.1 46.3 %collective-permute-start.4 = (bf16[256,2048]{1,0:T(8,128)(2,1)}, bf16[256,2048]{1,0:T(8,128)(2,1)}, u32[]{:S(2)}, u32[]{:S(2)}) collective-permute-start(bf16[256,2048]{1,0:T(8,128)(2,1)} %select_dynamic-update-slice_fusion.refs_0_.refs_7_.refs_4_), channel_id=1, source_target_pairs={{0,1},{1,0},{2,3},{3,2},{4,5},{5,4},{6,7},{7,6},{8,9},{9,8},{10,11... | collective-permute-start | bytes 3145736 | tf_op jit(solution)/shard_map/ppermute | solution.py:790
  127.2 44.4 %collective-permute-start.11 = (bf16[1024,1024]{1,0:T(8,128)(2,1)}, bf16[1024,1024]{1,0:T(8,128)(2,1)}, u32[]{:S(2)}, u32[]{:S(2)}) collective-permute-start(bf16[1024,1024]{1,0:T(8,128)(2,1)} %shard_map.206), channel_id=1, source_target_pairs={{0,4},{4,0},{8,12},{12,8},{16,20},{20,16},{24,28},{28,24},{1,5},{5... | collective-permute-start | bytes 6291464 | tf_op jit(solution)/shard_map/ppermute | solution.py:847
  127.2 44.4 %collective-permute-start.12 = (bf16[1024,1024]{1,0:T(8,128)(2,1)S(1)}, bf16[1024,1024]{1,0:T(8,128)(2,1)S(1)}, u32[]{:S(2)}, u32[]{:S(2)}) collective-permute-start(bf16[1024,1024]{1,0:T(8,128)(2,1)S(1)} %copy-done.10), channel_id=1, source_target_pairs={{0,4},{4,0},{8,12},{12,8},{16,20},{20,16},{24,28},{28,24},{1,5},{5... | collective-permute-start | bytes 6291464 | tf_op jit(solution)/shard_map/ppermute | solution.py:847
  127.7 14.0 %collective-permute-start.7 = (bf16[128,2048]{1,0:T(8,128)(2,1)}, bf16[128,2048]{1,0:T(8,128)(2,1)S(1)}, u32[]{:S(2)}, u32[]{:S(2)}) collective-permute-start(bf16[128,2048]{1,0:T(8,128)(2,1)} %get-tuple-element.209), channel_id=1, source_target_pairs={{0,1},{1,0},{2,3},{3,2},{4,5},{5,4},{6,7},{7,6},{8,9},{9,8},{10,11... | collective-permute-start | bytes 1572872 | tf_op jit(solution)/shard_map/ppermute | solution.py:790
  129.2 13.9 %collective-permute-start.8 = (bf16[128,2048]{1,0:T(8,128)(2,1)}, bf16[128,2048]{1,0:T(8,128)(2,1)}, u32[]{:S(2)}, u32[]{:S(2)}) collective-permute-start(bf16[128,2048]{1,0:T(8,128)(2,1)} %get-tuple-element.210), channel_id=1, source_target_pairs={{0,2},{1,3},{2,0},{3,1},{4,6},{5,7},{6,4},{7,5},{8,10},{9,11},{10,... | collective-permute-start | bytes 1572872 | tf_op jit(solution)/shard_map/ppermute | solution.py:790
  129.9 18.4 %collective-permute-start.13 = (bf16[1024,512]{1,0:T(8,128)(2,1)S(1)}, bf16[1024,512]{1,0:T(8,128)(2,1)}, u32[]{:S(2)}, u32[]{:S(2)}) collective-permute-start(bf16[1024,512]{1,0:T(8,128)(2,1)S(1)} %copy-done.11), channel_id=1, source_target_pairs={{0,4},{4,0},{8,12},{12,8},{16,20},{20,16},{24,28},{28,24},{1,5},{5... | collective-permute-start | bytes 3145736 | tf_op jit(solution)/shard_map/ppermute | solution.py:847
  146.3 24.1 %collective-permute-start.9 = (bf16[256,2048]{1,0:T(8,128)(2,1)}, bf16[256,2048]{1,0:T(8,128)(2,1)S(1)}, u32[]{:S(2)}, u32[]{:S(2)}) collective-permute-start(bf16[256,2048]{1,0:T(8,128)(2,1)} %get-tuple-element.211), channel_id=1, source_target_pairs={{0,1},{1,0},{2,3},{3,2},{4,5},{5,4},{6,7},{7,6},{8,9},{9,8},{10,11... | collective-permute-start | bytes 3145736 | tf_op jit(solution)/shard_map/ppermute | solution.py:790
  147.3 24.3 %collective-permute-start.10 = (bf16[256,2048]{1,0:T(8,128)(2,1)}, bf16[256,2048]{1,0:T(8,128)(2,1)S(1)}, u32[]{:S(2)}, u32[]{:S(2)}) collective-permute-start(bf16[256,2048]{1,0:T(8,128)(2,1)} %get-tuple-element.212), channel_id=1, source_target_pairs={{0,2},{1,3},{2,0},{3,1},{4,6},{5,7},{6,4},{7,5},{8,10},{9,11},{10,... | collective-permute-start | bytes 3145736 | tf_op jit(solution)/shard_map/ppermute | solution.py:790
  178.4 12.1 %collective-permute-start.15 = (bf16[128,2048]{1,0:T(8,128)(2,1)S(1)}, bf16[128,2048]{1,0:T(8,128)(2,1)S(1)}, u32[]{:S(2)}, u32[]{:S(2)}) collective-permute-start(bf16[128,2048]{1,0:T(8,128)(2,1)S(1)} %get-tuple-element.224), channel_id=1, source_target_pairs={{0,2},{1,3},{2,0},{3,1},{4,6},{5,7},{6,4},{7,5},{8,10},{9,11},{10,... | collective-permute-start | bytes 1572872 | tf_op jit(solution)/shard_map/ppermute | solution.py:790
  179.2 11.9 %collective-permute-start.14 = (bf16[128,2048]{1,0:T(8,128)(2,1)S(1)}, bf16[128,2048]{1,0:T(8,128)(2,1)S(1)}, u32[]{:S(2)}, u32[]{:S(2)}) collective-permute-start(bf16[128,2048]{1,0:T(8,128)(2,1)S(1)} %get-tuple-element.227), channel_id=1, source_target_pairs={{0,1},{1,0},{2,3},{3,2},{4,5},{5,4},{6,7},{7,6},{8,9},{9,8},{10,11... | collective-permute-start | bytes 1572872 | tf_op jit(solution)/shard_map/ppermute | solution.py:790
  191.1 26.6 %collective-permute-start.20 = (bf16[1024,3072]{1,0:T(8,128)(2,1)}, bf16[1024,3072]{1,0:T(8,128)(2,1)}, u32[]{:S(2)}, u32[]{:S(2)}) collective-permute-start(bf16[1024,3072]{1,0:T(8,128)(2,1)} %all-gather.6.cloned.1.call-done.refs_11_.refs_12_.refs_13_), channel_id=1, source_target_pairs={{0,4},{4,0},{8,12},{12,8},{16,20},{20,16},{24,28},{28,24},{1,5},{5... | collective-permute-start | bytes 18874376 | tf_op jit(solution)/shard_map/ppermute | solution.py:847
  191.2 285.1 %reduce-scatter.4.cloned.1.call-start = ((), (), s32[]{:S(2)}) async-start(), calls=%async_computation.6 | async-start | bytes 7864320 | tf_op jit(solution)/shard_map/reduce_scatter | solution.py:870
  191.2 14.8 %collective-permute-start.16 = (bf16[128,2048]{1,0:T(8,128)(2,1)S(1)}, bf16[128,2048]{1,0:T(8,128)(2,1)S(1)}, u32[]{:S(2)}, u32[]{:S(2)}) collective-permute-start(bf16[128,2048]{1,0:T(8,128)(2,1)S(1)} %get-tuple-element.224), channel_id=1, source_target_pairs={{0,1},{1,0},{2,3},{3,2},{4,5},{5,4},{6,7},{7,6},{8,9},{9,8},{10,11... | collective-permute-start | bytes 1572872 | tf_op jit(solution)/shard_map/ppermute | solution.py:790
  192.4 14.8 %collective-permute-start.17 = (bf16[128,2048]{1,0:T(8,128)(2,1)S(1)}, bf16[128,2048]{1,0:T(8,128)(2,1)S(1)}, u32[]{:S(2)}, u32[]{:S(2)}) collective-permute-start(bf16[128,2048]{1,0:T(8,128)(2,1)S(1)} %get-tuple-element.227), channel_id=1, source_target_pairs={{0,2},{1,3},{2,0},{3,1},{4,6},{5,7},{6,4},{7,5},{8,10},{9,11},{10,... | collective-permute-start | bytes 1572872 | tf_op jit(solution)/shard_map/ppermute | solution.py:790
  193.2 24.5 %collective-permute-start.19 = (bf16[128,2048]{1,0:T(8,128)(2,1)S(1)}, bf16[128,2048]{1,0:T(8,128)(2,1)S(1)}, u32[]{:S(2)}, u32[]{:S(2)}) collective-permute-start(bf16[128,2048]{1,0:T(8,128)(2,1)S(1)} %collective-permute-done.14.refs_2_), channel_id=1, source_target_pairs={{0,2},{1,3},{2,0},{3,1},{4,6},{5,7},{6,4},{7,5},{8,10},{9,11},{10,... | collective-permute-start | bytes 1572872 | tf_op jit(solution)/shard_map/ppermute | solution.py:790
  194.4 23.3 %collective-permute-start.18 = (bf16[128,2048]{1,0:T(8,128)(2,1)S(1)}, bf16[128,2048]{1,0:T(8,128)(2,1)S(1)}, u32[]{:S(2)}, u32[]{:S(2)}) collective-permute-start(bf16[128,2048]{1,0:T(8,128)(2,1)S(1)} %collective-permute-done.15.refs_3_), channel_id=1, source_target_pairs={{0,1},{1,0},{2,3},{3,2},{4,5},{5,4},{6,7},{7,6},{8,9},{9,8},{10,11... | collective-permute-start | bytes 1572872 | tf_op jit(solution)/shard_map/ppermute | solution.py:790
  221.7 37.2 %collective-permute-start.21 = (bf16[1024,1024]{1,0:T(8,128)(2,1)}, bf16[1024,1024]{1,0:T(8,128)(2,1)S(1)}, u32[]{:S(2)}, u32[]{:S(2)}) collective-permute-start(bf16[1024,1024]{1,0:T(8,128)(2,1)} %shard_map.209), channel_id=1, source_target_pairs={{0,4},{4,0},{8,12},{12,8},{16,20},{20,16},{24,28},{28,24},{1,5},{5... | collective-permute-start | bytes 6291464 | tf_op jit(solution)/shard_map/ppermute | solution.py:847
  259.0 6.8 %collective-permute-start.22 = (bf16[1024,1024]{1,0:T(8,128)(2,1)}, bf16[1024,1024]{1,0:T(8,128)(2,1)S(1)}, u32[]{:S(2)}, u32[]{:S(2)}) collective-permute-start(bf16[1024,1024]{1,0:T(8,128)(2,1)} %get-tuple-element.243.refs_13_), channel_id=1, source_target_pairs={{0,4},{4,0},{8,12},{12,8},{16,20},{20,16},{24,28},{28,24},{1,5},{5... | collective-permute-start | bytes 6291464 | tf_op jit(solution)/shard_map/ppermute | solution.py:847
  259.5 7.1 %collective-permute-start.23 = (bf16[1024,1024]{1,0:T(8,128)(2,1)}, bf16[1024,1024]{1,0:T(8,128)(2,1)}, u32[]{:S(2)}, u32[]{:S(2)}) collective-permute-start(bf16[1024,1024]{1,0:T(8,128)(2,1)} %get-tuple-element.244.refs_14_), channel_id=1, source_target_pairs={{0,4},{4,0},{8,12},{12,8},{16,20},{20,16},{24,28},{28,24},{1,5},{5... | collective-permute-start | bytes 6291464 | tf_op jit(solution)/shard_map/ppermute | solution.py:847
  259.6 10.0 %collective-permute-start.24 = (bf16[1024,1024]{1,0:T(8,128)(2,1)}, bf16[1024,1024]{1,0:T(8,128)(2,1)}, u32[]{:S(2)}, u32[]{:S(2)}) collective-permute-start(bf16[1024,1024]{1,0:T(8,128)(2,1)} %get-tuple-element.245.refs_15_), channel_id=1, source_target_pairs={{0,4},{4,0},{8,12},{12,8},{16,20},{20,16},{24,28},{28,24},{1,5},{5... | collective-permute-start | bytes 6291464 | tf_op jit(solution)/shard_map/ppermute | solution.py:847
  304.6 224.6 %reduce-scatter.6.cloned.1.call-start = ((), (), s32[]{:S(2)}) async-start(), calls=%async_computation.7 | async-start | bytes 7864320 | tf_op jit(solution)/shard_map/reduce_scatter | solution.py:870
  304.7 10.6 %collective-permute-start.25 = (bf16[1024,3072]{1,0:T(8,128)(2,1)}, bf16[1024,3072]{1,0:T(8,128)(2,1)}, u32[]{:S(2)}, u32[]{:S(2)}) collective-permute-start(bf16[1024,3072]{1,0:T(8,128)(2,1)} %all-gather.8.cloned.1.call-done.refs_11_.refs_12_.refs_13_), channel_id=1, source_target_pairs={{0,4},{4,0},{8,12},{12,8},{16,20},{20,16},{24,28},{28,24},{1,5},{5... | collective-permute-start | bytes 18874376 | tf_op jit(solution)/shard_map/ppermute | solution.py:847
  304.8 51.2 %collective-permute-start.28 = (bf16[1024,512]{1,0:T(8,128)(2,1)S(1)}, bf16[1024,512]{1,0:T(8,128)(2,1)S(1)}, u32[]{:S(2)}, u32[]{:S(2)}) collective-permute-start(bf16[1024,512]{1,0:T(8,128)(2,1)S(1)} %slice.176.refs_6_), channel_id=1, source_target_pairs={{0,3},{1,2},{2,1},{3,0},{4,7},{5,6},{6,5},{7,4},{8,11},{9,10},{10,... | collective-permute-start | bytes 3145736 | tf_op jit(solution)/shard_map/ppermute | solution.py:790
  307.2 48.9 %collective-permute-start.27 = (bf16[1024,512]{1,0:T(8,128)(2,1)S(1)}, bf16[1024,512]{1,0:T(8,128)(2,1)S(1)}, u32[]{:S(2)}, u32[]{:S(2)}) collective-permute-start(bf16[1024,512]{1,0:T(8,128)(2,1)S(1)} %slice.176.refs_6_), channel_id=1, source_target_pairs={{0,2},{1,3},{2,0},{3,1},{4,6},{5,7},{6,4},{7,5},{8,10},{9,11},{10,... | collective-permute-start | bytes 3145736 | tf_op jit(solution)/shard_map/ppermute | solution.py:790
  307.7 48.3 %collective-permute-start.26 = (bf16[1024,512]{1,0:T(8,128)(2,1)S(1)}, bf16[1024,512]{1,0:T(8,128)(2,1)}, u32[]{:S(2)}, u32[]{:S(2)}) collective-permute-start(bf16[1024,512]{1,0:T(8,128)(2,1)S(1)} %slice.176.refs_6_), channel_id=1, source_target_pairs={{0,1},{1,0},{2,3},{3,2},{4,5},{5,4},{6,7},{7,6},{8,9},{9,8},{10,11... | collective-permute-start | bytes 3145736 | tf_op jit(solution)/shard_map/ppermute | solution.py:790
  356.1 20.5 %collective-permute-start.31 = (bf16[1024,1024]{1,0:T(8,128)(2,1)}, bf16[1024,1024]{1,0:T(8,128)(2,1)}, u32[]{:S(2)}, u32[]{:S(2)}) collective-permute-start(bf16[1024,1024]{1,0:T(8,128)(2,1)} %get-tuple-element.268.refs_13_), channel_id=1, source_target_pairs={{0,4},{4,0},{8,12},{12,8},{16,20},{20,16},{24,28},{28,24},{1,5},{5... | collective-permute-start | bytes 6291464 | tf_op jit(solution)/shard_map/ppermute | solution.py:847
  356.3 20.4 %collective-permute-start.32 = (bf16[1024,1024]{1,0:T(8,128)(2,1)}, bf16[1024,1024]{1,0:T(8,128)(2,1)}, u32[]{:S(2)}, u32[]{:S(2)}) collective-permute-start(bf16[1024,1024]{1,0:T(8,128)(2,1)} %get-tuple-element.269.refs_14_), channel_id=1, source_target_pairs={{0,4},{4,0},{8,12},{12,8},{16,20},{20,16},{24,28},{28,24},{1,5},{5... | collective-permute-start | bytes 6291464 | tf_op jit(solution)/shard_map/ppermute | solution.py:847
  356.6 20.8 %collective-permute-start.33 = (bf16[1024,1024]{1,0:T(8,128)(2,1)}, bf16[1024,1024]{1,0:T(8,128)(2,1)}, u32[]{:S(2)}, u32[]{:S(2)}) collective-permute-start(bf16[1024,1024]{1,0:T(8,128)(2,1)} %get-tuple-element.270.refs_15_), channel_id=1, source_target_pairs={{0,4},{4,0},{8,12},{12,8},{16,20},{20,16},{24,28},{28,24},{1,5},{5... | collective-permute-start | bytes 6291464 | tf_op jit(solution)/shard_map/ppermute | solution.py:847
  356.8 14.4 %collective-permute-start.29 = (bf16[128,2048]{1,0:T(8,128)(2,1)}, bf16[128,2048]{1,0:T(8,128)(2,1)S(1)}, u32[]{:S(2)}, u32[]{:S(2)}) collective-permute-start(bf16[128,2048]{1,0:T(8,128)(2,1)} %get-tuple-element.261), channel_id=1, source_target_pairs={{0,1},{1,0},{2,3},{3,2},{4,5},{5,4},{6,7},{7,6},{8,9},{9,8},{10,11... | collective-permute-start | bytes 1572872 | tf_op jit(solution)/shard_map/ppermute | solution.py:790
  358.3 14.1 %collective-permute-start.30 = (bf16[128,2048]{1,0:T(8,128)(2,1)}, bf16[128,2048]{1,0:T(8,128)(2,1)S(1)}, u32[]{:S(2)}, u32[]{:S(2)}) collective-permute-start(bf16[128,2048]{1,0:T(8,128)(2,1)} %get-tuple-element.262), channel_id=1, source_target_pairs={{0,2},{1,3},{2,0},{3,1},{4,6},{5,7},{6,4},{7,5},{8,10},{9,11},{10,... | collective-permute-start | bytes 1572872 | tf_op jit(solution)/shard_map/ppermute | solution.py:790
  371.2 31.5 %collective-permute-start.36 = (bf16[1024,512]{1,0:T(8,128)(2,1)}, bf16[1024,512]{1,0:T(8,128)(2,1)S(1)}, u32[]{:S(2)}, u32[]{:S(2)}) collective-permute-start(bf16[1024,512]{1,0:T(8,128)(2,1)} %collective-permute-done.26.refs_7_), channel_id=1, source_target_pairs={{0,4},{4,0},{8,12},{12,8},{16,20},{20,16},{24,28},{28,24},{1,5},{5... | collective-permute-start | bytes 3145736 | tf_op jit(solution)/shard_map/ppermute | solution.py:847
  372.4 30.4 %collective-permute-start.37 = (bf16[1024,512]{1,0:T(8,128)(2,1)S(1)}, bf16[1024,512]{1,0:T(8,128)(2,1)}, u32[]{:S(2)}, u32[]{:S(2)}) collective-permute-start(bf16[1024,512]{1,0:T(8,128)(2,1)S(1)} %collective-permute-done.27.refs_8_), channel_id=1, source_target_pairs={{0,4},{4,0},{8,12},{12,8},{16,20},{20,16},{24,28},{28,24},{1,5},{5... | collective-permute-start | bytes 3145736 | tf_op jit(solution)/shard_map/ppermute | solution.py:847
  376.6 26.2 %collective-permute-start.38 = (bf16[1024,512]{1,0:T(8,128)(2,1)S(1)}, bf16[1024,512]{1,0:T(8,128)(2,1)}, u32[]{:S(2)}, u32[]{:S(2)}) collective-permute-start(bf16[1024,512]{1,0:T(8,128)(2,1)S(1)} %collective-permute-done.28.refs_9_), channel_id=1, source_target_pairs={{0,4},{4,0},{8,12},{12,8},{16,20},{20,16},{24,28},{28,24},{1,5},{5... | collective-permute-start | bytes 3145736 | tf_op jit(solution)/shard_map/ppermute | solution.py:847
  376.7 26.1 %collective-permute-start.34 = (bf16[256,2048]{1,0:T(8,128)(2,1)}, bf16[256,2048]{1,0:T(8,128)(2,1)}, u32[]{:S(2)}, u32[]{:S(2)}) collective-permute-start(bf16[256,2048]{1,0:T(8,128)(2,1)} %get-tuple-element.272), channel_id=1, source_target_pairs={{0,1},{1,0},{2,3},{3,2},{4,5},{5,4},{6,7},{7,6},{8,9},{9,8},{10,11... | collective-permute-start | bytes 3145736 | tf_op jit(solution)/shard_map/ppermute | solution.py:790
  377.4 25.4 %collective-permute-start.35 = (bf16[256,2048]{1,0:T(8,128)(2,1)}, bf16[256,2048]{1,0:T(8,128)(2,1)}, u32[]{:S(2)}, u32[]{:S(2)}) collective-permute-start(bf16[256,2048]{1,0:T(8,128)(2,1)} %get-tuple-element.273), channel_id=1, source_target_pairs={{0,2},{1,3},{2,0},{3,1},{4,6},{5,7},{6,4},{7,5},{8,10},{9,11},{10,... | collective-permute-start | bytes 3145736 | tf_op jit(solution)/shard_map/ppermute | solution.py:790
  403.7 181.4 %reduce-scatter.8.cloned.1.call-start = ((), (), s32[]{:S(2)}) async-start(), calls=%async_computation.8 | async-start | bytes 3276800 | tf_op jit(solution)/shard_map/reduce_scatter | solution.py:870
  407.8 37.2 %collective-permute-start.44 = (bf16[256,2048]{1,0:T(8,128)(2,1)S(1)}, bf16[256,2048]{1,0:T(8,128)(2,1)S(1)}, u32[]{:S(2)}, u32[]{:S(2)}) collective-permute-start(bf16[256,2048]{1,0:T(8,128)(2,1)S(1)} %get-tuple-element.358), channel_id=1, source_target_pairs={{0,2},{1,3},{2,0},{3,1},{4,6},{5,7},{6,4},{7,5},{8,10},{9,11},{10,... | collective-permute-start | bytes 3145736 | tf_op jit(solution)/shard_map/ppermute | solution.py:790
  408.4 36.6 %collective-permute-start.43 = (bf16[256,2048]{1,0:T(8,128)(2,1)S(1)}, bf16[256,2048]{1,0:T(8,128)(2,1)S(1)}, u32[]{:S(2)}, u32[]{:S(2)}) collective-permute-start(bf16[256,2048]{1,0:T(8,128)(2,1)S(1)} %get-tuple-element.359), channel_id=1, source_target_pairs={{0,1},{1,0},{2,3},{3,2},{4,5},{5,4},{6,7},{7,6},{8,9},{9,8},{10,11... | collective-permute-start | bytes 3145736 | tf_op jit(solution)/shard_map/ppermute | solution.py:790
  420.3 19.9 %collective-permute-start.39 = (bf16[256,512]{1,0:T(8,128)(2,1)}, bf16[256,512]{1,0:T(8,128)(2,1)S(1)}, u32[]{:S(2)}, u32[]{:S(2)}) collective-permute-start(bf16[256,512]{1,0:T(8,128)(2,1)} %get-tuple-element.288), channel_id=1, source_target_pairs={{0,1},{1,0},{2,3},{3,2},{4,5},{5,4},{6,7},{7,6},{8,9},{9,8},{10,11... | collective-permute-start | bytes 786440 | tf_op jit(solution)/shard_map/ppermute | solution.py:790
  420.8 19.3 %collective-permute-start.40 = (bf16[256,512]{1,0:T(8,128)(2,1)}, bf16[256,512]{1,0:T(8,128)(2,1)S(1)}, u32[]{:S(2)}, u32[]{:S(2)}) collective-permute-start(bf16[256,512]{1,0:T(8,128)(2,1)} %get-tuple-element.289), channel_id=1, source_target_pairs={{0,2},{1,3},{2,0},{3,1},{4,6},{5,7},{6,4},{7,5},{8,10},{9,11},{10,... | collective-permute-start | bytes 786440 | tf_op jit(solution)/shard_map/ppermute | solution.py:790
  422.2 22.8 %collective-permute-start.41 = (bf16[256,512]{1,0:T(8,128)(2,1)}, bf16[256,512]{1,0:T(8,128)(2,1)S(1)}, u32[]{:S(2)}, u32[]{:S(2)}) collective-permute-start(bf16[256,512]{1,0:T(8,128)(2,1)} %get-tuple-element.290), channel_id=1, source_target_pairs={{0,3},{1,2},{2,1},{3,0},{4,7},{5,6},{6,5},{7,4},{8,11},{9,10},{10,... | collective-permute-start | bytes 786440 | tf_op jit(solution)/shard_map/ppermute | solution.py:790
  446.1 38.4 %collective-permute-start.47 = (bf16[256,2048]{1,0:T(8,128)(2,1)}, bf16[256,2048]{1,0:T(8,128)(2,1)S(1)}, u32[]{:S(2)}, u32[]{:S(2)}) collective-permute-start(bf16[256,2048]{1,0:T(8,128)(2,1)} %get-tuple-element.315.refs_0_.refs_2_), channel_id=1, source_target_pairs={{0,3},{1,2},{2,1},{3,0},{4,7},{5,6},{6,5},{7,4},{8,11},{9,10},{10,... | collective-permute-start | bytes 3145736 | tf_op jit(solution)/shard_map/ppermute | solution.py:790
  447.5 45.7 %collective-permute-start.46 = (bf16[256,2048]{1,0:T(8,128)(2,1)}, bf16[256,2048]{1,0:T(8,128)(2,1)S(1)}, u32[]{:S(2)}, u32[]{:S(2)}) collective-permute-start(bf16[256,2048]{1,0:T(8,128)(2,1)} %get-tuple-element.315.refs_0_.refs_2_), channel_id=1, source_target_pairs={{0,2},{1,3},{2,0},{3,1},{4,6},{5,7},{6,4},{7,5},{8,10},{9,11},{10,... | collective-permute-start | bytes 3145736 | tf_op jit(solution)/shard_map/ppermute | solution.py:790
  449.0 44.2 %collective-permute-start.45 = (bf16[256,2048]{1,0:T(8,128)(2,1)}, bf16[256,2048]{1,0:T(8,128)(2,1)}, u32[]{:S(2)}, u32[]{:S(2)}) collective-permute-start(bf16[256,2048]{1,0:T(8,128)(2,1)} %get-tuple-element.315.refs_0_.refs_2_), channel_id=1, source_target_pairs={{0,1},{1,0},{2,3},{3,2},{4,5},{5,4},{6,7},{7,6},{8,9},{9,8},{10,11... | collective-permute-start | bytes 3145736 | tf_op jit(solution)/shard_map/ppermute | solution.py:790
  497.3 19.6 %collective-permute-start.50 = (bf16[1024,1024]{1,0:T(8,128)(2,1)}, bf16[1024,1024]{1,0:T(8,128)(2,1)}, u32[]{:S(2)}, u32[]{:S(2)}) collective-permute-start(bf16[1024,1024]{1,0:T(8,128)(2,1)} %shard_map.218), channel_id=1, source_target_pairs={{0,4},{4,0},{8,12},{12,8},{16,20},{20,16},{24,28},{28,24},{1,5},{5... | collective-permute-start | bytes 6291464 | tf_op jit(solution)/shard_map/ppermute | solution.py:847
  497.5 19.5 %collective-permute-start.51 = (bf16[1024,768]{1,0:T(8,128)(2,1)S(1)}, bf16[1024,768]{1,0:T(8,128)(2,1)}, u32[]{:S(2)}, u32[]{:S(2)}) collective-permute-start(bf16[1024,768]{1,0:T(8,128)(2,1)S(1)} %copy-done.3), channel_id=1, source_target_pairs={{0,4},{4,0},{8,12},{12,8},{16,20},{20,16},{24,28},{28,24},{1,5},{5... | collective-permute-start | bytes 4718600 | tf_op jit(solution)/shard_map/ppermute | solution.py:847
  497.9 14.2 %collective-permute-start.48 = (bf16[128,2048]{1,0:T(8,128)(2,1)}, bf16[128,2048]{1,0:T(8,128)(2,1)S(1)}, u32[]{:S(2)}, u32[]{:S(2)}) collective-permute-start(bf16[128,2048]{1,0:T(8,128)(2,1)} %get-tuple-element.310), channel_id=1, source_target_pairs={{0,1},{1,0},{2,3},{3,2},{4,5},{5,4},{6,7},{7,6},{8,9},{9,8},{10,11... | collective-permute-start | bytes 1572872 | tf_op jit(solution)/shard_map/ppermute | solution.py:790
  499.0 13.8 %collective-permute-start.49 = (bf16[128,2048]{1,0:T(8,128)(2,1)}, bf16[128,2048]{1,0:T(8,128)(2,1)S(1)}, u32[]{:S(2)}, u32[]{:S(2)}) collective-permute-start(bf16[128,2048]{1,0:T(8,128)(2,1)} %get-tuple-element.311), channel_id=1, source_target_pairs={{0,2},{1,3},{2,0},{3,1},{4,6},{5,7},{6,4},{7,5},{8,10},{9,11},{10,... | collective-permute-start | bytes 1572872 | tf_op jit(solution)/shard_map/ppermute | solution.py:790
  529.2 25.2 %collective-permute-start.52 = (bf16[256,2048]{1,0:T(8,128)(2,1)}, bf16[256,2048]{1,0:T(8,128)(2,1)S(1)}, u32[]{:S(2)}, u32[]{:S(2)}) collective-permute-start(bf16[256,2048]{1,0:T(8,128)(2,1)} %get-tuple-element.323), channel_id=1, source_target_pairs={{0,1},{1,0},{2,3},{3,2},{4,5},{5,4},{6,7},{7,6},{8,9},{9,8},{10,11... | collective-permute-start | bytes 3145736 | tf_op jit(solution)/shard_map/ppermute | solution.py:790
  530.8 24.9 %collective-permute-start.53 = (bf16[256,2048]{1,0:T(8,128)(2,1)}, bf16[256,2048]{1,0:T(8,128)(2,1)S(1)}, u32[]{:S(2)}, u32[]{:S(2)}) collective-permute-start(bf16[256,2048]{1,0:T(8,128)(2,1)} %get-tuple-element.324), channel_id=1, source_target_pairs={{0,2},{1,3},{2,0},{3,1},{4,6},{5,7},{6,4},{7,5},{8,10},{9,11},{10,... | collective-permute-start | bytes 3145736 | tf_op jit(solution)/shard_map/ppermute | solution.py:790
  534.2 6.0 %collective-permute-start.54 = (f32[256,2]{0,1:T(2,128)S(1)}, f32[256,2]{0,1:T(2,128)S(1)}, u32[]{:S(2)}, u32[]{:S(2)}) collective-permute-start(f32[256,2]{0,1:T(2,128)S(1)} %bitcast.44), channel_id=1, source_target_pairs={{0,8},{4,12},{8,16},{12,20},{16,24},{20,28},{24,0},{28,4},{1,9},{5... | collective-permute-start | bytes 6152 | tf_op jit(solution)/shard_map/ppermute | solution.py:878
  555.7 24.9 %collective-permute-start.57 = (bf16[256,2048]{1,0:T(8,128)(2,1)S(1)}, bf16[256,2048]{1,0:T(8,128)(2,1)}, u32[]{:S(2)}, u32[]{:S(2)}) collective-permute-start(bf16[256,2048]{1,0:T(8,128)(2,1)S(1)} %copy-done.22), channel_id=1, source_target_pairs={{0,3},{1,2},{2,1},{3,0},{4,7},{5,6},{6,5},{7,4},{8,11},{9,10},{10,... | collective-permute-start | bytes 3145736 | tf_op jit(solution)/shard_map/ppermute | solution.py:790
  562.1 18.5 %collective-permute-start.60 = (f32[64,2]{0,1:T(2,128)S(1)}, f32[64,2]{0,1:T(2,128)S(1)}, u32[]{:S(2)}, u32[]{:S(2)}) collective-permute-start(f32[64,2]{0,1:T(2,128)S(1)} %bitcast.47), channel_id=1, source_target_pairs={{0,3},{1,2},{2,1},{3,0},{4,7},{5,6},{6,5},{7,4},{8,11},{9,10},{10,... | collective-permute-start | bytes 1544 | tf_op jit(solution)/shard_map/ppermute | solution.py:790
  563.7 16.9 %collective-permute-start.58 = (f32[64,2]{0,1:T(2,128)S(1)}, f32[64,2]{0,1:T(2,128)S(1)}, u32[]{:S(2)}, u32[]{:S(2)}) collective-permute-start(f32[64,2]{0,1:T(2,128)S(1)} %bitcast.46), channel_id=1, source_target_pairs={{0,1},{1,0},{2,3},{3,2},{4,5},{5,4},{6,7},{7,6},{8,9},{9,8},{10,11... | collective-permute-start | bytes 1544 | tf_op jit(solution)/shard_map/ppermute | solution.py:790
  564.6 16.0 %collective-permute-start.59 = (f32[64,2]{0,1:T(2,128)S(1)}, f32[64,2]{0,1:T(2,128)S(1)}, u32[]{:S(2)}, u32[]{:S(2)}) collective-permute-start(f32[64,2]{0,1:T(2,128)S(1)} %bitcast.45), channel_id=1, source_target_pairs={{0,2},{1,3},{2,0},{3,1},{4,6},{5,7},{6,4},{7,5},{8,10},{9,11},{10,... | collective-permute-start | bytes 1544 | tf_op jit(solution)/shard_map/ppermute | solution.py:790
  (47 other events, 449.1 us)
Sparse Core Ops, SparseCore 0:
  16.5 56.4 all-gather.3
  75.1 114.1 all-gather.5
  191.3 113.2 all-gather.7
  306.7 108.9 reduce-scatter.3
  417.9 111.2 reduce-scatter.5
  531.4 52.5 reduce-scatter.7
